TPU v7x, 32 devices: a whole 2x2x4 slice. The times are simulated.
32 devices in a mesh: frow: 2 (over core), fcol: 16 (over z, y, x).
Axes of the slice: x: 2, y: 2, z: 4, core: 2. Of those that a mesh axis runs over, the one named last changes fastest.
Arguments:
- right_side: float32 [16, 512, 256], P('frow', 'fcol'), may hold values from -6 to 6
- noise_weight: float32 [16, 512, 256], P('frow', 'fcol'), may hold values from 3 to 4.5
- stencils: bfloat16 [9, 256, 256], replicated, may hold values from -1 to 1, as said below
- neighbours: int32 [16, 512, 9], P('frow', 'fcol'), may hold values from -1 to 8191, as said below
Outputs:
- solution: float32 [16, 512, 256], P('frow', 'fcol')
- coarse_residual: float32 [8, 256, 256], P('frow')
Inputs may be any that keep to these rules, and one draw needn't show every extreme that they name: `neighbours`: each entry is -1 (an empty slot) or the index r * 512 + c of the tile at row r = own row + k // 3 - 1 and column c = own column + k % 3 - 1 for slot k; slot 4 always holds the tile itself; if tile t holds tile s in slot k, then s holds t in slot 8 - k. stencils[8 - k] is the transpose of stencils[k], and stencils[4] is symmetric.
All inputs are finite; a program needn't handle non-finite values.
Results may differ from a plain program's by a relative error of at most 0.0031.
Values may be sent and summed in bfloat16 or wider, within the bound.
No kernel may reach another device: no remote copies, remote signals or barrier semaphores. Data moves between devices by JAX's collectives and lax.ppermute only.
A program may use at most 64 MiB of HBM per device.

v0:
```python
import functools

import jax
import jax.numpy as jnp
from jax import lax
from jax.experimental import pallas as pl
from jax.experimental.pallas import tpu as pltpu
from jax.sharding import PartitionSpec as P

DEG = 3
SWEEPS = 2
STEPS = DEG * SWEEPS
SIDE = 8
LANES = 128

lower_edge = 1.5
upper_edge = 6.0
center = 0.5 * (upper_edge + lower_edge)
half_width = 0.5 * (upper_edge - lower_edge)
weight_middle = 3.75

F32 = jnp.float32
BF16 = jnp.bfloat16
HBM_SPEC = pl.BlockSpec(memory_space=pl.ANY)
VMEM_SPEC = pl.BlockSpec(memory_space=pltpu.VMEM)


def step_factors():
    spread_ratio = center / half_width
    factors = []
    for sweep in range(SWEEPS):
        ratio = 1.0 / spread_ratio
        for step in range(DEG):
            if step < DEG - 1:
                ratio_next = 1.0 / (2.0 * spread_ratio - ratio)
                factors.append((ratio_next * ratio, 2.0 * ratio_next / half_width))
                ratio = ratio_next
            else:
                factors.append((0.0, 1.0 / center))
    return factors


def row_places(ends, own_rows):
    if ends == 1:
        flip = lax.axis_index("frow")
        place = [row + flip * (own_rows - 1 - 2 * row) for row in range(own_rows)]
        return place, [list(enumerate(place))], 0
    above = [(own_rows - STEPS + row, row) for row in range(STEPS)]
    below = [(row, row) for row in range(STEPS)]
    return list(range(own_rows)), [above, below], 1


def slot_places(ends, slots):
    if ends == 1:
        flip = lax.axis_index("frow")
        return [(slot // 3 + flip * (2 - 2 * (slot // 3))) * 3 + slot % 3 for slot in range(slots)]
    return list(range(slots))


def spread_flags(ends, mask, flags, own_rows, places):
    slots, _, cols, _ = mask.shape
    slot_place = slot_places(ends, slots)
    for slot in range(slots):
        for row, at in places:
            lane = slot * own_rows + row
            column = jnp.broadcast_to(flags[:, lane : lane + 1], (cols, LANES))
            mask[slot_place[slot], at] = column.astype(BF16)


def edge_kernel(right_hbm, weight_hbm, near_hbm, *refs):
    odd_ref, even_ref, held_ref, strips, near_ref, arrived = refs
    slots, rows, cols = near_ref.shape
    copies = [pltpu.make_async_copy(near_hbm, near_ref, arrived.at[4])]
    for end, start in enumerate((0, cols - SIDE)):
        for kind, source in enumerate((right_hbm, weight_hbm)):
            copies.append(
                pltpu.make_async_copy(
                    source.at[:, pl.ds(start, SIDE)],
                    strips.at[end, kind],
                    arrived.at[2 * end + kind],
                )
            )
    for copy in copies:
        copy.start()
    copies[0].wait()
    flags = jnp.where(near_ref[...] >= 0, 1.0, 0.0).astype(F32).reshape(slots * rows, cols)
    flags = jnp.concatenate([flags, jnp.zeros((slots * rows, LANES - cols), F32)], 1)
    flags = jnp.concatenate([flags, jnp.zeros((LANES - slots * rows, LANES), F32)], 0)
    turned = jnp.transpose(flags)[:cols]
    held_ref[...] = turned
    for copy in copies[1:]:
        copy.wait()
    parity = lax.rem(lax.axis_index("fcol"), 2)
    flags = [turned[:SIDE], turned[cols - SIDE :]]
    for ref, end in ((odd_ref, parity), (even_ref, 1 - parity)):
        ref[:rows] = jnp.concatenate([strips[end, 0], strips[end, 1] - weight_middle], 1).astype(
            BF16
        )
        strip = jnp.where(end == 0, flags[0], flags[1])
        strip = jnp.concatenate([strip, jnp.zeros((SIDE, LANES), F32)], 0)
        ref[rows, :, :LANES] = strip.astype(BF16)


def own_kernel(ends, stencil_hbm, right_hbm, weight_hbm, held_ref, *refs):
    whole_ref, stencil_ref, mask, residual, weight, arrived = refs
    slots = mask.shape[0]
    own_rows, own_cols, _ = residual.shape
    place, _, _ = row_places(ends, own_rows)
    slot_place = slot_places(ends, slots)
    copies = []
    for row in range(own_rows):
        for source, target in ((right_hbm, residual), (weight_hbm, weight)):
            copies.append(
                pltpu.make_async_copy(
                    source.at[row], target.at[place[row]], arrived.at[3 + len(copies)]
                )
            )
    stencil_copies = [
        pltpu.make_async_copy(
            stencil_hbm.at[pl.ds(slot, 3)],
            stencil_ref.at[pl.ds(slot_place[slot], 3)],
            arrived.at[slot // 3],
        )
        for slot in range(0, slots, 3)
    ]
    for copy in copies + stencil_copies:
        copy.start()
    flags = held_ref[...]
    spread_flags(ends, mask, flags, own_rows, list(enumerate(place)))
    whole_ref[own_rows, :own_cols, :LANES] = flags.astype(BF16)
    for copy in copies:
        copy.wait()
    for row, at in enumerate(place):
        whole_ref[row, :own_cols] = residual[at].astype(BF16)
        whole_ref[row, own_cols:] = (weight[at] - weight_middle).astype(BF16)
    for copy in stencil_copies:
        copy.wait()


def rows_kernel(ends, *refs):
    for index in range(ends):
        whole_ref = refs[index]
        mask, residual, weight = refs[ends + 3 * index : ends + 3 * index + 3]
        own_rows = whole_ref.shape[0] - 1
        own_cols = residual.shape[1]
        places = row_places(ends, own_rows)[1][index]
        for row, at in places:
            strip = whole_ref[row].astype(F32)
            residual[at] = strip[:own_cols]
            weight[at] = strip[own_cols:] + weight_middle
        flags = whole_ref[own_rows, :own_cols, :LANES].astype(F32)
        spread_flags(ends, mask, flags, own_rows, places)


def smooth_kernel(ends, *refs):
    stencil_ref, odd_ref, even_ref = refs[:3]
    sides = refs[3 : 3 + ends]
    own_block = refs[3 + ends : 6 + ends]
    halo_blocks = [refs[6 + ends + 3 * i : 9 + ends + 3 * i] for i in range(ends)]
    solution_ref, coarse_ref = refs[6 + 4 * ends : 8 + 4 * ends]
    residual, weight, direction, shifted, side_mask, smoothed, summed = refs[8 + 4 * ends :]
    own_rows, own_cols, pixels = solution_ref.shape
    slots = side_mask.shape[0]
    rows, cols, _ = residual.shape
    place, halos, ahead = row_places(ends, own_rows)
    blocks = halo_blocks[:ahead] + [own_block] + halo_blocks[ahead:]
    bases = [0]
    for block in blocks:
        bases.append(bases[-1] + block[1].shape[0])
    own_start = bases[ahead]

    def flags_of(slot, first, last):
        pieces = []
        for base, block in zip(bases, blocks):
            low, high = max(first - base, 0), min(last - base, block[1].shape[0])
            if low < high:
                pieces.append(block[0][slot, low:high])
        return pieces[0] if len(pieces) == 1 else jnp.concatenate(pieces, 0)

    first_of_even = lax.rem(lax.axis_index("fcol"), 2) == 0

    def fill(base, block, odd, even, places):
        here = slice(base, base + block[1].shape[0])
        residual[here, :own_cols, :] = block[1][...]
        weight[here, :own_cols, :] = block[2][...]

        def in_order(odd_piece, even_piece):
            after = jnp.where(first_of_even, even_piece, odd_piece)
            before = jnp.where(first_of_even, odd_piece, even_piece)
            return after, before

        flags = in_order(*(piece[own_rows, :, :LANES].astype(F32)[:SIDE] for piece in (odd, even)))
        places = [(row, base + at) for row, at in places]
        spread_flags(ends, side_mask, jnp.concatenate(flags, 0), own_rows, places)
        for row, at in places:
            after, before = in_order(odd[row].astype(F32), even[row].astype(F32))
            residual[at, own_cols : own_cols + SIDE, :] = after[:SIDE]
            residual[at, own_cols + SIDE :, :] = before[:SIDE]
            weight[at, own_cols : own_cols + SIDE, :] = after[SIDE:] + weight_middle
            weight[at, own_cols + SIDE :, :] = before[SIDE:] + weight_middle

    fill(own_start, own_block, odd_ref, even_ref, list(enumerate(place)))
    halo_bases = bases[:ahead] + bases[ahead + 1 : -1]
    for base, block, sides_ref, places in zip(halo_bases, halo_blocks, sides, halos):
        fill(base, block, sides_ref.at[0], sides_ref.at[1], places)

    def put_direction(slot, start, count, value):
        here = slice(start + 1, start + 1 + count)
        shifted[slot, 1, here] = value.astype(BF16)
        shifted[slot, 0, here] = pltpu.roll(value, 1, 1).astype(BF16)
        shifted[slot, 2, here] = pltpu.roll(value, cols - 1, 1).astype(BF16)

    edge = jnp.zeros((cols, pixels), BF16)
    for slot in range(2):
        for move in range(3):
            shifted[slot, move, 0] = edge
            shifted[slot, move, rows + 1] = edge
    value = residual[...] * (1.0 / center)
    direction[...] = value
    put_direction(0, 0, rows, value)

    own = slice(own_start, own_start + own_rows)
    stencil = stencil_ref[...].reshape(slots * pixels, pixels)
    factors = step_factors()
    for step in range(STEPS):
        now, later = step % 2, 1 - step % 2
        last = step == STEPS - 1
        moved = direction[own, :own_cols, :]
        smoothed[...] = moved if step == 0 else smoothed[...] + moved
        margin = STEPS - 1 - step
        count = own_rows + ends * margin
        start = own_start - (ends - 1) * margin
        width = own_cols if last else cols
        half = (count + 1) // 2
        for base, size in ((start, half), (start + half, count - half)):
            here = slice(base, base + size)
            picked = []
            for slot in range(slots):
                across, along = slot // 3, slot % 3
                keep = flags_of(slot, base, base + size)
                if not last:
                    keep = jnp.concatenate([keep, side_mask[slot, here]], 1)
                source = shifted[now, along, base + across : base + across + size, :width, :]
                picked.append(source[:, :, :LANES] * keep)
                picked.append(source[:, :, LANES:] * keep)
            picked = jnp.concatenate(picked, 2).reshape(size * width, slots * pixels)
            coupled = jnp.dot(picked, stencil, preferred_element_type=F32)
            coupled = coupled.reshape(size, width, pixels)
            moved = direction[here, :width, :]
            left = residual[here, :width, :] - (weight[here, :width, :] * moved + coupled)
            residual[here, :width, :] = left
            if not last:
                a, b = factors[step]
                value = b * left if a == 0.0 else a * moved + b * left
                direction[here, :width, :] = value
                put_direction(later, base, size, value)

    fine = residual[own, :own_cols, :].reshape(own_rows * own_cols, pixels)
    high = fine.astype(BF16)
    low = (fine - high.astype(F32)).astype(BF16)
    quarter = pixels // 4
    from_pixel = lax.broadcasted_iota(jnp.int32, (pixels, LANES), 0) // 4
    to_pixel = lax.broadcasted_iota(jnp.int32, (pixels, LANES), 1)
    adder = jnp.where(from_pixel == to_pixel, 1.0, 0.0).astype(BF16)
    total = jnp.dot(high, adder, preferred_element_type=F32) + jnp.dot(
        low, adder, preferred_element_type=F32
    )
    summed[...] = total.reshape(own_rows, own_cols, LANES)
    for row in range(own_rows // 2):
        pieces = []
        for across in range(2):
            for along in range(2):
                at = place[2 * row + across]
                piece = summed[at, pl.ds(along, own_cols // 2, stride=2), :]
                pieces.append(piece[:, :quarter])
        coarse_ref[row] = jnp.concatenate(pieces, 1).astype(BF16)
    for row, at in enumerate(place):
        solution_ref[row] = smoothed[at]


def widen_kernel(block_ref, out_hbm, wide, sent):
    rows, ring, _, _ = wide.shape
    copies = []
    for row in range(rows):
        for i in range(ring):
            wide[row, i] = block_ref[i, row].astype(F32)
        copies.append(pltpu.make_async_copy(wide.at[row], out_hbm.at[row], sent.at[row]))
        copies[-1].start()
    for copy in copies:
        copy.wait()


def body(right_side, noise_weight, stencils, neighbours):
    rows, cols, pixels = right_side.shape
    slots = stencils.shape[0]
    pairs, ring = lax.axis_size("frow"), lax.axis_size("fcol")
    swaps = [
        [(i, j) for low in range(first, ring - 1, 2) for i, j in ((low, low + 1), (low + 1, low))]
        for first in (0, 1)
    ]
    near = jnp.transpose(neighbours, (2, 0, 1))
    right_hbm, weight_hbm, near_hbm, stencil_hbm = [
        pltpu.with_memory_space_constraint(array, pltpu.HBM)
        for array in (right_side, noise_weight, near, stencils)
    ]
    small = pltpu.CompilerParams(vmem_limit_bytes=8 * 1024 * 1024)

    side = pltpu.VMEM((rows + 1, 2 * SIDE, pixels), BF16)
    odd, even, held = pl.pallas_call(
        edge_kernel,
        out_shape=(side, side, pltpu.VMEM((cols, LANES), F32)),
        in_specs=[HBM_SPEC] * 3,
        out_specs=(VMEM_SPEC,) * 3,
        scratch_shapes=[
            pltpu.VMEM((2, 2, rows, SIDE, pixels), F32),
            pltpu.VMEM((slots, rows, cols), jnp.int32),
            pltpu.SemaphoreType.DMA((5,)),
        ],
        compiler_params=small,
        name="edges",
    )(right_hbm, weight_hbm, near_hbm)

    odd_side = lax.ppermute(odd, "fcol", swaps[1])
    even_side = lax.ppermute(even, "fcol", swaps[0])
    if pairs == 2:
        moves = [[(0, 1), (1, 0)]]
    else:
        moves = [
            [(i, i + 1) for i in range(pairs - 1)],
            [(i + 1, i) for i in range(pairs - 1)],
        ]
    ends = len(moves)

    def block_types(count):
        return (
            pltpu.VMEM((slots, count, cols, LANES), BF16),
            pltpu.VMEM((count, cols, pixels), F32),
            pltpu.VMEM((count, cols, pixels), F32),
        )

    whole, stencil, *own_block = pl.pallas_call(
        functools.partial(own_kernel, ends),
        out_shape=(
            pltpu.VMEM((rows + 1, 2 * cols, pixels), BF16),
            pltpu.VMEM(stencils.shape, stencils.dtype),
        )
        + block_types(rows),
        in_specs=[HBM_SPEC] * 3 + [VMEM_SPEC],
        out_specs=(VMEM_SPEC,) * 5,
        scratch_shapes=[pltpu.SemaphoreType.DMA((3 + 2 * rows,))],
        compiler_params=small,
        cost_estimate=pl.CostEstimate(flops=0, bytes_accessed=6000000, transcendentals=0),
        name="own",
    )(stencil_hbm, right_hbm, weight_hbm, held)

    wholes = [lax.ppermute(whole, "frow", move) for move in moves]
    sides = jnp.stack([odd_side, even_side])
    sides_held = [lax.ppermute(sides, "frow", move) for move in moves]
    far_rows = rows if ends == 1 else STEPS
    halo_blocks = pl.pallas_call(
        functools.partial(rows_kernel, ends),
        out_shape=block_types(far_rows) * ends,
        in_specs=[VMEM_SPEC] * ends,
        out_specs=(VMEM_SPEC,) * (3 * ends),
        compiler_params=small,
        cost_estimate=pl.CostEstimate(flops=0, bytes_accessed=4000000, transcendentals=0),
        name="rows",
    )(*wholes)

    cols_held = cols + 2 * SIDE
    rows_held = rows + ends * far_rows
    solution, coarse = pl.pallas_call(
        functools.partial(smooth_kernel, ends),
        out_shape=(
            jax.ShapeDtypeStruct((rows, cols, pixels), F32),
            pltpu.VMEM((rows // 2, cols // 2, pixels), BF16),
        ),
        in_specs=[VMEM_SPEC] * (6 + 4 * ends),
        out_specs=(VMEM_SPEC,) * 2,
        scratch_shapes=[
            pltpu.VMEM((rows_held, cols_held, pixels), F32),
            pltpu.VMEM((rows_held, cols_held, pixels), F32),
            pltpu.VMEM((rows_held, cols_held, pixels), F32),
            pltpu.VMEM((2, 3, rows_held + 2, cols_held, pixels), BF16),
            pltpu.VMEM((slots, rows_held, 2 * SIDE, LANES), BF16),
            pltpu.VMEM((rows, cols, pixels), F32),
            pltpu.VMEM((rows, cols, LANES), F32),
        ],
        compiler_params=pltpu.CompilerParams(vmem_limit_bytes=24 * 1024 * 1024),
        name="smooth",
    )(stencil, odd_side, even_side, *sides_held, *own_block, *halo_blocks)

    spread = jnp.broadcast_to(coarse[None], (ring,) + coarse.shape)
    block = lax.all_to_all(spread, "fcol", 0, 0)
    widened = (rows // 2, ring, cols // 2, pixels)
    gathered = pl.pallas_call(
        widen_kernel,
        out_shape=jax.ShapeDtypeStruct(widened, F32),
        in_specs=[VMEM_SPEC],
        out_specs=HBM_SPEC,
        scratch_shapes=[pltpu.VMEM(widened, F32), pltpu.SemaphoreType.DMA((rows // 2,))],
        compiler_params=small,
        name="widen",
    )(block)
    return solution, gathered.reshape(rows // 2, ring * (cols // 2), pixels)


def solution(mesh):
    placed = (P("frow", "fcol", None), P("frow", "fcol", None), P(), P("frow", "fcol", None))
    return jax.shard_map(
        body,
        mesh=mesh,
        in_specs=placed,
        out_specs=(P("frow", "fcol", None), P("frow", None, None)),
        check_vma=False,
    )
```

profile of v0, /device:TPU:0, one launch (start us, length us, event | category | flops | bytes accessed | tf_op | source)
XLA Modules:
  0.0 40.6 jit_solution(9124225170829153887)
XLA Ops:
  0.6 1.0 %edges.1 = (bf16[9,16,256]{2,1,0:T(8,128)(2,1)S(1)}, bf16[9,16,256]{2,1,0:T(8,128)(2,1)S(1)}, f32[32,128]{1,0:T(8,128)S(1)}) custom-call(f32[8,32,256]{2,1,0:T(8,128)} %right_hbm.3, f32[8,32,256]{2,1,0:T(8,128)} %weight_hbm.3, s32[9,8,32]{2,1,0:T(8,128)} %bitcast.7), custom_call_target="tpu_custom_call" | custom-call | tf_op jit(solution)/shard_map/edges/pallas_call | solution.py:309
  1.7 0.7 %collective-permute-start = (bf16[9,16,256]{2,1,0:T(8,128)(2,1)S(1)}, bf16[9,16,256]{2,1,0:T(8,128)(2,1)S(1)}, u32[]{:S(2)}, u32[]{:S(2)}) collective-permute-start(bf16[9,16,256]{2,1,0:T(8,128)(2,1)S(1)} %get-tuple-element.17), channel_id=1, source_target_pairs={{1,2},{2,1},{3,4},{4,3},{5,6},{6,5},{7,8},{8,7},{9,10},{10,9},{11,... | collective-permute-start | bytes 221192 | tf_op jit(solution)/shard_map/ppermute | solution.py:323
  2.3 5.7 %collective-permute-start.1 = (bf16[9,16,256]{2,1,0:T(8,128)(2,1)S(1)}, bf16[9,16,256]{2,1,0:T(8,128)(2,1)S(1)}, u32[]{:S(2)}, u32[]{:S(2)}) collective-permute-start(bf16[9,16,256]{2,1,0:T(8,128)(2,1)S(1)} %get-tuple-element.18), channel_id=1, source_target_pairs={{0,1},{1,0},{2,3},{3,2},{4,5},{5,4},{6,7},{7,6},{8,9},{9,8},{10,11... | collective-permute-start | bytes 221192 | tf_op jit(solution)/shard_map/ppermute | solution.py:324
  8.1 1.9 %own.1 = (bf16[9,64,256]{2,1,0:T(8,128)(2,1)S(1)}, bf16[9,256,256]{2,1,0:T(8,128)(2,1)S(1)}, bf16[9,8,32,128]{3,2,1,0:T(8,128)(2,1)S(1)}, f32[8,32,256]{2,1,0:T(8,128)S(1)}, f32[8,32,256]{2,1,0:T(8,128)S(1)}) custom-call(bf16[9,256,256]{2,1,0:T(8,128)(2,1)} %stencil_hbm.1, f32[8,32,256]{2,1,0:T(8,128)} %right_hbm.3, f32[8,32,256]{2,1,0:T(8,128)} %weight_hbm.3, ...), custom_call_target="tpu_custom_call" | custom-call | bytes 6000000 | tf_op jit(solution)/shard_map/own/pallas_call | solution.py:341
  10.0 0.1 collective-permute-start.3
  10.1 0.0 collective-permute-done.refs_1_
  10.1 1.5 %collective-permute-done.1.refs_2_ = bf16[9,16,256]{2,1,0:T(8,128)(2,1)S(1)} collective-permute-done((bf16[9,16,256]{2,1,0:T(8,128)(2,1)S(1)}, bf16[9,16,256]{2,1,0:T(8,128)(2,1)S(1)}, u32[]{:S(2)}, u32[]{:S(2)}) %collective-permute-start.1) | collective-permute-done | bytes 73760 | tf_op jit(solution)/shard_map/ppermute | solution.py:324
  11.6 0.1 collective-permute-start.2
  11.6 0.0 collective-permute-done.3.refs_0_
  11.7 0.3 rows.1
  12.0 1.0 %collective-permute-done.2.refs_3_ = bf16[2,9,16,256]{3,2,1,0:T(8,128)(2,1)S(1)} collective-permute-done((bf16[2,9,16,256]{3,2,1,0:T(8,128)(2,1)S(1)}, bf16[2,9,16,256]{3,2,1,0:T(8,128)(2,1)S(1)}, u32[]{:S(2)}, u32[]{:S(2)}) %collective-permute-start.2) | collective-permute-done | bytes 147488 | tf_op jit(solution)/shard_map/ppermute | solution.py:358
  13.0 5.5 %smooth.1 = (f32[8,32,256]{2,1,0:T(8,128)}, bf16[4,16,256]{2,1,0:T(8,128)(2,1)S(1)}) custom-call(bf16[9,256,256]{2,1,0:T(8,128)(2,1)S(1)} %get-tuple-element.16.refs_0_, bf16[9,16,256]{2,1,0:T(8,128)(2,1)S(1)} %collective-permute-done.refs_1_, bf16[9,16,256]{2,1,0:T(8,128)(2,1)S(1)} %collective-permute-done.1.refs_2_, ...), custom_call_target="tpu_custom_call" | custom-call | tf_op jit(solution)/shard_map/smooth/pallas_call | solution.py:372
  18.5 21.1 %all_to_all.5.block_ref = bf16[16,4,16,256]{3,2,1,0:T(8,128)(2,1)S(1)} all-to-all(bf16[16,4,16,256]{3,2,1,0:T(8,128)(2,1)S(1)} %broadcast_in_dim.2), channel_id=1, replica_groups=mesh['frow'=2,'fcol'=16] {'fcol'}, dimensions={0} | all-to-all | bytes 1048576 | tf_op jit(solution)/shard_map/all_to_all | solution.py:394
  39.6 1.0 %widen.1 = f32[4,16,16,256]{3,2,1,0:T(8,128)} custom-call(bf16[16,4,16,256]{3,2,1,0:T(8,128)(2,1)S(1)} %all_to_all.5.block_ref), custom_call_target="tpu_custom_call" | custom-call | tf_op jit(solution)/shard_map/widen/pallas_call | solution.py:396
  (2 shorter events, 0.1 us)
Async XLA Ops:
  1.7 8.4 %collective-permute-start = (bf16[9,16,256]{2,1,0:T(8,128)(2,1)S(1)}, bf16[9,16,256]{2,1,0:T(8,128)(2,1)S(1)}, u32[]{:S(2)}, u32[]{:S(2)}) collective-permute-start(bf16[9,16,256]{2,1,0:T(8,128)(2,1)S(1)} %get-tuple-element.17), channel_id=1, source_target_pairs={{1,2},{2,1},{3,4},{4,3},{5,6},{6,5},{7,8},{8,7},{9,10},{10,9},{11,... | collective-permute-start | bytes 221192 | tf_op jit(solution)/shard_map/ppermute | solution.py:323
  2.3 9.2 %collective-permute-start.1 = (bf16[9,16,256]{2,1,0:T(8,128)(2,1)S(1)}, bf16[9,16,256]{2,1,0:T(8,128)(2,1)S(1)}, u32[]{:S(2)}, u32[]{:S(2)}) collective-permute-start(bf16[9,16,256]{2,1,0:T(8,128)(2,1)S(1)} %get-tuple-element.18), channel_id=1, source_target_pairs={{0,1},{1,0},{2,3},{3,2},{4,5},{5,4},{6,7},{7,6},{8,9},{9,8},{10,11... | collective-permute-start | bytes 221192 | tf_op jit(solution)/shard_map/ppermute | solution.py:324
  10.0 1.6 %collective-permute-start.3 = (bf16[9,64,256]{2,1,0:T(8,128)(2,1)S(1)}, bf16[9,64,256]{2,1,0:T(8,128)(2,1)S(1)}, u32[]{:S(2)}, u32[]{:S(2)}) collective-permute-start(bf16[9,64,256]{2,1,0:T(8,128)(2,1)S(1)} %get-tuple-element.22), channel_id=1, source_target_pairs={{0,16},{16,0},{1,17},{17,1},{2,18},{18,2},{3,19},{19,3},{4,20},{20... | collective-permute-start | bytes 884744 | tf_op jit(solution)/shard_map/ppermute | solution.py:356
  11.6 1.4 %collective-permute-start.2 = (bf16[2,9,16,256]{3,2,1,0:T(8,128)(2,1)S(1)}, bf16[2,9,16,256]{3,2,1,0:T(8,128)(2,1)S(1)}, u32[]{:S(2)}, u32[]{:S(2)}) collective-permute-start(bf16[2,9,16,256]{3,2,1,0:T(8,128)(2,1)S(1)} %pad_maximum_fusion), channel_id=1, source_target_pairs={{0,16},{16,0},{1,17},{17,1},{2,18},{18,2},{3,19},{19,3},{4,20},{20... | collective-permute-start | bytes 442376 | tf_op jit(solution)/shard_map/ppermute | solution.py:358
where the time goes:
time: 40.8 us; the launch traced here: 40.6 us
  blocking collectives  21.1 us (52%)
  Pallas kernels  9.73 us (24%)
  starting transfers between devices  6.55 us (16%)
  waiting for transfers between devices  2.5 us (6%)
  between operations  0.7 us (2%)
    all_to_all x1, blocking collectives, body(): block = lax.all_to_all(spread, 'fcol', 0, 0)  21.1 us
    ppermute x1, starting transfers between devices, body(): even_side = lax.ppermute(even, 'fcol', swaps[0])  5.74 us
    pallas_call x1, Pallas kernels, body(): pl.pallas_call(functools.partial(smooth_kernel, ends), out_shape=(jax.Sha...  5.48 us
    pallas_call x1, Pallas kernels, body(): pl.pallas_call(functools.partial(own_kernel, ends), out_shape=(pltpu.VMEM...  1.92 us
    ppermute x1, waiting for transfers between devices, body(): even_side = lax.ppermute(even, 'fcol', swaps[0])  1.46 us
    ppermute x1, waiting for transfers between devices, body(): sides_held = [lax.ppermute(sides, 'frow', move) for move in moves]  1.04 us
    pallas_call x1, Pallas kernels, body(): pl.pallas_call(edge_kernel, out_shape=(side, side, pltpu.VMEM((cols, LANE...  1.02 us
    pallas_call x1, Pallas kernels, body(): pl.pallas_call(widen_kernel, out_shape=jax.ShapeDtypeStruct(widened, F32)...  1.01 us
  transfers between devices with their start and end apart: 4, of which 2 were waited for; matrix products, arithmetic and copies ran while one was open for 0% of the time, Pallas kernels for 5%

commit v1 on v0

--- a/solution.py
+++ b/solution.py
@@ -231,8 +231,7 @@
         count = own_rows + ends * margin
         start = own_start - (ends - 1) * margin
         width = own_cols if last else cols
-        half = (count + 1) // 2
-        for base, size in ((start, half), (start + half, count - half)):
+        for base, size in ((start, count),):
             here = slice(base, base + size)
             picked = []
             for slot in range(slots):
@@ -280,10 +279,13 @@
 
 def widen_kernel(block_ref, out_hbm, wide, sent):
     rows, ring, _, _ = wide.shape
+    half = ring // 2
+    own_half = lax.axis_index("fcol") // half
     copies = []
     for row in range(rows):
-        for i in range(ring):
-            wide[row, i] = block_ref[i, row].astype(F32)
+        for i in range(half):
+            wide[row, own_half * half + i] = block_ref[i, 0, row].astype(F32)
+            wide[row, (1 - own_half) * half + i] = block_ref[i, 1, row].astype(F32)
         copies.append(pltpu.make_async_copy(wide.at[row], out_hbm.at[row], sent.at[row]))
         copies[-1].start()
     for copy in copies:
@@ -390,8 +392,12 @@
         name="smooth",
     )(stencil, odd_side, even_side, *sides_held, *own_block, *halo_blocks)
 
-    spread = jnp.broadcast_to(coarse[None], (ring,) + coarse.shape)
-    block = lax.all_to_all(spread, "fcol", 0, 0)
+    half = ring // 2
+    across = [(i, (i + half) % ring) for i in range(ring)]
+    pair = jnp.stack([coarse, lax.ppermute(coarse, "fcol", across)])
+    halves = [list(range(half)), list(range(half, ring))]
+    spread = jnp.broadcast_to(pair[None], (half,) + pair.shape)
+    block = lax.all_to_all(spread, "fcol", 0, 0, axis_index_groups=halves)
     widened = (rows // 2, ring, cols // 2, pixels)
     gathered = pl.pallas_call(
         widen_kernel,

time: 40.8 us -> 40.2 us (0.985)
  blocking collectives: 21.1 us -> 12.9 us
  starting transfers between devices: 6.55 us -> 9.48 us
  Pallas kernels: 9.73 us -> 12.4 us
  waiting for transfers between devices: 2.5 us -> 4.39 us
    all_to_all x1, blocking collectives: 21.1 us -> 12.9 us  [body(): block = lax.all_to_all(spread, 'fcol', 0, 0, axis_index_groups=halves)]
    ppermute x0 -> x1, starting transfers between devices: none -> 2.93 us  [body(): pair = jnp.stack([coarse, lax.ppermute(coarse, 'fcol', across)])]
    pallas_call x1, Pallas kernels: 5.48 us -> 8.17 us  [body(): pl.pallas_call(functools.partial(smooth_kernel, ends), out_shape=(jax.Sha...]
    ppermute x0 -> x1, waiting for transfers between devices: none -> 1.89 us  [body(): pair = jnp.stack([coarse, lax.ppermute(coarse, 'fcol', across)])]
  transfers between devices with their start and end apart: 4 -> 5, of which waited for: 2 -> 3; matrix products, arithmetic and copies ran while one was open for 0% -> 0% of each run, Pallas kernels for 5% -> 6%
where the time goes in v1:
time: 40.2 us; the launch traced here: 40 us
  blocking collectives  12.9 us (32%)
  Pallas kernels  12.4 us (31%)
  starting transfers between devices  9.48 us (24%)
  waiting for transfers between devices  4.39 us (11%)
  between operations  0.71 us (2%)
    all_to_all x1, blocking collectives, body(): block = lax.all_to_all(spread, 'fcol', 0, 0, axis_index_groups=halves)  12.9 us
    pallas_call x1, Pallas kernels, body(): pl.pallas_call(functools.partial(smooth_kernel, ends), out_shape=(jax.Sha...  8.17 us
    ppermute x1, starting transfers between devices, body(): even_side = lax.ppermute(even, 'fcol', swaps[0])  5.74 us
    ppermute x1, starting transfers between devices, body(): pair = jnp.stack([coarse, lax.ppermute(coarse, 'fcol', across)])  2.93 us
    pallas_call x1, Pallas kernels, body(): pl.pallas_call(functools.partial(own_kernel, ends), out_shape=(pltpu.VMEM...  1.92 us
    ppermute x1, waiting for transfers between devices, body(): pair = jnp.stack([coarse, lax.ppermute(coarse, 'fcol', across)])  1.89 us
    ppermute x1, waiting for transfers between devices, body(): even_side = lax.ppermute(even, 'fcol', swaps[0])  1.46 us
    ppermute x1, waiting for transfers between devices, body(): sides_held = [lax.ppermute(sides, 'frow', move) for move in moves]  1.04 us
  transfers between devices with their start and end apart: 5, of which 3 were waited for; matrix products, arithmetic and copies ran while one was open for 0% of the time, Pallas kernels for 6%

profile of v1, /device:TPU:0, one launch (start us, length us, event | category | flops | bytes accessed | tf_op | source)
XLA Modules:
  0.0 40.0 jit_solution(148344692425726333)
XLA Ops:
  0.6 1.0 %edges.1 = (bf16[9,16,256]{2,1,0:T(8,128)(2,1)S(1)}, bf16[9,16,256]{2,1,0:T(8,128)(2,1)S(1)}, f32[32,128]{1,0:T(8,128)S(1)}) custom-call(f32[8,32,256]{2,1,0:T(8,128)} %right_hbm.3, f32[8,32,256]{2,1,0:T(8,128)} %weight_hbm.3, s32[9,8,32]{2,1,0:T(8,128)} %bitcast.10), custom_call_target="tpu_custom_call" | custom-call | tf_op jit(solution)/shard_map/edges/pallas_call | solution.py:311
  1.7 0.7 %collective-permute-start = (bf16[9,16,256]{2,1,0:T(8,128)(2,1)S(1)}, bf16[9,16,256]{2,1,0:T(8,128)(2,1)S(1)}, u32[]{:S(2)}, u32[]{:S(2)}) collective-permute-start(bf16[9,16,256]{2,1,0:T(8,128)(2,1)S(1)} %get-tuple-element.17), channel_id=1, source_target_pairs={{1,2},{2,1},{3,4},{4,3},{5,6},{6,5},{7,8},{8,7},{9,10},{10,9},{11,... | collective-permute-start | bytes 221192 | tf_op jit(solution)/shard_map/ppermute | solution.py:325
  2.3 5.7 %collective-permute-start.1 = (bf16[9,16,256]{2,1,0:T(8,128)(2,1)S(1)}, bf16[9,16,256]{2,1,0:T(8,128)(2,1)S(1)}, u32[]{:S(2)}, u32[]{:S(2)}) collective-permute-start(bf16[9,16,256]{2,1,0:T(8,128)(2,1)S(1)} %get-tuple-element.18), channel_id=1, source_target_pairs={{0,1},{1,0},{2,3},{3,2},{4,5},{5,4},{6,7},{7,6},{8,9},{9,8},{10,11... | collective-permute-start | bytes 221192 | tf_op jit(solution)/shard_map/ppermute | solution.py:326
  8.1 1.9 %own.1 = (bf16[9,64,256]{2,1,0:T(8,128)(2,1)S(1)}, bf16[9,256,256]{2,1,0:T(8,128)(2,1)S(1)}, bf16[9,8,32,128]{3,2,1,0:T(8,128)(2,1)S(1)}, f32[8,32,256]{2,1,0:T(8,128)S(1)}, f32[8,32,256]{2,1,0:T(8,128)S(1)}) custom-call(bf16[9,256,256]{2,1,0:T(8,128)(2,1)} %stencil_hbm.1, f32[8,32,256]{2,1,0:T(8,128)} %right_hbm.3, f32[8,32,256]{2,1,0:T(8,128)} %weight_hbm.3, ...), custom_call_target="tpu_custom_call" | custom-call | bytes 6000000 | tf_op jit(solution)/shard_map/own/pallas_call | solution.py:343
  10.0 0.1 collective-permute-start.3
  10.1 0.0 collective-permute-done.refs_1_
  10.1 1.5 %collective-permute-done.1.refs_2_ = bf16[9,16,256]{2,1,0:T(8,128)(2,1)S(1)} collective-permute-done((bf16[9,16,256]{2,1,0:T(8,128)(2,1)S(1)}, bf16[9,16,256]{2,1,0:T(8,128)(2,1)S(1)}, u32[]{:S(2)}, u32[]{:S(2)}) %collective-permute-start.1) | collective-permute-done | bytes 73760 | tf_op jit(solution)/shard_map/ppermute | solution.py:326
  11.6 0.1 collective-permute-start.2
  11.6 0.0 collective-permute-done.3.refs_0_
  11.7 0.3 rows.1
  12.0 1.0 %collective-permute-done.2.refs_3_ = bf16[2,9,16,256]{3,2,1,0:T(8,128)(2,1)S(1)} collective-permute-done((bf16[2,9,16,256]{3,2,1,0:T(8,128)(2,1)S(1)}, bf16[2,9,16,256]{3,2,1,0:T(8,128)(2,1)S(1)}, u32[]{:S(2)}, u32[]{:S(2)}) %collective-permute-start.2) | collective-permute-done | bytes 147488 | tf_op jit(solution)/shard_map/ppermute | solution.py:360
  13.0 8.2 %smooth.1 = (f32[8,32,256]{2,1,0:T(8,128)}, bf16[4,16,256]{2,1,0:T(8,128)(2,1)S(1)}) custom-call(bf16[9,256,256]{2,1,0:T(8,128)(2,1)S(1)} %get-tuple-element.16.refs_0_, bf16[9,16,256]{2,1,0:T(8,128)(2,1)S(1)} %collective-permute-done.refs_1_, bf16[9,16,256]{2,1,0:T(8,128)(2,1)S(1)} %collective-permute-done.1.refs_2_, ...), custom_call_target="tpu_custom_call" | custom-call | tf_op jit(solution)/shard_map/smooth/pallas_call | solution.py:374
  21.2 2.9 %collective-permute-start.4 = (bf16[4,16,256]{2,1,0:T(8,128)(2,1)S(1)}, bf16[4,16,256]{2,1,0:T(8,128)(2,1)S(1)}, u32[]{:S(2)}, u32[]{:S(2)}) collective-permute-start(bf16[4,16,256]{2,1,0:T(8,128)(2,1)S(1)} %get-tuple-element.27), channel_id=1, source_target_pairs={{0,8},{1,9},{2,10},{3,11},{4,12},{5,13},{6,14},{7,15},{8,0},{9,1},... | collective-permute-start | bytes 98312 | tf_op jit(solution)/shard_map/ppermute | solution.py:397
  24.1 1.9 %collective-permute-done.4 = bf16[4,16,256]{2,1,0:T(8,128)(2,1)S(1)} collective-permute-done((bf16[4,16,256]{2,1,0:T(8,128)(2,1)S(1)}, bf16[4,16,256]{2,1,0:T(8,128)(2,1)S(1)}, u32[]{:S(2)}, u32[]{:S(2)}) %collective-permute-start.4) | collective-permute-done | bytes 32800 | tf_op jit(solution)/shard_map/ppermute | solution.py:397
  26.1 12.9 %all_to_all.5.block_ref = bf16[8,2,4,16,256]{4,3,2,1,0:T(8,128)(2,1)S(1)} all-to-all(bf16[8,2,4,16,256]{4,3,2,1,0:T(8,128)(2,1)S(1)} %broadcast_in_dim.2), channel_id=1, replica_groups={{0,1,2,3,4,5,6,7},{8,9,10,11,12,13,14,15},{16,17,18,19,20,21,22,23},{24..., dimensions={0} | all-to-all | bytes 1048576 | tf_op jit(solution)/shard_map/all_to_all | solution.py:400
  38.9 1.0 %widen.1 = f32[4,16,16,256]{3,2,1,0:T(8,128)} custom-call(bf16[8,2,4,16,256]{4,3,2,1,0:T(8,128)(2,1)S(1)} %all_to_all.5.block_ref), custom_call_target="tpu_custom_call" | custom-call | tf_op jit(solution)/shard_map/widen/pallas_call | solution.py:402
  (3 shorter events, 0.1 us)
Async XLA Ops:
  1.7 8.4 %collective-permute-start = (bf16[9,16,256]{2,1,0:T(8,128)(2,1)S(1)}, bf16[9,16,256]{2,1,0:T(8,128)(2,1)S(1)}, u32[]{:S(2)}, u32[]{:S(2)}) collective-permute-start(bf16[9,16,256]{2,1,0:T(8,128)(2,1)S(1)} %get-tuple-element.17), channel_id=1, source_target_pairs={{1,2},{2,1},{3,4},{4,3},{5,6},{6,5},{7,8},{8,7},{9,10},{10,9},{11,... | collective-permute-start | bytes 221192 | tf_op jit(solution)/shard_map/ppermute | solution.py:325
  2.3 9.2 %collective-permute-start.1 = (bf16[9,16,256]{2,1,0:T(8,128)(2,1)S(1)}, bf16[9,16,256]{2,1,0:T(8,128)(2,1)S(1)}, u32[]{:S(2)}, u32[]{:S(2)}) collective-permute-start(bf16[9,16,256]{2,1,0:T(8,128)(2,1)S(1)} %get-tuple-element.18), channel_id=1, source_target_pairs={{0,1},{1,0},{2,3},{3,2},{4,5},{5,4},{6,7},{7,6},{8,9},{9,8},{10,11... | collective-permute-start | bytes 221192 | tf_op jit(solution)/shard_map/ppermute | solution.py:326
  10.0 1.6 %collective-permute-start.3 = (bf16[9,64,256]{2,1,0:T(8,128)(2,1)S(1)}, bf16[9,64,256]{2,1,0:T(8,128)(2,1)S(1)}, u32[]{:S(2)}, u32[]{:S(2)}) collective-permute-start(bf16[9,64,256]{2,1,0:T(8,128)(2,1)S(1)} %get-tuple-element.22), channel_id=1, source_target_pairs={{0,16},{16,0},{1,17},{17,1},{2,18},{18,2},{3,19},{19,3},{4,20},{20... | collective-permute-start | bytes 884744 | tf_op jit(solution)/shard_map/ppermute | solution.py:358
  11.6 1.4 %collective-permute-start.2 = (bf16[2,9,16,256]{3,2,1,0:T(8,128)(2,1)S(1)}, bf16[2,9,16,256]{3,2,1,0:T(8,128)(2,1)S(1)}, u32[]{:S(2)}, u32[]{:S(2)}) collective-permute-start(bf16[2,9,16,256]{3,2,1,0:T(8,128)(2,1)S(1)} %pad_maximum_fusion), channel_id=1, source_target_pairs={{0,16},{16,0},{1,17},{17,1},{2,18},{18,2},{3,19},{19,3},{4,20},{20... | collective-permute-start | bytes 442376 | tf_op jit(solution)/shard_map/ppermute | solution.py:360
  21.2 4.8 %collective-permute-start.4 = (bf16[4,16,256]{2,1,0:T(8,128)(2,1)S(1)}, bf16[4,16,256]{2,1,0:T(8,128)(2,1)S(1)}, u32[]{:S(2)}, u32[]{:S(2)}) collective-permute-start(bf16[4,16,256]{2,1,0:T(8,128)(2,1)S(1)} %get-tuple-element.27), channel_id=1, source_target_pairs={{0,8},{1,9},{2,10},{3,11},{4,12},{5,13},{6,14},{7,15},{8,0},{9,1},... | collective-permute-start | bytes 98312 | tf_op jit(solution)/shard_map/ppermute | solution.py:397

commit v2 on v1

--- a/solution.py
+++ b/solution.py
@@ -12,6 +12,7 @@
 STEPS = DEG * SWEEPS
 SIDE = 8
 LANES = 128
+PIECE_ROWS = 4
 
 lower_edge = 1.5
 upper_edge = 6.0
@@ -231,7 +232,9 @@
         count = own_rows + ends * margin
         start = own_start - (ends - 1) * margin
         width = own_cols if last else cols
-        for base, size in ((start, count),):
+        pieces = -(-count // PIECE_ROWS)
+        cuts = [start + count * i // pieces for i in range(pieces + 1)]
+        for base, size in zip(cuts, (high - low for low, high in zip(cuts, cuts[1:]))):
             here = slice(base, base + size)
             picked = []
             for slot in range(slots):

time: 40.2 us -> 37.4 us (0.930)
  Pallas kernels: 12.4 us -> 9.66 us
    pallas_call x1, Pallas kernels: 8.17 us -> 5.4 us  [body(): pl.pallas_call(functools.partial(smooth_kernel, ends), out_shape=(jax.Sha...]
where the time goes in v2:
time: 37.4 us; the launch traced here: 37.2 us
  blocking collectives  12.9 us (34%)
  Pallas kernels  9.66 us (26%)
  starting transfers between devices  9.48 us (25%)
  waiting for transfers between devices  4.39 us (12%)
  between operations  0.71 us (2%)
    all_to_all x1, blocking collectives, body(): block = lax.all_to_all(spread, 'fcol', 0, 0, axis_index_groups=halves)  12.9 us
    ppermute x1, starting transfers between devices, body(): even_side = lax.ppermute(even, 'fcol', swaps[0])  5.74 us
    pallas_call x1, Pallas kernels, body(): pl.pallas_call(functools.partial(smooth_kernel, ends), out_shape=(jax.Sha...  5.4 us
    ppermute x1, starting transfers between devices, body(): pair = jnp.stack([coarse, lax.ppermute(coarse, 'fcol', across)])  2.94 us
    pallas_call x1, Pallas kernels, body(): pl.pallas_call(functools.partial(own_kernel, ends), out_shape=(pltpu.VMEM...  1.92 us
    ppermute x1, waiting for transfers between devices, body(): pair = jnp.stack([coarse, lax.ppermute(coarse, 'fcol', across)])  1.89 us
    ppermute x1, waiting for transfers between devices, body(): even_side = lax.ppermute(even, 'fcol', swaps[0])  1.46 us
    ppermute x1, waiting for transfers between devices, body(): sides_held = [lax.ppermute(sides, 'frow', move) for move in moves]  1.04 us
  transfers between devices with their start and end apart: 5, of which 3 were waited for; matrix products, arithmetic and copies ran while one was open for 0% of the time, Pallas kernels for 6%

profile of v2, /device:TPU:0, one launch (start us, length us, event | category | flops | bytes accessed | tf_op | source)
XLA Modules:
  0.0 37.2 jit_solution(17097976678247907014)
XLA Ops:
  0.6 1.0 %edges.1 = (bf16[9,16,256]{2,1,0:T(8,128)(2,1)S(1)}, bf16[9,16,256]{2,1,0:T(8,128)(2,1)S(1)}, f32[32,128]{1,0:T(8,128)S(1)}) custom-call(f32[8,32,256]{2,1,0:T(8,128)} %right_hbm.3, f32[8,32,256]{2,1,0:T(8,128)} %weight_hbm.3, s32[9,8,32]{2,1,0:T(8,128)} %bitcast.10), custom_call_target="tpu_custom_call" | custom-call | tf_op jit(solution)/shard_map/edges/pallas_call | solution.py:314
  1.7 0.7 %collective-permute-start = (bf16[9,16,256]{2,1,0:T(8,128)(2,1)S(1)}, bf16[9,16,256]{2,1,0:T(8,128)(2,1)S(1)}, u32[]{:S(2)}, u32[]{:S(2)}) collective-permute-start(bf16[9,16,256]{2,1,0:T(8,128)(2,1)S(1)} %get-tuple-element.17), channel_id=1, source_target_pairs={{1,2},{2,1},{3,4},{4,3},{5,6},{6,5},{7,8},{8,7},{9,10},{10,9},{11,... | collective-permute-start | bytes 221192 | tf_op jit(solution)/shard_map/ppermute | solution.py:328
  2.3 5.7 %collective-permute-start.1 = (bf16[9,16,256]{2,1,0:T(8,128)(2,1)S(1)}, bf16[9,16,256]{2,1,0:T(8,128)(2,1)S(1)}, u32[]{:S(2)}, u32[]{:S(2)}) collective-permute-start(bf16[9,16,256]{2,1,0:T(8,128)(2,1)S(1)} %get-tuple-element.18), channel_id=1, source_target_pairs={{0,1},{1,0},{2,3},{3,2},{4,5},{5,4},{6,7},{7,6},{8,9},{9,8},{10,11... | collective-permute-start | bytes 221192 | tf_op jit(solution)/shard_map/ppermute | solution.py:329
  8.1 1.9 %own.1 = (bf16[9,64,256]{2,1,0:T(8,128)(2,1)S(1)}, bf16[9,256,256]{2,1,0:T(8,128)(2,1)S(1)}, bf16[9,8,32,128]{3,2,1,0:T(8,128)(2,1)S(1)}, f32[8,32,256]{2,1,0:T(8,128)S(1)}, f32[8,32,256]{2,1,0:T(8,128)S(1)}) custom-call(bf16[9,256,256]{2,1,0:T(8,128)(2,1)} %stencil_hbm.1, f32[8,32,256]{2,1,0:T(8,128)} %right_hbm.3, f32[8,32,256]{2,1,0:T(8,128)} %weight_hbm.3, ...), custom_call_target="tpu_custom_call" | custom-call | bytes 6000000 | tf_op jit(solution)/shard_map/own/pallas_call | solution.py:346
  10.0 0.1 collective-permute-start.3
  10.1 0.0 collective-permute-done.refs_1_
  10.1 1.5 %collective-permute-done.1.refs_2_ = bf16[9,16,256]{2,1,0:T(8,128)(2,1)S(1)} collective-permute-done((bf16[9,16,256]{2,1,0:T(8,128)(2,1)S(1)}, bf16[9,16,256]{2,1,0:T(8,128)(2,1)S(1)}, u32[]{:S(2)}, u32[]{:S(2)}) %collective-permute-start.1) | collective-permute-done | bytes 73760 | tf_op jit(solution)/shard_map/ppermute | solution.py:329
  11.6 0.1 collective-permute-start.2
  11.6 0.0 collective-permute-done.3.refs_0_
  11.7 0.3 rows.1
  12.0 1.0 %collective-permute-done.2.refs_3_ = bf16[2,9,16,256]{3,2,1,0:T(8,128)(2,1)S(1)} collective-permute-done((bf16[2,9,16,256]{3,2,1,0:T(8,128)(2,1)S(1)}, bf16[2,9,16,256]{3,2,1,0:T(8,128)(2,1)S(1)}, u32[]{:S(2)}, u32[]{:S(2)}) %collective-permute-start.2) | collective-permute-done | bytes 147488 | tf_op jit(solution)/shard_map/ppermute | solution.py:363
  13.0 5.4 %smooth.1 = (f32[8,32,256]{2,1,0:T(8,128)}, bf16[4,16,256]{2,1,0:T(8,128)(2,1)S(1)}) custom-call(bf16[9,256,256]{2,1,0:T(8,128)(2,1)S(1)} %get-tuple-element.16.refs_0_, bf16[9,16,256]{2,1,0:T(8,128)(2,1)S(1)} %collective-permute-done.refs_1_, bf16[9,16,256]{2,1,0:T(8,128)(2,1)S(1)} %collective-permute-done.1.refs_2_, ...), custom_call_target="tpu_custom_call" | custom-call | tf_op jit(solution)/shard_map/smooth/pallas_call | solution.py:377
  18.4 2.9 %collective-permute-start.4 = (bf16[4,16,256]{2,1,0:T(8,128)(2,1)S(1)}, bf16[4,16,256]{2,1,0:T(8,128)(2,1)S(1)}, u32[]{:S(2)}, u32[]{:S(2)}) collective-permute-start(bf16[4,16,256]{2,1,0:T(8,128)(2,1)S(1)} %get-tuple-element.27), channel_id=1, source_target_pairs={{0,8},{1,9},{2,10},{3,11},{4,12},{5,13},{6,14},{7,15},{8,0},{9,1},... | collective-permute-start | bytes 98312 | tf_op jit(solution)/shard_map/ppermute | solution.py:400
  21.3 1.9 %collective-permute-done.4 = bf16[4,16,256]{2,1,0:T(8,128)(2,1)S(1)} collective-permute-done((bf16[4,16,256]{2,1,0:T(8,128)(2,1)S(1)}, bf16[4,16,256]{2,1,0:T(8,128)(2,1)S(1)}, u32[]{:S(2)}, u32[]{:S(2)}) %collective-permute-start.4) | collective-permute-done | bytes 32800 | tf_op jit(solution)/shard_map/ppermute | solution.py:400
  23.3 12.9 %all_to_all.5.block_ref = bf16[8,2,4,16,256]{4,3,2,1,0:T(8,128)(2,1)S(1)} all-to-all(bf16[8,2,4,16,256]{4,3,2,1,0:T(8,128)(2,1)S(1)} %broadcast_in_dim.2), channel_id=1, replica_groups={{0,1,2,3,4,5,6,7},{8,9,10,11,12,13,14,15},{16,17,18,19,20,21,22,23},{24..., dimensions={0} | all-to-all | bytes 1048576 | tf_op jit(solution)/shard_map/all_to_all | solution.py:403
  36.2 1.0 %widen.1 = f32[4,16,16,256]{3,2,1,0:T(8,128)} custom-call(bf16[8,2,4,16,256]{4,3,2,1,0:T(8,128)(2,1)S(1)} %all_to_all.5.block_ref), custom_call_target="tpu_custom_call" | custom-call | tf_op jit(solution)/shard_map/widen/pallas_call | solution.py:405
  (3 shorter events, 0.1 us)
Async XLA Ops:
  1.7 8.4 %collective-permute-start = (bf16[9,16,256]{2,1,0:T(8,128)(2,1)S(1)}, bf16[9,16,256]{2,1,0:T(8,128)(2,1)S(1)}, u32[]{:S(2)}, u32[]{:S(2)}) collective-permute-start(bf16[9,16,256]{2,1,0:T(8,128)(2,1)S(1)} %get-tuple-element.17), channel_id=1, source_target_pairs={{1,2},{2,1},{3,4},{4,3},{5,6},{6,5},{7,8},{8,7},{9,10},{10,9},{11,... | collective-permute-start | bytes 221192 | tf_op jit(solution)/shard_map/ppermute | solution.py:328
  2.3 9.2 %collective-permute-start.1 = (bf16[9,16,256]{2,1,0:T(8,128)(2,1)S(1)}, bf16[9,16,256]{2,1,0:T(8,128)(2,1)S(1)}, u32[]{:S(2)}, u32[]{:S(2)}) collective-permute-start(bf16[9,16,256]{2,1,0:T(8,128)(2,1)S(1)} %get-tuple-element.18), channel_id=1, source_target_pairs={{0,1},{1,0},{2,3},{3,2},{4,5},{5,4},{6,7},{7,6},{8,9},{9,8},{10,11... | collective-permute-start | bytes 221192 | tf_op jit(solution)/shard_map/ppermute | solution.py:329
  10.0 1.6 %collective-permute-start.3 = (bf16[9,64,256]{2,1,0:T(8,128)(2,1)S(1)}, bf16[9,64,256]{2,1,0:T(8,128)(2,1)S(1)}, u32[]{:S(2)}, u32[]{:S(2)}) collective-permute-start(bf16[9,64,256]{2,1,0:T(8,128)(2,1)S(1)} %get-tuple-element.22), channel_id=1, source_target_pairs={{0,16},{16,0},{1,17},{17,1},{2,18},{18,2},{3,19},{19,3},{4,20},{20... | collective-permute-start | bytes 884744 | tf_op jit(solution)/shard_map/ppermute | solution.py:361
  11.6 1.4 %collective-permute-start.2 = (bf16[2,9,16,256]{3,2,1,0:T(8,128)(2,1)S(1)}, bf16[2,9,16,256]{3,2,1,0:T(8,128)(2,1)S(1)}, u32[]{:S(2)}, u32[]{:S(2)}) collective-permute-start(bf16[2,9,16,256]{3,2,1,0:T(8,128)(2,1)S(1)} %pad_maximum_fusion), channel_id=1, source_target_pairs={{0,16},{16,0},{1,17},{17,1},{2,18},{18,2},{3,19},{19,3},{4,20},{20... | collective-permute-start | bytes 442376 | tf_op jit(solution)/shard_map/ppermute | solution.py:363
  18.4 4.8 %collective-permute-start.4 = (bf16[4,16,256]{2,1,0:T(8,128)(2,1)S(1)}, bf16[4,16,256]{2,1,0:T(8,128)(2,1)S(1)}, u32[]{:S(2)}, u32[]{:S(2)}) collective-permute-start(bf16[4,16,256]{2,1,0:T(8,128)(2,1)S(1)} %get-tuple-element.27), channel_id=1, source_target_pairs={{0,8},{1,9},{2,10},{3,11},{4,12},{5,13},{6,14},{7,15},{8,0},{9,1},... | collective-permute-start | bytes 98312 | tf_op jit(solution)/shard_map/ppermute | solution.py:400

commit v3 on v2

--- a/solution.py
+++ b/solution.py
@@ -12,6 +12,7 @@
 STEPS = DEG * SWEEPS
 SIDE = 8
 LANES = 128
+STRIPS = ((0, STEPS - 1), (SIDE - STEPS, 0))
 PIECE_ROWS = 4
 
 lower_edge = 1.5
@@ -69,7 +70,7 @@
 
 
 def edge_kernel(right_hbm, weight_hbm, near_hbm, *refs):
-    odd_ref, even_ref, held_ref, strips, near_ref, arrived = refs
+    odd_ref, even_ref, held_ref, strips, flat, near_ref, arrived = refs
     slots, rows, cols = near_ref.shape
     copies = [pltpu.make_async_copy(near_hbm, near_ref, arrived.at[4])]
     for end, start in enumerate((0, cols - SIDE)):
@@ -91,15 +92,17 @@
     held_ref[...] = turned
     for copy in copies[1:]:
         copy.wait()
+    for end, (low, far) in enumerate(STRIPS):
+        for row in range(rows):
+            base = 2 * STEPS * row
+            flat[end, base : base + STEPS] = strips[end, 0, row, low : low + STEPS]
+            weight = strips[end, 1, row, low : low + STEPS] - weight_middle
+            flat[end, base + STEPS : base + 2 * STEPS] = weight
+            column = row + end * (cols - SIDE)
+            flat[end, base + STEPS + far, :LANES] = turned[column]
     parity = lax.rem(lax.axis_index("fcol"), 2)
-    flags = [turned[:SIDE], turned[cols - SIDE :]]
-    for ref, end in ((odd_ref, parity), (even_ref, 1 - parity)):
-        ref[:rows] = jnp.concatenate([strips[end, 0], strips[end, 1] - weight_middle], 1).astype(
-            BF16
-        )
-        strip = jnp.where(end == 0, flags[0], flags[1])
-        strip = jnp.concatenate([strip, jnp.zeros((SIDE, LANES), F32)], 0)
-        ref[rows, :, :LANES] = strip.astype(BF16)
+    odd_ref[...] = flat[parity].astype(BF16)
+    even_ref[...] = flat[1 - parity].astype(BF16)
 
 
 def own_kernel(ends, stencil_hbm, right_hbm, weight_hbm, held_ref, *refs):
@@ -159,7 +162,9 @@
     own_block = refs[3 + ends : 6 + ends]
     halo_blocks = [refs[6 + ends + 3 * i : 9 + ends + 3 * i] for i in range(ends)]
     solution_ref, coarse_ref = refs[6 + 4 * ends : 8 + 4 * ends]
-    residual, weight, direction, shifted, side_mask, smoothed, summed = refs[8 + 4 * ends :]
+    residual, weight, direction, shifted, side_mask, strips, turned, smoothed, summed = refs[
+        8 + 4 * ends :
+    ]
     own_rows, own_cols, pixels = solution_ref.shape
     slots = side_mask.shape[0]
     rows, cols, _ = residual.shape
@@ -180,30 +185,34 @@
 
     first_of_even = lax.rem(lax.axis_index("fcol"), 2) == 0
 
-    def fill(base, block, odd, even, places):
+    def fill(index, base, block, odd, even, places):
         here = slice(base, base + block[1].shape[0])
         residual[here, :own_cols, :] = block[1][...]
         weight[here, :own_cols, :] = block[2][...]
-
-        def in_order(odd_piece, even_piece):
-            after = jnp.where(first_of_even, even_piece, odd_piece)
-            before = jnp.where(first_of_even, odd_piece, even_piece)
-            return after, before
-
-        flags = in_order(*(piece[own_rows, :, :LANES].astype(F32)[:SIDE] for piece in (odd, even)))
+        unused = jnp.zeros((block[1].shape[0], cols - own_cols, pixels), F32)
+        residual[here, own_cols:, :] = unused
+        weight[here, own_cols:, :] = unused
+        strips[index, 0] = jnp.where(first_of_even, even[...], odd[...]).astype(F32)
+        strips[index, 1] = jnp.where(first_of_even, odd[...], even[...]).astype(F32)
         places = [(row, base + at) for row, at in places]
-        spread_flags(ends, side_mask, jnp.concatenate(flags, 0), own_rows, places)
-        for row, at in places:
-            after, before = in_order(odd[row].astype(F32), even[row].astype(F32))
-            residual[at, own_cols : own_cols + SIDE, :] = after[:SIDE]
-            residual[at, own_cols + SIDE :, :] = before[:SIDE]
-            weight[at, own_cols : own_cols + SIDE, :] = after[SIDE:] + weight_middle
-            weight[at, own_cols + SIDE :, :] = before[SIDE:] + weight_middle
-
-    fill(own_start, own_block, odd_ref, even_ref, list(enumerate(place)))
+        for end, (low, far) in enumerate(STRIPS):
+            side = slice(own_cols + end * SIDE + low, own_cols + end * SIDE + low + STEPS)
+            for row, at in places:
+                flat = 2 * STEPS * row
+                residual[at, side, :] = strips[index, end, flat : flat + STEPS]
+                moved = strips[index, end, flat + STEPS : flat + 2 * STEPS]
+                weight[at, side, :] = moved + weight_middle
+            for column in range(SIDE):
+                flat = 2 * STEPS * column + STEPS + far
+                turned[index, end * SIDE + column] = strips[index, end, flat, :LANES]
+        spread_flags(ends, side_mask, turned[index], own_rows, places)
+
+    fill(0, own_start, own_block, odd_ref, even_ref, list(enumerate(place)))
     halo_bases = bases[:ahead] + bases[ahead + 1 : -1]
-    for base, block, sides_ref, places in zip(halo_bases, halo_blocks, sides, halos):
-        fill(base, block, sides_ref.at[0], sides_ref.at[1], places)
+    for index, (base, block, sides_ref, places) in enumerate(
+        zip(halo_bases, halo_blocks, sides, halos)
+    ):
+        fill(1 + index, base, block, sides_ref.at[0], sides_ref.at[1], places)
 
     def put_direction(slot, start, count, value):
         here = slice(start + 1, start + 1 + count)
@@ -310,7 +319,7 @@
     ]
     small = pltpu.CompilerParams(vmem_limit_bytes=8 * 1024 * 1024)
 
-    side = pltpu.VMEM((rows + 1, 2 * SIDE, pixels), BF16)
+    side = pltpu.VMEM((2 * STEPS * rows, pixels), BF16)
     odd, even, held = pl.pallas_call(
         edge_kernel,
         out_shape=(side, side, pltpu.VMEM((cols, LANES), F32)),
@@ -318,6 +327,7 @@
         out_specs=(VMEM_SPEC,) * 3,
         scratch_shapes=[
             pltpu.VMEM((2, 2, rows, SIDE, pixels), F32),
+            pltpu.VMEM((2, 2 * STEPS * rows, pixels), F32),
             pltpu.VMEM((slots, rows, cols), jnp.int32),
             pltpu.SemaphoreType.DMA((5,)),
         ],
@@ -388,6 +398,8 @@
             pltpu.VMEM((rows_held, cols_held, pixels), F32),
             pltpu.VMEM((2, 3, rows_held + 2, cols_held, pixels), BF16),
             pltpu.VMEM((slots, rows_held, 2 * SIDE, LANES), BF16),
+            pltpu.VMEM((1 + ends, 2, 2 * STEPS * rows, pixels), F32),
+            pltpu.VMEM((1 + ends, 2 * SIDE, LANES), F32),
             pltpu.VMEM((rows, cols, pixels), F32),
             pltpu.VMEM((rows, cols, LANES), F32),
         ],

time: 37.4 us -> 39.3 us (1.051)
  waiting for transfers between devices: 4.39 us -> 5.93 us
    ppermute x1, waiting for transfers between devices: 1.46 us -> 3.07 us  [body(): even_side = lax.ppermute(even, 'fcol', swaps[0])]
    ppermute x1, starting transfers between devices: 0.07 us -> 0.52 us  [body(): wholes = [lax.ppermute(whole, 'frow', move) for move in moves]]
    ppermute x1, starting transfers between devices: 5.74 us -> 5.31 us  [body(): even_side = lax.ppermute(even, 'fcol', swaps[0])]
  transfers between devices with their start and end apart: 5 -> 5, of which waited for: 3 -> 3; matrix products, arithmetic and copies ran while one was open for 0% -> 0% of each run, Pallas kernels for 6% -> 1%
where the time goes in v3:
time: 39.3 us; the launch traced here: 39 us
  blocking collectives  13.1 us (33%)
  Pallas kernels  9.78 us (25%)
  starting transfers between devices  9.51 us (24%)
  waiting for transfers between devices  5.93 us (15%)
  between operations  0.69 us (2%)
    all_to_all x1, blocking collectives, body(): block = lax.all_to_all(spread, 'fcol', 0, 0, axis_index_groups=halves)  13.1 us
    pallas_call x1, Pallas kernels, body(): pl.pallas_call(functools.partial(smooth_kernel, ends), out_shape=(jax.Sha...  5.47 us
    ppermute x1, starting transfers between devices, body(): even_side = lax.ppermute(even, 'fcol', swaps[0])  5.31 us
    ppermute x1, waiting for transfers between devices, body(): even_side = lax.ppermute(even, 'fcol', swaps[0])  3.07 us
    ppermute x1, starting transfers between devices, body(): pair = jnp.stack([coarse, lax.ppermute(coarse, 'fcol', across)])  2.96 us
    pallas_call x1, Pallas kernels, body(): pl.pallas_call(functools.partial(own_kernel, ends), out_shape=(pltpu.VMEM...  1.92 us
    ppermute x1, waiting for transfers between devices, body(): pair = jnp.stack([coarse, lax.ppermute(coarse, 'fcol', across)])  1.89 us
    pallas_call x1, Pallas kernels, body(): pl.pallas_call(edge_kernel, out_shape=(side, side, pltpu.VMEM((cols, LANE...  1.05 us
  transfers between devices with their start and end apart: 5, of which 3 were waited for; matrix products, arithmetic and copies ran while one was open for 0% of the time, Pallas kernels for 1%

profile of v3, /device:TPU:0, one launch (start us, length us, event | category | flops | bytes accessed | tf_op | source)
XLA Modules:
  0.0 39.0 jit_solution(2965822830182231230)
XLA Ops:
  0.6 1.1 %edges.1 = (bf16[96,256]{1,0:T(8,128)(2,1)S(1)}, bf16[96,256]{1,0:T(8,128)(2,1)S(1)}, f32[32,128]{1,0:T(8,128)S(1)}) custom-call(f32[8,32,256]{2,1,0:T(8,128)} %right_hbm.3, f32[8,32,256]{2,1,0:T(8,128)} %weight_hbm.3, s32[9,8,32]{2,1,0:T(8,128)} %bitcast.10), custom_call_target="tpu_custom_call" | custom-call | tf_op jit(solution)/shard_map/edges/pallas_call | solution.py:323
  1.7 1.9 %own.1 = (bf16[9,64,256]{2,1,0:T(8,128)(2,1)S(1)}, bf16[9,256,256]{2,1,0:T(8,128)(2,1)S(1)}, bf16[9,8,32,128]{3,2,1,0:T(8,128)(2,1)S(1)}, f32[8,32,256]{2,1,0:T(8,128)S(1)}, f32[8,32,256]{2,1,0:T(8,128)S(1)}) custom-call(bf16[9,256,256]{2,1,0:T(8,128)(2,1)} %stencil_hbm.1, f32[8,32,256]{2,1,0:T(8,128)} %right_hbm.3, f32[8,32,256]{2,1,0:T(8,128)} %weight_hbm.3, ...), custom_call_target="tpu_custom_call" | custom-call | bytes 6000000 | tf_op jit(solution)/shard_map/own/pallas_call | solution.py:356
  3.6 0.5 %collective-permute-start.3 = (bf16[9,64,256]{2,1,0:T(8,128)(2,1)S(1)}, bf16[9,64,256]{2,1,0:T(8,128)(2,1)S(1)}, u32[]{:S(2)}, u32[]{:S(2)}) collective-permute-start(bf16[9,64,256]{2,1,0:T(8,128)(2,1)S(1)} %get-tuple-element.22), channel_id=1, source_target_pairs={{0,16},{16,0},{1,17},{17,1},{2,18},{18,2},{3,19},{19,3},{4,20},{20... | collective-permute-start | bytes 884744 | tf_op jit(solution)/shard_map/ppermute | solution.py:371
  4.1 0.7 %collective-permute-start = (bf16[96,256]{1,0:T(8,128)(2,1)S(1)}, bf16[96,256]{1,0:T(8,128)(2,1)S(1)}, u32[]{:S(2)}, u32[]{:S(2)}) collective-permute-start(bf16[96,256]{1,0:T(8,128)(2,1)S(1)} %get-tuple-element.17), channel_id=1, source_target_pairs={{1,2},{2,1},{3,4},{4,3},{5,6},{6,5},{7,8},{8,7},{9,10},{10,9},{11,... | collective-permute-start | bytes 147464 | tf_op jit(solution)/shard_map/ppermute | solution.py:338
  4.8 5.3 %collective-permute-start.1 = (bf16[96,256]{1,0:T(8,128)(2,1)S(1)}, bf16[96,256]{1,0:T(8,128)(2,1)S(1)}, u32[]{:S(2)}, u32[]{:S(2)}) collective-permute-start(bf16[96,256]{1,0:T(8,128)(2,1)S(1)} %get-tuple-element.18), channel_id=1, source_target_pairs={{0,1},{1,0},{2,3},{3,2},{4,5},{5,4},{6,7},{7,6},{8,9},{9,8},{10,11... | collective-permute-start | bytes 147464 | tf_op jit(solution)/shard_map/ppermute | solution.py:339
  10.1 0.0 collective-permute-done.refs_1_
  10.1 3.1 %collective-permute-done.1.refs_2_ = bf16[96,256]{1,0:T(8,128)(2,1)S(1)} collective-permute-done((bf16[96,256]{1,0:T(8,128)(2,1)S(1)}, bf16[96,256]{1,0:T(8,128)(2,1)S(1)}, u32[]{:S(2)}, u32[]{:S(2)}) %collective-permute-start.1) | collective-permute-done | bytes 49184 | tf_op jit(solution)/shard_map/ppermute | solution.py:339
  13.2 0.1 collective-permute-start.2
  13.3 0.0 collective-permute-done.3.refs_0_
  13.3 0.3 rows.1
  13.6 1.0 %collective-permute-done.2.refs_3_ = bf16[2,96,256]{2,1,0:T(8,128)(2,1)S(1)} collective-permute-done((bf16[2,96,256]{2,1,0:T(8,128)(2,1)S(1)}, bf16[2,96,256]{2,1,0:T(8,128)(2,1)S(1)}, u32[]{:S(2)}, u32[]{:S(2)}) %collective-permute-start.2) | collective-permute-done | bytes 98336 | tf_op jit(solution)/shard_map/ppermute | solution.py:373
  14.6 5.5 %smooth.1 = (f32[8,32,256]{2,1,0:T(8,128)}, bf16[4,16,256]{2,1,0:T(8,128)(2,1)S(1)}) custom-call(bf16[9,256,256]{2,1,0:T(8,128)(2,1)S(1)} %get-tuple-element.16.refs_0_, bf16[96,256]{1,0:T(8,128)(2,1)S(1)} %collective-permute-done.refs_1_, bf16[96,256]{1,0:T(8,128)(2,1)S(1)} %collective-permute-done.1.refs_2_, ...), custom_call_target="tpu_custom_call" | custom-call | tf_op jit(solution)/shard_map/smooth/pallas_call | solution.py:387
  20.0 3.0 %collective-permute-start.4 = (bf16[4,16,256]{2,1,0:T(8,128)(2,1)S(1)}, bf16[4,16,256]{2,1,0:T(8,128)(2,1)S(1)}, u32[]{:S(2)}, u32[]{:S(2)}) collective-permute-start(bf16[4,16,256]{2,1,0:T(8,128)(2,1)S(1)} %get-tuple-element.27), channel_id=1, source_target_pairs={{0,8},{1,9},{2,10},{3,11},{4,12},{5,13},{6,14},{7,15},{8,0},{9,1},... | collective-permute-start | bytes 98312 | tf_op jit(solution)/shard_map/ppermute | solution.py:412
  23.0 1.9 %collective-permute-done.4 = bf16[4,16,256]{2,1,0:T(8,128)(2,1)S(1)} collective-permute-done((bf16[4,16,256]{2,1,0:T(8,128)(2,1)S(1)}, bf16[4,16,256]{2,1,0:T(8,128)(2,1)S(1)}, u32[]{:S(2)}, u32[]{:S(2)}) %collective-permute-start.4) | collective-permute-done | bytes 32800 | tf_op jit(solution)/shard_map/ppermute | solution.py:412
  25.0 13.1 %all_to_all.5.block_ref = bf16[8,2,4,16,256]{4,3,2,1,0:T(8,128)(2,1)S(1)} all-to-all(bf16[8,2,4,16,256]{4,3,2,1,0:T(8,128)(2,1)S(1)} %broadcast_in_dim.2), channel_id=1, replica_groups={{0,1,2,3,4,5,6,7},{8,9,10,11,12,13,14,15},{16,17,18,19,20,21,22,23},{24..., dimensions={0} | all-to-all | bytes 1048576 | tf_op jit(solution)/shard_map/all_to_all | solution.py:415
  38.0 1.0 %widen.1 = f32[4,16,16,256]{3,2,1,0:T(8,128)} custom-call(bf16[8,2,4,16,256]{4,3,2,1,0:T(8,128)(2,1)S(1)} %all_to_all.5.block_ref), custom_call_target="tpu_custom_call" | custom-call | tf_op jit(solution)/shard_map/widen/pallas_call | solution.py:417
  (3 shorter events, 0.1 us)
Async XLA Ops:
  3.6 9.7 %collective-permute-start.3 = (bf16[9,64,256]{2,1,0:T(8,128)(2,1)S(1)}, bf16[9,64,256]{2,1,0:T(8,128)(2,1)S(1)}, u32[]{:S(2)}, u32[]{:S(2)}) collective-permute-start(bf16[9,64,256]{2,1,0:T(8,128)(2,1)S(1)} %get-tuple-element.22), channel_id=1, source_target_pairs={{0,16},{16,0},{1,17},{17,1},{2,18},{18,2},{3,19},{19,3},{4,20},{20... | collective-permute-start | bytes 884744 | tf_op jit(solution)/shard_map/ppermute | solution.py:371
  4.1 6.0 %collective-permute-start = (bf16[96,256]{1,0:T(8,128)(2,1)S(1)}, bf16[96,256]{1,0:T(8,128)(2,1)S(1)}, u32[]{:S(2)}, u32[]{:S(2)}) collective-permute-start(bf16[96,256]{1,0:T(8,128)(2,1)S(1)} %get-tuple-element.17), channel_id=1, source_target_pairs={{1,2},{2,1},{3,4},{4,3},{5,6},{6,5},{7,8},{8,7},{9,10},{10,9},{11,... | collective-permute-start | bytes 147464 | tf_op jit(solution)/shard_map/ppermute | solution.py:338
  4.8 8.4 %collective-permute-start.1 = (bf16[96,256]{1,0:T(8,128)(2,1)S(1)}, bf16[96,256]{1,0:T(8,128)(2,1)S(1)}, u32[]{:S(2)}, u32[]{:S(2)}) collective-permute-start(bf16[96,256]{1,0:T(8,128)(2,1)S(1)} %get-tuple-element.18), channel_id=1, source_target_pairs={{0,1},{1,0},{2,3},{3,2},{4,5},{5,4},{6,7},{7,6},{8,9},{9,8},{10,11... | collective-permute-start | bytes 147464 | tf_op jit(solution)/shard_map/ppermute | solution.py:339
  13.2 1.4 %collective-permute-start.2 = (bf16[2,96,256]{2,1,0:T(8,128)(2,1)S(1)}, bf16[2,96,256]{2,1,0:T(8,128)(2,1)S(1)}, u32[]{:S(2)}, u32[]{:S(2)}) collective-permute-start(bf16[2,96,256]{2,1,0:T(8,128)(2,1)S(1)} %pad_maximum_fusion), channel_id=1, source_target_pairs={{0,16},{16,0},{1,17},{17,1},{2,18},{18,2},{3,19},{19,3},{4,20},{20... | collective-permute-start | bytes 294920 | tf_op jit(solution)/shard_map/ppermute | solution.py:373
  20.0 4.9 %collective-permute-start.4 = (bf16[4,16,256]{2,1,0:T(8,128)(2,1)S(1)}, bf16[4,16,256]{2,1,0:T(8,128)(2,1)S(1)}, u32[]{:S(2)}, u32[]{:S(2)}) collective-permute-start(bf16[4,16,256]{2,1,0:T(8,128)(2,1)S(1)} %get-tuple-element.27), channel_id=1, source_target_pairs={{0,8},{1,9},{2,10},{3,11},{4,12},{5,13},{6,14},{7,15},{8,0},{9,1},... | collective-permute-start | bytes 98312 | tf_op jit(solution)/shard_map/ppermute | solution.py:412

commit v4 on v3

--- a/solution.py
+++ b/solution.py
@@ -50,6 +50,15 @@
     above = [(own_rows - STEPS + row, row) for row in range(STEPS)]
     below = [(row, row) for row in range(STEPS)]
     return list(range(own_rows)), [above, below], 1
+
+
+def rows_sent(ends, own_rows):
+    if ends == 1:
+        return [([own_rows - 1 - row for row in range(STEPS)], STEPS - 1)]
+    return [
+        ([own_rows - STEPS + row for row in range(STEPS)], 0),
+        (list(range(STEPS)), STEPS - 1),
+    ]
 
 
 def slot_places(ends, slots):
@@ -106,7 +115,8 @@
 
 
 def own_kernel(ends, stencil_hbm, right_hbm, weight_hbm, held_ref, *refs):
-    whole_ref, stencil_ref, mask, residual, weight, arrived = refs
+    whole_refs = refs[:ends]
+    stencil_ref, mask, residual, weight, arrived = refs[ends:]
     slots = mask.shape[0]
     own_rows, own_cols, _ = residual.shape
     place, _, _ = row_places(ends, own_rows)
@@ -131,12 +141,16 @@
         copy.start()
     flags = held_ref[...]
     spread_flags(ends, mask, flags, own_rows, list(enumerate(place)))
-    whole_ref[own_rows, :own_cols, :LANES] = flags.astype(BF16)
     for copy in copies:
         copy.wait()
-    for row, at in enumerate(place):
-        whole_ref[row, :own_cols] = residual[at].astype(BF16)
-        whole_ref[row, own_cols:] = (weight[at] - weight_middle).astype(BF16)
+    for whole_ref, (sent, far) in zip(whole_refs, rows_sent(ends, own_rows)):
+        for row, at in enumerate(sent):
+            whole_ref[row, :own_cols] = residual[at].astype(BF16)
+            if row == far:
+                whole_ref[row, own_cols:, :LANES] = flags.astype(BF16)
+                whole_ref[row, own_cols:, LANES:] = flags.astype(BF16)
+            else:
+                whole_ref[row, own_cols:] = (weight[at] - weight_middle).astype(BF16)
     for copy in stencil_copies:
         copy.wait()
 
@@ -145,14 +159,14 @@
     for index in range(ends):
         whole_ref = refs[index]
         mask, residual, weight = refs[ends + 3 * index : ends + 3 * index + 3]
-        own_rows = whole_ref.shape[0] - 1
-        own_cols = residual.shape[1]
+        own_rows, own_cols = mask.shape[1], residual.shape[1]
+        for row in range(STEPS):
+            strip = whole_ref[row].astype(F32)
+            residual[row] = strip[:own_cols]
+            weight[row] = strip[own_cols:] + weight_middle
+        far = rows_sent(ends, own_rows)[index][1]
+        flags = whole_ref[far, own_cols:, :LANES].astype(F32)
         places = row_places(ends, own_rows)[1][index]
-        for row, at in places:
-            strip = whole_ref[row].astype(F32)
-            residual[at] = strip[:own_cols]
-            weight[at] = strip[own_cols:] + weight_middle
-        flags = whole_ref[own_rows, :own_cols, :LANES].astype(F32)
         spread_flags(ends, mask, flags, own_rows, places)
 
 
@@ -173,6 +187,10 @@
     bases = [0]
     for block in blocks:
         bases.append(bases[-1] + block[1].shape[0])
+    if bases[-1] < rows:
+        unused = jnp.zeros((rows - bases[-1], cols, pixels), F32)
+        residual[bases[-1] :] = unused
+        weight[bases[-1] :] = unused
     own_start = bases[ahead]
 
     def flags_of(slot, first, last):
@@ -348,33 +366,30 @@
 
     def block_types(count):
         return (
-            pltpu.VMEM((slots, count, cols, LANES), BF16),
+            pltpu.VMEM((slots, rows, cols, LANES), BF16),
             pltpu.VMEM((count, cols, pixels), F32),
             pltpu.VMEM((count, cols, pixels), F32),
         )
 
-    whole, stencil, *own_block = pl.pallas_call(
+    *sent, stencil, mask, right, weight = pl.pallas_call(
         functools.partial(own_kernel, ends),
-        out_shape=(
-            pltpu.VMEM((rows + 1, 2 * cols, pixels), BF16),
-            pltpu.VMEM(stencils.shape, stencils.dtype),
-        )
+        out_shape=(pltpu.VMEM((STEPS, 2 * cols, pixels), BF16),) * ends
+        + (pltpu.VMEM(stencils.shape, stencils.dtype),)
         + block_types(rows),
         in_specs=[HBM_SPEC] * 3 + [VMEM_SPEC],
-        out_specs=(VMEM_SPEC,) * 5,
+        out_specs=(VMEM_SPEC,) * (4 + ends),
         scratch_shapes=[pltpu.SemaphoreType.DMA((3 + 2 * rows,))],
         compiler_params=small,
         cost_estimate=pl.CostEstimate(flops=0, bytes_accessed=6000000, transcendentals=0),
         name="own",
     )(stencil_hbm, right_hbm, weight_hbm, held)
 
-    wholes = [lax.ppermute(whole, "frow", move) for move in moves]
+    wholes = [lax.ppermute(whole, "frow", move) for whole, move in zip(sent, moves)]
     sides = jnp.stack([odd_side, even_side])
     sides_held = [lax.ppermute(sides, "frow", move) for move in moves]
-    far_rows = rows if ends == 1 else STEPS
     halo_blocks = pl.pallas_call(
         functools.partial(rows_kernel, ends),
-        out_shape=block_types(far_rows) * ends,
+        out_shape=block_types(STEPS) * ends,
         in_specs=[VMEM_SPEC] * ends,
         out_specs=(VMEM_SPEC,) * (3 * ends),
         compiler_params=small,
@@ -383,7 +398,7 @@
     )(*wholes)
 
     cols_held = cols + 2 * SIDE
-    rows_held = rows + ends * far_rows
+    rows_held = 2 * rows if ends == 1 else rows + 2 * STEPS
     solution, coarse = pl.pallas_call(
         functools.partial(smooth_kernel, ends),
         out_shape=(
@@ -405,7 +420,7 @@
         ],
         compiler_params=pltpu.CompilerParams(vmem_limit_bytes=24 * 1024 * 1024),
         name="smooth",
-    )(stencil, odd_side, even_side, *sides_held, *own_block, *halo_blocks)
+    )(stencil, odd_side, even_side, *sides_held, mask, right, weight, *halo_blocks)
 
     half = ring // 2
     across = [(i, (i + half) % ring) for i in range(ring)]

time: 39.3 us -> 37.3 us (0.949)
  waiting for transfers between devices: 5.93 us -> 3.34 us
  starting transfers between devices: 9.51 us -> 10.1 us
    ppermute x1, waiting for transfers between devices: 3.07 us -> 0.49 us  [body(): even_side = lax.ppermute(even, 'fcol', swaps[0])]
    ppermute x1, waiting for transfers between devices: 0.97 us -> 0.13 us  [body(): sides_held = [lax.ppermute(sides, 'frow', move) for move in moves]]
    ppermute x1, waiting for transfers between devices: 0.01 us -> 0.83 us  [body(): lax.ppermute(whole, 'frow', move)]
    ppermute x1, starting transfers between devices: 2.96 us -> 3.53 us  [body(): pair = jnp.stack([coarse, lax.ppermute(coarse, 'fcol', across)])]
    ppermute x1, starting transfers between devices: 0.52 us -> 0.07 us  [body(): lax.ppermute(whole, 'frow', move)]
    ppermute x1, starting transfers between devices: 5.31 us -> 5.74 us  [body(): even_side = lax.ppermute(even, 'fcol', swaps[0])]
  transfers between devices with their start and end apart: 5 -> 5, of which waited for: 3 -> 4; matrix products, arithmetic and copies ran while one was open for 0% -> 0% of each run, Pallas kernels for 1% -> 6%
where the time goes in v4:
time: 37.3 us; the launch traced here: 37 us
  blocking collectives  13 us (35%)
  starting transfers between devices  10.1 us (27%)
  Pallas kernels  9.78 us (26%)
  waiting for transfers between devices  3.34 us (9%)
  between operations  0.7 us (2%)
    all_to_all x1, blocking collectives, body(): block = lax.all_to_all(spread, 'fcol', 0, 0, axis_index_groups=halves)  13 us
    ppermute x1, starting transfers between devices, body(): even_side = lax.ppermute(even, 'fcol', swaps[0])  5.74 us
    pallas_call x1, Pallas kernels, body(): pl.pallas_call(functools.partial(smooth_kernel, ends), out_shape=(jax.Sha...  5.47 us
    ppermute x1, starting transfers between devices, body(): pair = jnp.stack([coarse, lax.ppermute(coarse, 'fcol', across)])  3.53 us
    pallas_call x1, Pallas kernels, body(): pl.pallas_call(functools.partial(own_kernel, ends), out_shape=(pltpu.VMEM...  1.92 us
    ppermute x1, waiting for transfers between devices, body(): pair = jnp.stack([coarse, lax.ppermute(coarse, 'fcol', across)])  1.89 us
    pallas_call x1, Pallas kernels, body(): pl.pallas_call(edge_kernel, out_shape=(side, side, pltpu.VMEM((cols, LANE...  1.05 us
    pallas_call x1, Pallas kernels, body(): pl.pallas_call(widen_kernel, out_shape=jax.ShapeDtypeStruct(widened, F32)...  1.02 us
  transfers between devices with their start and end apart: 5, of which 4 were waited for; matrix products, arithmetic and copies ran while one was open for 0% of the time, Pallas kernels for 6%

profile of v4, /device:TPU:0, one launch (start us, length us, event | category | flops | bytes accessed | tf_op | source)
XLA Modules:
  0.0 37.0 jit_solution(6751082853744789925)
XLA Ops:
  0.6 1.1 %edges.1 = (bf16[96,256]{1,0:T(8,128)(2,1)S(1)}, bf16[96,256]{1,0:T(8,128)(2,1)S(1)}, f32[32,128]{1,0:T(8,128)S(1)}) custom-call(f32[8,32,256]{2,1,0:T(8,128)} %right_hbm.3, f32[8,32,256]{2,1,0:T(8,128)} %weight_hbm.3, s32[9,8,32]{2,1,0:T(8,128)} %bitcast.10), custom_call_target="tpu_custom_call" | custom-call | tf_op jit(solution)/shard_map/edges/pallas_call | solution.py:341
  1.7 0.7 %collective-permute-start = (bf16[96,256]{1,0:T(8,128)(2,1)S(1)}, bf16[96,256]{1,0:T(8,128)(2,1)S(1)}, u32[]{:S(2)}, u32[]{:S(2)}) collective-permute-start(bf16[96,256]{1,0:T(8,128)(2,1)S(1)} %get-tuple-element.17), channel_id=1, source_target_pairs={{1,2},{2,1},{3,4},{4,3},{5,6},{6,5},{7,8},{8,7},{9,10},{10,9},{11,... | collective-permute-start | bytes 147464 | tf_op jit(solution)/shard_map/ppermute | solution.py:356
  2.4 5.7 %collective-permute-start.1 = (bf16[96,256]{1,0:T(8,128)(2,1)S(1)}, bf16[96,256]{1,0:T(8,128)(2,1)S(1)}, u32[]{:S(2)}, u32[]{:S(2)}) collective-permute-start(bf16[96,256]{1,0:T(8,128)(2,1)S(1)} %get-tuple-element.18), channel_id=1, source_target_pairs={{0,1},{1,0},{2,3},{3,2},{4,5},{5,4},{6,7},{7,6},{8,9},{9,8},{10,11... | collective-permute-start | bytes 147464 | tf_op jit(solution)/shard_map/ppermute | solution.py:357
  8.1 1.9 %own.1 = (bf16[6,64,256]{2,1,0:T(8,128)(2,1)S(1)}, bf16[9,256,256]{2,1,0:T(8,128)(2,1)S(1)}, bf16[9,8,32,128]{3,2,1,0:T(8,128)(2,1)S(1)}, f32[8,32,256]{2,1,0:T(8,128)S(1)}, f32[8,32,256]{2,1,0:T(8,128)S(1)}) custom-call(bf16[9,256,256]{2,1,0:T(8,128)(2,1)} %stencil_hbm.1, f32[8,32,256]{2,1,0:T(8,128)} %right_hbm.3, f32[8,32,256]{2,1,0:T(8,128)} %weight_hbm.3, ...), custom_call_target="tpu_custom_call" | custom-call | bytes 6000000 | tf_op jit(solution)/shard_map/own/pallas_call | solution.py:374
  10.0 0.1 collective-permute-start.3
  10.1 0.0 collective-permute-done.refs_1_
  10.1 0.5 %collective-permute-done.1.refs_2_ = bf16[96,256]{1,0:T(8,128)(2,1)S(1)} collective-permute-done((bf16[96,256]{1,0:T(8,128)(2,1)S(1)}, bf16[96,256]{1,0:T(8,128)(2,1)S(1)}, u32[]{:S(2)}, u32[]{:S(2)}) %collective-permute-start.1) | collective-permute-done | bytes 49184 | tf_op jit(solution)/shard_map/ppermute | solution.py:357
  10.6 0.1 collective-permute-start.2
  10.7 0.8 %collective-permute-done.3.refs_0_ = bf16[6,64,256]{2,1,0:T(8,128)(2,1)S(1)} collective-permute-done((bf16[6,64,256]{2,1,0:T(8,128)(2,1)S(1)}, bf16[6,64,256]{2,1,0:T(8,128)(2,1)S(1)}, u32[]{:S(2)}, u32[]{:S(2)}) %collective-permute-start.3) | collective-permute-done | bytes 196640 | tf_op jit(solution)/shard_map/ppermute | solution.py:387
  11.5 0.3 rows.1
  11.9 0.1 collective-permute-done.2.refs_3_
  12.0 5.5 %smooth.1 = (f32[8,32,256]{2,1,0:T(8,128)}, bf16[4,16,256]{2,1,0:T(8,128)(2,1)S(1)}) custom-call(bf16[9,256,256]{2,1,0:T(8,128)(2,1)S(1)} %get-tuple-element.16.refs_0_, bf16[96,256]{1,0:T(8,128)(2,1)S(1)} %collective-permute-done.refs_1_, bf16[96,256]{1,0:T(8,128)(2,1)S(1)} %collective-permute-done.1.refs_2_, ...), custom_call_target="tpu_custom_call" | custom-call | tf_op jit(solution)/shard_map/smooth/pallas_call | solution.py:402
  17.5 3.5 %collective-permute-start.4 = (bf16[4,16,256]{2,1,0:T(8,128)(2,1)S(1)}, bf16[4,16,256]{2,1,0:T(8,128)(2,1)S(1)}, u32[]{:S(2)}, u32[]{:S(2)}) collective-permute-start(bf16[4,16,256]{2,1,0:T(8,128)(2,1)S(1)} %get-tuple-element.27), channel_id=1, source_target_pairs={{0,8},{1,9},{2,10},{3,11},{4,12},{5,13},{6,14},{7,15},{8,0},{9,1},... | collective-permute-start | bytes 98312 | tf_op jit(solution)/shard_map/ppermute | solution.py:427
  21.0 1.9 %collective-permute-done.4 = bf16[4,16,256]{2,1,0:T(8,128)(2,1)S(1)} collective-permute-done((bf16[4,16,256]{2,1,0:T(8,128)(2,1)S(1)}, bf16[4,16,256]{2,1,0:T(8,128)(2,1)S(1)}, u32[]{:S(2)}, u32[]{:S(2)}) %collective-permute-start.4) | collective-permute-done | bytes 32800 | tf_op jit(solution)/shard_map/ppermute | solution.py:427
  22.9 13.0 %all_to_all.5.block_ref = bf16[8,2,4,16,256]{4,3,2,1,0:T(8,128)(2,1)S(1)} all-to-all(bf16[8,2,4,16,256]{4,3,2,1,0:T(8,128)(2,1)S(1)} %broadcast_in_dim.2), channel_id=1, replica_groups={{0,1,2,3,4,5,6,7},{8,9,10,11,12,13,14,15},{16,17,18,19,20,21,22,23},{24..., dimensions={0} | all-to-all | bytes 1048576 | tf_op jit(solution)/shard_map/all_to_all | solution.py:430
  36.0 1.0 %widen.1 = f32[4,16,16,256]{3,2,1,0:T(8,128)} custom-call(bf16[8,2,4,16,256]{4,3,2,1,0:T(8,128)(2,1)S(1)} %all_to_all.5.block_ref), custom_call_target="tpu_custom_call" | custom-call | tf_op jit(solution)/shard_map/widen/pallas_call | solution.py:432
  (3 shorter events, 0.1 us)
Async XLA Ops:
  1.7 8.4 %collective-permute-start = (bf16[96,256]{1,0:T(8,128)(2,1)S(1)}, bf16[96,256]{1,0:T(8,128)(2,1)S(1)}, u32[]{:S(2)}, u32[]{:S(2)}) collective-permute-start(bf16[96,256]{1,0:T(8,128)(2,1)S(1)} %get-tuple-element.17), channel_id=1, source_target_pairs={{1,2},{2,1},{3,4},{4,3},{5,6},{6,5},{7,8},{8,7},{9,10},{10,9},{11,... | collective-permute-start | bytes 147464 | tf_op jit(solution)/shard_map/ppermute | solution.py:356
  2.4 8.2 %collective-permute-start.1 = (bf16[96,256]{1,0:T(8,128)(2,1)S(1)}, bf16[96,256]{1,0:T(8,128)(2,1)S(1)}, u32[]{:S(2)}, u32[]{:S(2)}) collective-permute-start(bf16[96,256]{1,0:T(8,128)(2,1)S(1)} %get-tuple-element.18), channel_id=1, source_target_pairs={{0,1},{1,0},{2,3},{3,2},{4,5},{5,4},{6,7},{7,6},{8,9},{9,8},{10,11... | collective-permute-start | bytes 147464 | tf_op jit(solution)/shard_map/ppermute | solution.py:357
  10.0 1.5 %collective-permute-start.3 = (bf16[6,64,256]{2,1,0:T(8,128)(2,1)S(1)}, bf16[6,64,256]{2,1,0:T(8,128)(2,1)S(1)}, u32[]{:S(2)}, u32[]{:S(2)}) collective-permute-start(bf16[6,64,256]{2,1,0:T(8,128)(2,1)S(1)} %get-tuple-element.22), channel_id=1, source_target_pairs={{0,16},{16,0},{1,17},{17,1},{2,18},{18,2},{3,19},{19,3},{4,20},{20... | collective-permute-start | bytes 589832 | tf_op jit(solution)/shard_map/ppermute | solution.py:387
  10.6 1.4 %collective-permute-start.2 = (bf16[2,96,256]{2,1,0:T(8,128)(2,1)S(1)}, bf16[2,96,256]{2,1,0:T(8,128)(2,1)S(1)}, u32[]{:S(2)}, u32[]{:S(2)}) collective-permute-start(bf16[2,96,256]{2,1,0:T(8,128)(2,1)S(1)} %pad_maximum_fusion), channel_id=1, source_target_pairs={{0,16},{16,0},{1,17},{17,1},{2,18},{18,2},{3,19},{19,3},{4,20},{20... | collective-permute-start | bytes 294920 | tf_op jit(solution)/shard_map/ppermute | solution.py:389
  17.5 5.4 %collective-permute-start.4 = (bf16[4,16,256]{2,1,0:T(8,128)(2,1)S(1)}, bf16[4,16,256]{2,1,0:T(8,128)(2,1)S(1)}, u32[]{:S(2)}, u32[]{:S(2)}) collective-permute-start(bf16[4,16,256]{2,1,0:T(8,128)(2,1)S(1)} %get-tuple-element.27), channel_id=1, source_target_pairs={{0,8},{1,9},{2,10},{3,11},{4,12},{5,13},{6,14},{7,15},{8,0},{9,1},... | collective-permute-start | bytes 98312 | tf_op jit(solution)/shard_map/ppermute | solution.py:427

commit v5 on v4

--- a/solution.py
+++ b/solution.py
@@ -72,6 +72,8 @@
     slots, _, cols, _ = mask.shape
     slot_place = slot_places(ends, slots)
     for slot in range(slots):
+        if slot == slots // 2:
+            continue
         for row, at in places:
             lane = slot * own_rows + row
             column = jnp.broadcast_to(flags[:, lane : lane + 1], (cols, LANES))
@@ -170,17 +172,39 @@
         spread_flags(ends, mask, flags, own_rows, places)
 
 
+def lay_sides(ends, odd_ref, even_ref, places, own_rows, mask, right, weight, strips, turned):
+    first_of_even = lax.rem(lax.axis_index("fcol"), 2) == 0
+    strips[0] = jnp.where(first_of_even, even_ref[...], odd_ref[...]).astype(F32)
+    strips[1] = jnp.where(first_of_even, odd_ref[...], even_ref[...]).astype(F32)
+    right[...] = jnp.zeros(right.shape, F32)
+    weight[...] = jnp.zeros(weight.shape, F32)
+    for end, (low, far) in enumerate(STRIPS):
+        side = slice(end * SIDE + low, end * SIDE + low + STEPS)
+        for row, at in places:
+            flat = 2 * STEPS * row
+            right[at, side, :] = strips[end, flat : flat + STEPS]
+            weight[at, side, :] = strips[end, flat + STEPS : flat + 2 * STEPS] + weight_middle
+        for column in range(SIDE):
+            flat = 2 * STEPS * column + STEPS + far
+            turned[end * SIDE + column] = strips[end, flat, :LANES]
+    spread_flags(ends, mask, turned[...], own_rows, places)
+
+
+def sides_kernel(ends, odd_ref, even_ref, mask, right, weight, strips, turned):
+    own_rows = right.shape[0]
+    places = list(enumerate(row_places(ends, own_rows)[0]))
+    lay_sides(ends, odd_ref, even_ref, places, own_rows, mask, right, weight, strips, turned)
+
+
 def smooth_kernel(ends, *refs):
-    stencil_ref, odd_ref, even_ref = refs[:3]
-    sides = refs[3 : 3 + ends]
-    own_block = refs[3 + ends : 6 + ends]
-    halo_blocks = [refs[6 + ends + 3 * i : 9 + ends + 3 * i] for i in range(ends)]
-    solution_ref, coarse_ref = refs[6 + 4 * ends : 8 + 4 * ends]
-    residual, weight, direction, shifted, side_mask, strips, turned, smoothed, summed = refs[
-        8 + 4 * ends :
-    ]
+    stencil_ref, *beside = refs[:4]
+    sides = refs[4 : 4 + ends]
+    own_block = refs[4 + ends : 7 + ends]
+    halo_blocks = [refs[7 + ends + 3 * i : 10 + ends + 3 * i] for i in range(ends)]
+    solution_ref, coarse_ref, residual, weight, direction, shifted = refs[7 + 4 * ends :][:6]
+    far_masks, far_right, far_weight, strips, turned, smoothed, summed = refs[13 + 4 * ends :]
     own_rows, own_cols, pixels = solution_ref.shape
-    slots = side_mask.shape[0]
+    slots = beside[0].shape[0]
     rows, cols, _ = residual.shape
     place, halos, ahead = row_places(ends, own_rows)
     blocks = halo_blocks[:ahead] + [own_block] + halo_blocks[ahead:]
@@ -193,44 +217,32 @@
         weight[bases[-1] :] = unused
     own_start = bases[ahead]
 
-    def flags_of(slot, first, last):
+    def flags_of(masks, slot, first, last):
         pieces = []
-        for base, block in zip(bases, blocks):
+        for base, block, flags in zip(bases, blocks, masks):
             low, high = max(first - base, 0), min(last - base, block[1].shape[0])
             if low < high:
-                pieces.append(block[0][slot, low:high])
+                pieces.append(flags[slot, low:high])
         return pieces[0] if len(pieces) == 1 else jnp.concatenate(pieces, 0)
 
-    first_of_even = lax.rem(lax.axis_index("fcol"), 2) == 0
-
-    def fill(index, base, block, odd, even, places):
+    for base, block in zip(bases, blocks):
         here = slice(base, base + block[1].shape[0])
         residual[here, :own_cols, :] = block[1][...]
         weight[here, :own_cols, :] = block[2][...]
-        unused = jnp.zeros((block[1].shape[0], cols - own_cols, pixels), F32)
-        residual[here, own_cols:, :] = unused
-        weight[here, own_cols:, :] = unused
-        strips[index, 0] = jnp.where(first_of_even, even[...], odd[...]).astype(F32)
-        strips[index, 1] = jnp.where(first_of_even, odd[...], even[...]).astype(F32)
-        places = [(row, base + at) for row, at in places]
-        for end, (low, far) in enumerate(STRIPS):
-            side = slice(own_cols + end * SIDE + low, own_cols + end * SIDE + low + STEPS)
-            for row, at in places:
-                flat = 2 * STEPS * row
-                residual[at, side, :] = strips[index, end, flat : flat + STEPS]
-                moved = strips[index, end, flat + STEPS : flat + 2 * STEPS]
-                weight[at, side, :] = moved + weight_middle
-            for column in range(SIDE):
-                flat = 2 * STEPS * column + STEPS + far
-                turned[index, end * SIDE + column] = strips[index, end, flat, :LANES]
-        spread_flags(ends, side_mask, turned[index], own_rows, places)
-
-    fill(0, own_start, own_block, odd_ref, even_ref, list(enumerate(place)))
+    here = slice(own_start, own_start + own_rows)
+    residual[here, own_cols:, :] = beside[1][...]
+    weight[here, own_cols:, :] = beside[2][...]
     halo_bases = bases[:ahead] + bases[ahead + 1 : -1]
-    for index, (base, block, sides_ref, places) in enumerate(
-        zip(halo_bases, halo_blocks, sides, halos)
-    ):
-        fill(1 + index, base, block, sides_ref.at[0], sides_ref.at[1], places)
+    for index, (base, sides_ref, places) in enumerate(zip(halo_bases, sides, halos)):
+        lay_sides(
+            ends, sides_ref.at[0], sides_ref.at[1], places, own_rows, far_masks.at[index],
+            far_right.at[index], far_weight.at[index], strips.at[index], turned,
+        )
+        count = halo_blocks[index][1].shape[0]
+        residual[base : base + count, own_cols:, :] = far_right[index, :count]
+        weight[base : base + count, own_cols:, :] = far_weight[index, :count]
+    side_masks = [far_masks.at[index] for index in range(ends)]
+    side_masks = side_masks[:ahead] + [beside[0]] + side_masks[ahead:]
 
     def put_direction(slot, start, count, value):
         here = slice(start + 1, start + 1 + count)
@@ -266,10 +278,14 @@
             picked = []
             for slot in range(slots):
                 across, along = slot // 3, slot % 3
-                keep = flags_of(slot, base, base + size)
+                source = shifted[now, along, base + across : base + across + size, :width, :]
+                if slot == slots // 2:
+                    picked.append(source)
+                    continue
+                keep = flags_of([block[0] for block in blocks], slot, base, base + size)
                 if not last:
-                    keep = jnp.concatenate([keep, side_mask[slot, here]], 1)
-                source = shifted[now, along, base + across : base + across + size, :width, :]
+                    keep_sides = flags_of(side_masks, slot, base, base + size)
+                    keep = jnp.concatenate([keep, keep_sides], 1)
                 picked.append(source[:, :, :LANES] * keep)
                 picked.append(source[:, :, LANES:] * keep)
             picked = jnp.concatenate(picked, 2).reshape(size * width, slots * pixels)
@@ -397,6 +413,25 @@
         name="rows",
     )(*wholes)
 
+    side_types = (
+        pltpu.VMEM((slots, rows, 2 * SIDE, LANES), BF16),
+        pltpu.VMEM((rows, 2 * SIDE, pixels), F32),
+        pltpu.VMEM((rows, 2 * SIDE, pixels), F32),
+    )
+    beside = pl.pallas_call(
+        functools.partial(sides_kernel, ends),
+        out_shape=side_types,
+        in_specs=[VMEM_SPEC] * 2,
+        out_specs=(VMEM_SPEC,) * 3,
+        scratch_shapes=[
+            pltpu.VMEM((2, 2 * STEPS * rows, pixels), F32),
+            pltpu.VMEM((2 * SIDE, LANES), F32),
+        ],
+        compiler_params=small,
+        cost_estimate=pl.CostEstimate(flops=0, bytes_accessed=1000000, transcendentals=0),
+        name="sides",
+    )(odd_side, even_side)
+
     cols_held = cols + 2 * SIDE
     rows_held = 2 * rows if ends == 1 else rows + 2 * STEPS
     solution, coarse = pl.pallas_call(
@@ -405,22 +440,24 @@
             jax.ShapeDtypeStruct((rows, cols, pixels), F32),
             pltpu.VMEM((rows // 2, cols // 2, pixels), BF16),
         ),
-        in_specs=[VMEM_SPEC] * (6 + 4 * ends),
+        in_specs=[VMEM_SPEC] * (7 + 4 * ends),
         out_specs=(VMEM_SPEC,) * 2,
         scratch_shapes=[
             pltpu.VMEM((rows_held, cols_held, pixels), F32),
             pltpu.VMEM((rows_held, cols_held, pixels), F32),
             pltpu.VMEM((rows_held, cols_held, pixels), F32),
             pltpu.VMEM((2, 3, rows_held + 2, cols_held, pixels), BF16),
-            pltpu.VMEM((slots, rows_held, 2 * SIDE, LANES), BF16),
-            pltpu.VMEM((1 + ends, 2, 2 * STEPS * rows, pixels), F32),
-            pltpu.VMEM((1 + ends, 2 * SIDE, LANES), F32),
+            pltpu.VMEM((ends, slots, rows, 2 * SIDE, LANES), BF16),
+            pltpu.VMEM((ends, rows, 2 * SIDE, pixels), F32),
+            pltpu.VMEM((ends, rows, 2 * SIDE, pixels), F32),
+            pltpu.VMEM((ends, 2, 2 * STEPS * rows, pixels), F32),
+            pltpu.VMEM((2 * SIDE, LANES), F32),
             pltpu.VMEM((rows, cols, pixels), F32),
             pltpu.VMEM((rows, cols, LANES), F32),
         ],
         compiler_params=pltpu.CompilerParams(vmem_limit_bytes=24 * 1024 * 1024),
         name="smooth",
-    )(stencil, odd_side, even_side, *sides_held, mask, right, weight, *halo_blocks)
+    )(stencil, *beside, *sides_held, mask, right, weight, *halo_blocks)
 
     half = ring // 2
     across = [(i, (i + half) % ring) for i in range(ring)]

time: 37.3 us -> 37 us (level)
  transfers between devices with their start and end apart: 5 -> 5, of which waited for: 4 -> 4; matrix products, arithmetic and copies ran while one was open for 0% -> 0% of each run, Pallas kernels for 6% -> 7%
where the time goes in v5:
time: 37 us; the launch traced here: 36.8 us
  blocking collectives  13 us (35%)
  starting transfers between devices  10.1 us (27%)
  Pallas kernels  9.74 us (26%)
  waiting for transfers between devices  3.17 us (9%)
  between operations  0.71 us (2%)
    all_to_all x1, blocking collectives, body(): block = lax.all_to_all(spread, 'fcol', 0, 0, axis_index_groups=halves)  13 us
    ppermute x1, starting transfers between devices, body(): even_side = lax.ppermute(even, 'fcol', swaps[0])  5.74 us
    pallas_call x1, Pallas kernels, body(): pl.pallas_call(functools.partial(smooth_kernel, ends), out_shape=(jax.Sha...  5.26 us
    ppermute x1, starting transfers between devices, body(): pair = jnp.stack([coarse, lax.ppermute(coarse, 'fcol', across)])  3.53 us
    ppermute x1, waiting for transfers between devices, body(): pair = jnp.stack([coarse, lax.ppermute(coarse, 'fcol', across)])  1.89 us
    pallas_call x1, Pallas kernels, body(): pl.pallas_call(functools.partial(own_kernel, ends), out_shape=(pltpu.VMEM...  1.89 us
    pallas_call x1, Pallas kernels, body(): pl.pallas_call(edge_kernel, out_shape=(side, side, pltpu.VMEM((cols, LANE...  1.05 us
    pallas_call x1, Pallas kernels, body(): pl.pallas_call(widen_kernel, out_shape=jax.ShapeDtypeStruct(widened, F32)...  1.02 us
  transfers between devices with their start and end apart: 5, of which 4 were waited for; matrix products, arithmetic and copies ran while one was open for 0% of the time, Pallas kernels for 7%

profile of v5, /device:TPU:0, one launch (start us, length us, event | category | flops | bytes accessed | tf_op | source)
XLA Modules:
  0.0 36.8 jit_solution(17167032208633553912)
XLA Ops:
  0.6 1.1 %edges.1 = (bf16[96,256]{1,0:T(8,128)(2,1)S(1)}, bf16[96,256]{1,0:T(8,128)(2,1)S(1)}, f32[32,128]{1,0:T(8,128)S(1)}) custom-call(f32[8,32,256]{2,1,0:T(8,128)} %right_hbm.3, f32[8,32,256]{2,1,0:T(8,128)} %weight_hbm.3, s32[9,8,32]{2,1,0:T(8,128)} %bitcast.10), custom_call_target="tpu_custom_call" | custom-call | tf_op jit(solution)/shard_map/edges/pallas_call | solution.py:357
  1.7 0.7 %collective-permute-start = (bf16[96,256]{1,0:T(8,128)(2,1)S(1)}, bf16[96,256]{1,0:T(8,128)(2,1)S(1)}, u32[]{:S(2)}, u32[]{:S(2)}) collective-permute-start(bf16[96,256]{1,0:T(8,128)(2,1)S(1)} %get-tuple-element.20), channel_id=1, source_target_pairs={{1,2},{2,1},{3,4},{4,3},{5,6},{6,5},{7,8},{8,7},{9,10},{10,9},{11,... | collective-permute-start | bytes 147464 | tf_op jit(solution)/shard_map/ppermute | solution.py:372
  2.4 5.7 %collective-permute-start.1 = (bf16[96,256]{1,0:T(8,128)(2,1)S(1)}, bf16[96,256]{1,0:T(8,128)(2,1)S(1)}, u32[]{:S(2)}, u32[]{:S(2)}) collective-permute-start(bf16[96,256]{1,0:T(8,128)(2,1)S(1)} %get-tuple-element.21), channel_id=1, source_target_pairs={{0,1},{1,0},{2,3},{3,2},{4,5},{5,4},{6,7},{7,6},{8,9},{9,8},{10,11... | collective-permute-start | bytes 147464 | tf_op jit(solution)/shard_map/ppermute | solution.py:373
  8.1 1.9 %own.1 = (bf16[6,64,256]{2,1,0:T(8,128)(2,1)S(1)}, bf16[9,256,256]{2,1,0:T(8,128)(2,1)S(1)}, bf16[9,8,32,128]{3,2,1,0:T(8,128)(2,1)S(1)}, f32[8,32,256]{2,1,0:T(8,128)S(1)}, f32[8,32,256]{2,1,0:T(8,128)S(1)}) custom-call(bf16[9,256,256]{2,1,0:T(8,128)(2,1)} %stencil_hbm.1, f32[8,32,256]{2,1,0:T(8,128)} %right_hbm.3, f32[8,32,256]{2,1,0:T(8,128)} %weight_hbm.3, ...), custom_call_target="tpu_custom_call" | custom-call | bytes 6000000 | tf_op jit(solution)/shard_map/own/pallas_call | solution.py:390
  10.0 0.1 collective-permute-start.3
  10.1 0.0 collective-permute-done.odd_ref
  10.1 0.5 %collective-permute-done.1.even_ref = bf16[96,256]{1,0:T(8,128)(2,1)S(1)} collective-permute-done((bf16[96,256]{1,0:T(8,128)(2,1)S(1)}, bf16[96,256]{1,0:T(8,128)(2,1)S(1)}, u32[]{:S(2)}, u32[]{:S(2)}) %collective-permute-start.1) | collective-permute-done | bytes 49184 | tf_op jit(solution)/shard_map/ppermute | solution.py:373
  10.6 0.1 collective-permute-start.2
  10.7 0.2 sides.1
  10.9 0.6 %collective-permute-done.3.refs_0_ = bf16[6,64,256]{2,1,0:T(8,128)(2,1)S(1)} collective-permute-done((bf16[6,64,256]{2,1,0:T(8,128)(2,1)S(1)}, bf16[6,64,256]{2,1,0:T(8,128)(2,1)S(1)}, u32[]{:S(2)}, u32[]{:S(2)}) %collective-permute-start.3) | collective-permute-done | bytes 196640 | tf_op jit(solution)/shard_map/ppermute | solution.py:403
  11.5 0.3 rows.1
  11.8 0.2 collective-permute-done.2.refs_4_
  12.0 5.3 %smooth.1 = (f32[8,32,256]{2,1,0:T(8,128)}, bf16[4,16,256]{2,1,0:T(8,128)(2,1)S(1)}) custom-call(bf16[9,256,256]{2,1,0:T(8,128)(2,1)S(1)} %get-tuple-element.19.refs_0_, bf16[9,8,16,128]{3,2,1,0:T(8,128)(2,1)S(1)} %get-tuple-element.22.refs_1_, f32[8,16,256]{2,1,0:T(8,128)S(1)} %get-tuple-element.23.refs_2_, f32[8,16,256]{2,1,0:T(8,128)S(1)} %get-tuple-element.24.refs_3_, ...), custom_call_target="tpu_custom_call" | custom-call | tf_op jit(solution)/shard_map/smooth/pallas_call | solution.py:437
  17.3 3.5 %collective-permute-start.4 = (bf16[4,16,256]{2,1,0:T(8,128)(2,1)S(1)}, bf16[4,16,256]{2,1,0:T(8,128)(2,1)S(1)}, u32[]{:S(2)}, u32[]{:S(2)}) collective-permute-start(bf16[4,16,256]{2,1,0:T(8,128)(2,1)S(1)} %get-tuple-element.33), channel_id=1, source_target_pairs={{0,8},{1,9},{2,10},{3,11},{4,12},{5,13},{6,14},{7,15},{8,0},{9,1},... | collective-permute-start | bytes 98312 | tf_op jit(solution)/shard_map/ppermute | solution.py:464
  20.8 1.9 %collective-permute-done.4 = bf16[4,16,256]{2,1,0:T(8,128)(2,1)S(1)} collective-permute-done((bf16[4,16,256]{2,1,0:T(8,128)(2,1)S(1)}, bf16[4,16,256]{2,1,0:T(8,128)(2,1)S(1)}, u32[]{:S(2)}, u32[]{:S(2)}) %collective-permute-start.4) | collective-permute-done | bytes 32800 | tf_op jit(solution)/shard_map/ppermute | solution.py:464
  22.7 13.0 %all_to_all.5.block_ref = bf16[8,2,4,16,256]{4,3,2,1,0:T(8,128)(2,1)S(1)} all-to-all(bf16[8,2,4,16,256]{4,3,2,1,0:T(8,128)(2,1)S(1)} %broadcast_in_dim.2), channel_id=1, replica_groups={{0,1,2,3,4,5,6,7},{8,9,10,11,12,13,14,15},{16,17,18,19,20,21,22,23},{24..., dimensions={0} | all-to-all | bytes 1048576 | tf_op jit(solution)/shard_map/all_to_all | solution.py:467
  35.8 1.0 %widen.1 = f32[4,16,16,256]{3,2,1,0:T(8,128)} custom-call(bf16[8,2,4,16,256]{4,3,2,1,0:T(8,128)(2,1)S(1)} %all_to_all.5.block_ref), custom_call_target="tpu_custom_call" | custom-call | tf_op jit(solution)/shard_map/widen/pallas_call | solution.py:469
  (3 shorter events, 0.1 us)
Async XLA Ops:
  1.7 8.4 %collective-permute-start = (bf16[96,256]{1,0:T(8,128)(2,1)S(1)}, bf16[96,256]{1,0:T(8,128)(2,1)S(1)}, u32[]{:S(2)}, u32[]{:S(2)}) collective-permute-start(bf16[96,256]{1,0:T(8,128)(2,1)S(1)} %get-tuple-element.20), channel_id=1, source_target_pairs={{1,2},{2,1},{3,4},{4,3},{5,6},{6,5},{7,8},{8,7},{9,10},{10,9},{11,... | collective-permute-start | bytes 147464 | tf_op jit(solution)/shard_map/ppermute | solution.py:372
  2.4 8.2 %collective-permute-start.1 = (bf16[96,256]{1,0:T(8,128)(2,1)S(1)}, bf16[96,256]{1,0:T(8,128)(2,1)S(1)}, u32[]{:S(2)}, u32[]{:S(2)}) collective-permute-start(bf16[96,256]{1,0:T(8,128)(2,1)S(1)} %get-tuple-element.21), channel_id=1, source_target_pairs={{0,1},{1,0},{2,3},{3,2},{4,5},{5,4},{6,7},{7,6},{8,9},{9,8},{10,11... | collective-permute-start | bytes 147464 | tf_op jit(solution)/shard_map/ppermute | solution.py:373
  10.0 1.5 %collective-permute-start.3 = (bf16[6,64,256]{2,1,0:T(8,128)(2,1)S(1)}, bf16[6,64,256]{2,1,0:T(8,128)(2,1)S(1)}, u32[]{:S(2)}, u32[]{:S(2)}) collective-permute-start(bf16[6,64,256]{2,1,0:T(8,128)(2,1)S(1)} %get-tuple-element.28), channel_id=1, source_target_pairs={{0,16},{16,0},{1,17},{17,1},{2,18},{18,2},{3,19},{19,3},{4,20},{20... | collective-permute-start | bytes 589832 | tf_op jit(solution)/shard_map/ppermute | solution.py:403
  10.6 1.4 %collective-permute-start.2 = (bf16[2,96,256]{2,1,0:T(8,128)(2,1)S(1)}, bf16[2,96,256]{2,1,0:T(8,128)(2,1)S(1)}, u32[]{:S(2)}, u32[]{:S(2)}) collective-permute-start(bf16[2,96,256]{2,1,0:T(8,128)(2,1)S(1)} %pad_maximum_fusion), channel_id=1, source_target_pairs={{0,16},{16,0},{1,17},{17,1},{2,18},{18,2},{3,19},{19,3},{4,20},{20... | collective-permute-start | bytes 294920 | tf_op jit(solution)/shard_map/ppermute | solution.py:405
  17.3 5.4 %collective-permute-start.4 = (bf16[4,16,256]{2,1,0:T(8,128)(2,1)S(1)}, bf16[4,16,256]{2,1,0:T(8,128)(2,1)S(1)}, u32[]{:S(2)}, u32[]{:S(2)}) collective-permute-start(bf16[4,16,256]{2,1,0:T(8,128)(2,1)S(1)} %get-tuple-element.33), channel_id=1, source_target_pairs={{0,8},{1,9},{2,10},{3,11},{4,12},{5,13},{6,14},{7,15},{8,0},{9,1},... | collective-permute-start | bytes 98312 | tf_op jit(solution)/shard_map/ppermute | solution.py:464

commit v6 on v5

--- a/solution.py
+++ b/solution.py
@@ -260,7 +260,6 @@
     put_direction(0, 0, rows, value)
 
     own = slice(own_start, own_start + own_rows)
-    stencil = stencil_ref[...].reshape(slots * pixels, pixels)
     factors = step_factors()
     for step in range(STEPS):
         now, later = step % 2, 1 - step % 2
@@ -275,21 +274,23 @@
         cuts = [start + count * i // pieces for i in range(pieces + 1)]
         for base, size in zip(cuts, (high - low for low, high in zip(cuts, cuts[1:]))):
             here = slice(base, base + size)
-            picked = []
+            coupled = jnp.zeros((size * width, pixels), F32)
             for slot in range(slots):
                 across, along = slot // 3, slot % 3
                 source = shifted[now, along, base + across : base + across + size, :width, :]
-                if slot == slots // 2:
-                    picked.append(source)
-                    continue
-                keep = flags_of([block[0] for block in blocks], slot, base, base + size)
-                if not last:
-                    keep_sides = flags_of(side_masks, slot, base, base + size)
-                    keep = jnp.concatenate([keep, keep_sides], 1)
-                picked.append(source[:, :, :LANES] * keep)
-                picked.append(source[:, :, LANES:] * keep)
-            picked = jnp.concatenate(picked, 2).reshape(size * width, slots * pixels)
-            coupled = jnp.dot(picked, stencil, preferred_element_type=F32)
+                if slot != slots // 2:
+                    keep = flags_of([block[0] for block in blocks], slot, base, base + size)
+                    if not last:
+                        keep_sides = flags_of(side_masks, slot, base, base + size)
+                        keep = jnp.concatenate([keep, keep_sides], 1)
+                    source = jnp.concatenate(
+                        [source[:, :, :LANES] * keep, source[:, :, LANES:] * keep], 2
+                    )
+                coupled += jnp.dot(
+                    source.reshape(size * width, pixels),
+                    stencil_ref[slot],
+                    preferred_element_type=F32,
+                )
             coupled = coupled.reshape(size, width, pixels)
             moved = direction[here, :width, :]
             left = residual[here, :width, :] - (weight[here, :width, :] * moved + coupled)

time: 37 us -> 37 us (level)
  no operation moved by 1% of the time
where the time goes in v6:
time: 37 us; the launch traced here: 36.8 us
  blocking collectives  13.1 us (35%)
  starting transfers between devices  10.1 us (27%)
  Pallas kernels  9.72 us (26%)
  waiting for transfers between devices  3.17 us (9%)
  between operations  0.71 us (2%)
    all_to_all x1, blocking collectives, body(): block = lax.all_to_all(spread, 'fcol', 0, 0, axis_index_groups=halves)  13.1 us
    ppermute x1, starting transfers between devices, body(): even_side = lax.ppermute(even, 'fcol', swaps[0])  5.74 us
    pallas_call x1, Pallas kernels, body(): pl.pallas_call(functools.partial(smooth_kernel, ends), out_shape=(jax.Sha...  5.24 us
    ppermute x1, starting transfers between devices, body(): pair = jnp.stack([coarse, lax.ppermute(coarse, 'fcol', across)])  3.53 us
    ppermute x1, waiting for transfers between devices, body(): pair = jnp.stack([coarse, lax.ppermute(coarse, 'fcol', across)])  1.89 us
    pallas_call x1, Pallas kernels, body(): pl.pallas_call(functools.partial(own_kernel, ends), out_shape=(pltpu.VMEM...  1.89 us
    pallas_call x1, Pallas kernels, body(): pl.pallas_call(edge_kernel, out_shape=(side, side, pltpu.VMEM((cols, LANE...  1.05 us
    pallas_call x1, Pallas kernels, body(): pl.pallas_call(widen_kernel, out_shape=jax.ShapeDtypeStruct(widened, F32)...  1.02 us
  transfers between devices with their start and end apart: 5, of which 4 were waited for; matrix products, arithmetic and copies ran while one was open for 0% of the time, Pallas kernels for 7%

profile of v6, /device:TPU:0, one launch (start us, length us, event | category | flops | bytes accessed | tf_op | source)
XLA Modules:
  0.0 36.8 jit_solution(6539488603615957044)
XLA Ops:
  0.6 1.1 %edges.1 = (bf16[96,256]{1,0:T(8,128)(2,1)S(1)}, bf16[96,256]{1,0:T(8,128)(2,1)S(1)}, f32[32,128]{1,0:T(8,128)S(1)}) custom-call(f32[8,32,256]{2,1,0:T(8,128)} %right_hbm.3, f32[8,32,256]{2,1,0:T(8,128)} %weight_hbm.3, s32[9,8,32]{2,1,0:T(8,128)} %bitcast.10), custom_call_target="tpu_custom_call" | custom-call | tf_op jit(solution)/shard_map/edges/pallas_call | solution.py:358
  1.7 0.7 %collective-permute-start = (bf16[96,256]{1,0:T(8,128)(2,1)S(1)}, bf16[96,256]{1,0:T(8,128)(2,1)S(1)}, u32[]{:S(2)}, u32[]{:S(2)}) collective-permute-start(bf16[96,256]{1,0:T(8,128)(2,1)S(1)} %get-tuple-element.20), channel_id=1, source_target_pairs={{1,2},{2,1},{3,4},{4,3},{5,6},{6,5},{7,8},{8,7},{9,10},{10,9},{11,... | collective-permute-start | bytes 147464 | tf_op jit(solution)/shard_map/ppermute | solution.py:373
  2.4 5.7 %collective-permute-start.1 = (bf16[96,256]{1,0:T(8,128)(2,1)S(1)}, bf16[96,256]{1,0:T(8,128)(2,1)S(1)}, u32[]{:S(2)}, u32[]{:S(2)}) collective-permute-start(bf16[96,256]{1,0:T(8,128)(2,1)S(1)} %get-tuple-element.21), channel_id=1, source_target_pairs={{0,1},{1,0},{2,3},{3,2},{4,5},{5,4},{6,7},{7,6},{8,9},{9,8},{10,11... | collective-permute-start | bytes 147464 | tf_op jit(solution)/shard_map/ppermute | solution.py:374
  8.1 1.9 %own.1 = (bf16[6,64,256]{2,1,0:T(8,128)(2,1)S(1)}, bf16[9,256,256]{2,1,0:T(8,128)(2,1)S(1)}, bf16[9,8,32,128]{3,2,1,0:T(8,128)(2,1)S(1)}, f32[8,32,256]{2,1,0:T(8,128)S(1)}, f32[8,32,256]{2,1,0:T(8,128)S(1)}) custom-call(bf16[9,256,256]{2,1,0:T(8,128)(2,1)} %stencil_hbm.1, f32[8,32,256]{2,1,0:T(8,128)} %right_hbm.3, f32[8,32,256]{2,1,0:T(8,128)} %weight_hbm.3, ...), custom_call_target="tpu_custom_call" | custom-call | bytes 6000000 | tf_op jit(solution)/shard_map/own/pallas_call | solution.py:391
  10.0 0.1 collective-permute-start.3
  10.1 0.0 collective-permute-done.odd_ref
  10.1 0.5 %collective-permute-done.1.even_ref = bf16[96,256]{1,0:T(8,128)(2,1)S(1)} collective-permute-done((bf16[96,256]{1,0:T(8,128)(2,1)S(1)}, bf16[96,256]{1,0:T(8,128)(2,1)S(1)}, u32[]{:S(2)}, u32[]{:S(2)}) %collective-permute-start.1) | collective-permute-done | bytes 49184 | tf_op jit(solution)/shard_map/ppermute | solution.py:374
  10.6 0.1 collective-permute-start.2
  10.7 0.2 sides.1
  10.9 0.6 %collective-permute-done.3.refs_0_ = bf16[6,64,256]{2,1,0:T(8,128)(2,1)S(1)} collective-permute-done((bf16[6,64,256]{2,1,0:T(8,128)(2,1)S(1)}, bf16[6,64,256]{2,1,0:T(8,128)(2,1)S(1)}, u32[]{:S(2)}, u32[]{:S(2)}) %collective-permute-start.3) | collective-permute-done | bytes 196640 | tf_op jit(solution)/shard_map/ppermute | solution.py:404
  11.5 0.3 rows.1
  11.8 0.2 collective-permute-done.2.refs_4_
  12.0 5.2 %smooth.1 = (f32[8,32,256]{2,1,0:T(8,128)}, bf16[4,16,256]{2,1,0:T(8,128)(2,1)S(1)}) custom-call(bf16[9,256,256]{2,1,0:T(8,128)(2,1)S(1)} %get-tuple-element.19.refs_0_, bf16[9,8,16,128]{3,2,1,0:T(8,128)(2,1)S(1)} %get-tuple-element.22.refs_1_, f32[8,16,256]{2,1,0:T(8,128)S(1)} %get-tuple-element.23.refs_2_, f32[8,16,256]{2,1,0:T(8,128)S(1)} %get-tuple-element.24.refs_3_, ...), custom_call_target="tpu_custom_call" | custom-call | tf_op jit(solution)/shard_map/smooth/pallas_call | solution.py:438
  17.2 3.5 %collective-permute-start.4 = (bf16[4,16,256]{2,1,0:T(8,128)(2,1)S(1)}, bf16[4,16,256]{2,1,0:T(8,128)(2,1)S(1)}, u32[]{:S(2)}, u32[]{:S(2)}) collective-permute-start(bf16[4,16,256]{2,1,0:T(8,128)(2,1)S(1)} %get-tuple-element.33), channel_id=1, source_target_pairs={{0,8},{1,9},{2,10},{3,11},{4,12},{5,13},{6,14},{7,15},{8,0},{9,1},... | collective-permute-start | bytes 98312 | tf_op jit(solution)/shard_map/ppermute | solution.py:465
  20.8 1.9 %collective-permute-done.4 = bf16[4,16,256]{2,1,0:T(8,128)(2,1)S(1)} collective-permute-done((bf16[4,16,256]{2,1,0:T(8,128)(2,1)S(1)}, bf16[4,16,256]{2,1,0:T(8,128)(2,1)S(1)}, u32[]{:S(2)}, u32[]{:S(2)}) %collective-permute-start.4) | collective-permute-done | bytes 32800 | tf_op jit(solution)/shard_map/ppermute | solution.py:465
  22.7 13.1 %all_to_all.5.block_ref = bf16[8,2,4,16,256]{4,3,2,1,0:T(8,128)(2,1)S(1)} all-to-all(bf16[8,2,4,16,256]{4,3,2,1,0:T(8,128)(2,1)S(1)} %broadcast_in_dim.2), channel_id=1, replica_groups={{0,1,2,3,4,5,6,7},{8,9,10,11,12,13,14,15},{16,17,18,19,20,21,22,23},{24..., dimensions={0} | all-to-all | bytes 1048576 | tf_op jit(solution)/shard_map/all_to_all | solution.py:468
  35.8 1.0 %widen.1 = f32[4,16,16,256]{3,2,1,0:T(8,128)} custom-call(bf16[8,2,4,16,256]{4,3,2,1,0:T(8,128)(2,1)S(1)} %all_to_all.5.block_ref), custom_call_target="tpu_custom_call" | custom-call | tf_op jit(solution)/shard_map/widen/pallas_call | solution.py:470
  (3 shorter events, 0.1 us)
Async XLA Ops:
  1.7 8.4 %collective-permute-start = (bf16[96,256]{1,0:T(8,128)(2,1)S(1)}, bf16[96,256]{1,0:T(8,128)(2,1)S(1)}, u32[]{:S(2)}, u32[]{:S(2)}) collective-permute-start(bf16[96,256]{1,0:T(8,128)(2,1)S(1)} %get-tuple-element.20), channel_id=1, source_target_pairs={{1,2},{2,1},{3,4},{4,3},{5,6},{6,5},{7,8},{8,7},{9,10},{10,9},{11,... | collective-permute-start | bytes 147464 | tf_op jit(solution)/shard_map/ppermute | solution.py:373
  2.4 8.2 %collective-permute-start.1 = (bf16[96,256]{1,0:T(8,128)(2,1)S(1)}, bf16[96,256]{1,0:T(8,128)(2,1)S(1)}, u32[]{:S(2)}, u32[]{:S(2)}) collective-permute-start(bf16[96,256]{1,0:T(8,128)(2,1)S(1)} %get-tuple-element.21), channel_id=1, source_target_pairs={{0,1},{1,0},{2,3},{3,2},{4,5},{5,4},{6,7},{7,6},{8,9},{9,8},{10,11... | collective-permute-start | bytes 147464 | tf_op jit(solution)/shard_map/ppermute | solution.py:374
  10.0 1.5 %collective-permute-start.3 = (bf16[6,64,256]{2,1,0:T(8,128)(2,1)S(1)}, bf16[6,64,256]{2,1,0:T(8,128)(2,1)S(1)}, u32[]{:S(2)}, u32[]{:S(2)}) collective-permute-start(bf16[6,64,256]{2,1,0:T(8,128)(2,1)S(1)} %get-tuple-element.28), channel_id=1, source_target_pairs={{0,16},{16,0},{1,17},{17,1},{2,18},{18,2},{3,19},{19,3},{4,20},{20... | collective-permute-start | bytes 589832 | tf_op jit(solution)/shard_map/ppermute | solution.py:404
  10.6 1.4 %collective-permute-start.2 = (bf16[2,96,256]{2,1,0:T(8,128)(2,1)S(1)}, bf16[2,96,256]{2,1,0:T(8,128)(2,1)S(1)}, u32[]{:S(2)}, u32[]{:S(2)}) collective-permute-start(bf16[2,96,256]{2,1,0:T(8,128)(2,1)S(1)} %pad_maximum_fusion), channel_id=1, source_target_pairs={{0,16},{16,0},{1,17},{17,1},{2,18},{18,2},{3,19},{19,3},{4,20},{20... | collective-permute-start | bytes 294920 | tf_op jit(solution)/shard_map/ppermute | solution.py:406
  17.2 5.4 %collective-permute-start.4 = (bf16[4,16,256]{2,1,0:T(8,128)(2,1)S(1)}, bf16[4,16,256]{2,1,0:T(8,128)(2,1)S(1)}, u32[]{:S(2)}, u32[]{:S(2)}) collective-permute-start(bf16[4,16,256]{2,1,0:T(8,128)(2,1)S(1)} %get-tuple-element.33), channel_id=1, source_target_pairs={{0,8},{1,9},{2,10},{3,11},{4,12},{5,13},{6,14},{7,15},{8,0},{9,1},... | collective-permute-start | bytes 98312 | tf_op jit(solution)/shard_map/ppermute | solution.py:465

commit v7 on v6

--- a/solution.py
+++ b/solution.py
@@ -13,7 +13,7 @@
 SIDE = 8
 LANES = 128
 STRIPS = ((0, STEPS - 1), (SIDE - STEPS, 0))
-PIECE_ROWS = 4
+PIECE_ROWS = 7
 
 lower_edge = 1.5
 upper_edge = 6.0

time: 37 us -> 37.3 us (level)
  transfers between devices with their start and end apart: 5 -> 5, of which waited for: 4 -> 4; matrix products, arithmetic and copies ran while one was open for 0% -> 0% of each run, Pallas kernels for 7% -> 6%
where the time goes in v7:
time: 37.3 us; the launch traced here: 37 us
  blocking collectives  13.1 us (35%)
  starting transfers between devices  10.1 us (27%)
  Pallas kernels  9.95 us (27%)
  waiting for transfers between devices  3.17 us (8%)
  between operations  0.71 us (2%)
    all_to_all x1, blocking collectives, body(): block = lax.all_to_all(spread, 'fcol', 0, 0, axis_index_groups=halves)  13.1 us
    ppermute x1, starting transfers between devices, body(): even_side = lax.ppermute(even, 'fcol', swaps[0])  5.74 us
    pallas_call x1, Pallas kernels, body(): pl.pallas_call(functools.partial(smooth_kernel, ends), out_shape=(jax.Sha...  5.48 us
    ppermute x1, starting transfers between devices, body(): pair = jnp.stack([coarse, lax.ppermute(coarse, 'fcol', across)])  3.52 us
    ppermute x1, waiting for transfers between devices, body(): pair = jnp.stack([coarse, lax.ppermute(coarse, 'fcol', across)])  1.89 us
    pallas_call x1, Pallas kernels, body(): pl.pallas_call(functools.partial(own_kernel, ends), out_shape=(pltpu.VMEM...  1.89 us
    pallas_call x1, Pallas kernels, body(): pl.pallas_call(edge_kernel, out_shape=(side, side, pltpu.VMEM((cols, LANE...  1.05 us
    pallas_call x1, Pallas kernels, body(): pl.pallas_call(widen_kernel, out_shape=jax.ShapeDtypeStruct(widened, F32)...  1.02 us
  transfers between devices with their start and end apart: 5, of which 4 were waited for; matrix products, arithmetic and copies ran while one was open for 0% of the time, Pallas kernels for 6%

profile of v7, /device:TPU:0, one launch (start us, length us, event | category | flops | bytes accessed | tf_op | source)
XLA Modules:
  0.0 37.0 jit_solution(17159490122954179647)
XLA Ops:
  0.6 1.1 %edges.1 = (bf16[96,256]{1,0:T(8,128)(2,1)S(1)}, bf16[96,256]{1,0:T(8,128)(2,1)S(1)}, f32[32,128]{1,0:T(8,128)S(1)}) custom-call(f32[8,32,256]{2,1,0:T(8,128)} %right_hbm.3, f32[8,32,256]{2,1,0:T(8,128)} %weight_hbm.3, s32[9,8,32]{2,1,0:T(8,128)} %bitcast.10), custom_call_target="tpu_custom_call" | custom-call | tf_op jit(solution)/shard_map/edges/pallas_call | solution.py:358
  1.7 0.7 %collective-permute-start = (bf16[96,256]{1,0:T(8,128)(2,1)S(1)}, bf16[96,256]{1,0:T(8,128)(2,1)S(1)}, u32[]{:S(2)}, u32[]{:S(2)}) collective-permute-start(bf16[96,256]{1,0:T(8,128)(2,1)S(1)} %get-tuple-element.20), channel_id=1, source_target_pairs={{1,2},{2,1},{3,4},{4,3},{5,6},{6,5},{7,8},{8,7},{9,10},{10,9},{11,... | collective-permute-start | bytes 147464 | tf_op jit(solution)/shard_map/ppermute | solution.py:373
  2.4 5.7 %collective-permute-start.1 = (bf16[96,256]{1,0:T(8,128)(2,1)S(1)}, bf16[96,256]{1,0:T(8,128)(2,1)S(1)}, u32[]{:S(2)}, u32[]{:S(2)}) collective-permute-start(bf16[96,256]{1,0:T(8,128)(2,1)S(1)} %get-tuple-element.21), channel_id=1, source_target_pairs={{0,1},{1,0},{2,3},{3,2},{4,5},{5,4},{6,7},{7,6},{8,9},{9,8},{10,11... | collective-permute-start | bytes 147464 | tf_op jit(solution)/shard_map/ppermute | solution.py:374
  8.1 1.9 %own.1 = (bf16[6,64,256]{2,1,0:T(8,128)(2,1)S(1)}, bf16[9,256,256]{2,1,0:T(8,128)(2,1)S(1)}, bf16[9,8,32,128]{3,2,1,0:T(8,128)(2,1)S(1)}, f32[8,32,256]{2,1,0:T(8,128)S(1)}, f32[8,32,256]{2,1,0:T(8,128)S(1)}) custom-call(bf16[9,256,256]{2,1,0:T(8,128)(2,1)} %stencil_hbm.1, f32[8,32,256]{2,1,0:T(8,128)} %right_hbm.3, f32[8,32,256]{2,1,0:T(8,128)} %weight_hbm.3, ...), custom_call_target="tpu_custom_call" | custom-call | bytes 6000000 | tf_op jit(solution)/shard_map/own/pallas_call | solution.py:391
  10.0 0.1 collective-permute-start.3
  10.1 0.0 collective-permute-done.odd_ref
  10.1 0.5 %collective-permute-done.1.even_ref = bf16[96,256]{1,0:T(8,128)(2,1)S(1)} collective-permute-done((bf16[96,256]{1,0:T(8,128)(2,1)S(1)}, bf16[96,256]{1,0:T(8,128)(2,1)S(1)}, u32[]{:S(2)}, u32[]{:S(2)}) %collective-permute-start.1) | collective-permute-done | bytes 49184 | tf_op jit(solution)/shard_map/ppermute | solution.py:374
  10.6 0.1 collective-permute-start.2
  10.7 0.2 sides.1
  10.9 0.6 %collective-permute-done.3.refs_0_ = bf16[6,64,256]{2,1,0:T(8,128)(2,1)S(1)} collective-permute-done((bf16[6,64,256]{2,1,0:T(8,128)(2,1)S(1)}, bf16[6,64,256]{2,1,0:T(8,128)(2,1)S(1)}, u32[]{:S(2)}, u32[]{:S(2)}) %collective-permute-start.3) | collective-permute-done | bytes 196640 | tf_op jit(solution)/shard_map/ppermute | solution.py:404
  11.5 0.3 rows.1
  11.8 0.2 collective-permute-done.2.refs_4_
  12.0 5.5 %smooth.1 = (f32[8,32,256]{2,1,0:T(8,128)}, bf16[4,16,256]{2,1,0:T(8,128)(2,1)S(1)}) custom-call(bf16[9,256,256]{2,1,0:T(8,128)(2,1)S(1)} %get-tuple-element.19.refs_0_, bf16[9,8,16,128]{3,2,1,0:T(8,128)(2,1)S(1)} %get-tuple-element.22.refs_1_, f32[8,16,256]{2,1,0:T(8,128)S(1)} %get-tuple-element.23.refs_2_, f32[8,16,256]{2,1,0:T(8,128)S(1)} %get-tuple-element.24.refs_3_, ...), custom_call_target="tpu_custom_call" | custom-call | tf_op jit(solution)/shard_map/smooth/pallas_call | solution.py:438
  17.5 3.5 %collective-permute-start.4 = (bf16[4,16,256]{2,1,0:T(8,128)(2,1)S(1)}, bf16[4,16,256]{2,1,0:T(8,128)(2,1)S(1)}, u32[]{:S(2)}, u32[]{:S(2)}) collective-permute-start(bf16[4,16,256]{2,1,0:T(8,128)(2,1)S(1)} %get-tuple-element.33), channel_id=1, source_target_pairs={{0,8},{1,9},{2,10},{3,11},{4,12},{5,13},{6,14},{7,15},{8,0},{9,1},... | collective-permute-start | bytes 98312 | tf_op jit(solution)/shard_map/ppermute | solution.py:465
  21.0 1.9 %collective-permute-done.4 = bf16[4,16,256]{2,1,0:T(8,128)(2,1)S(1)} collective-permute-done((bf16[4,16,256]{2,1,0:T(8,128)(2,1)S(1)}, bf16[4,16,256]{2,1,0:T(8,128)(2,1)S(1)}, u32[]{:S(2)}, u32[]{:S(2)}) %collective-permute-start.4) | collective-permute-done | bytes 32800 | tf_op jit(solution)/shard_map/ppermute | solution.py:465
  22.9 13.1 %all_to_all.5.block_ref = bf16[8,2,4,16,256]{4,3,2,1,0:T(8,128)(2,1)S(1)} all-to-all(bf16[8,2,4,16,256]{4,3,2,1,0:T(8,128)(2,1)S(1)} %broadcast_in_dim.2), channel_id=1, replica_groups={{0,1,2,3,4,5,6,7},{8,9,10,11,12,13,14,15},{16,17,18,19,20,21,22,23},{24..., dimensions={0} | all-to-all | bytes 1048576 | tf_op jit(solution)/shard_map/all_to_all | solution.py:468
  36.0 1.0 %widen.1 = f32[4,16,16,256]{3,2,1,0:T(8,128)} custom-call(bf16[8,2,4,16,256]{4,3,2,1,0:T(8,128)(2,1)S(1)} %all_to_all.5.block_ref), custom_call_target="tpu_custom_call" | custom-call | tf_op jit(solution)/shard_map/widen/pallas_call | solution.py:470
  (3 shorter events, 0.1 us)
Async XLA Ops:
  1.7 8.4 %collective-permute-start = (bf16[96,256]{1,0:T(8,128)(2,1)S(1)}, bf16[96,256]{1,0:T(8,128)(2,1)S(1)}, u32[]{:S(2)}, u32[]{:S(2)}) collective-permute-start(bf16[96,256]{1,0:T(8,128)(2,1)S(1)} %get-tuple-element.20), channel_id=1, source_target_pairs={{1,2},{2,1},{3,4},{4,3},{5,6},{6,5},{7,8},{8,7},{9,10},{10,9},{11,... | collective-permute-start | bytes 147464 | tf_op jit(solution)/shard_map/ppermute | solution.py:373
  2.4 8.2 %collective-permute-start.1 = (bf16[96,256]{1,0:T(8,128)(2,1)S(1)}, bf16[96,256]{1,0:T(8,128)(2,1)S(1)}, u32[]{:S(2)}, u32[]{:S(2)}) collective-permute-start(bf16[96,256]{1,0:T(8,128)(2,1)S(1)} %get-tuple-element.21), channel_id=1, source_target_pairs={{0,1},{1,0},{2,3},{3,2},{4,5},{5,4},{6,7},{7,6},{8,9},{9,8},{10,11... | collective-permute-start | bytes 147464 | tf_op jit(solution)/shard_map/ppermute | solution.py:374
  10.0 1.5 %collective-permute-start.3 = (bf16[6,64,256]{2,1,0:T(8,128)(2,1)S(1)}, bf16[6,64,256]{2,1,0:T(8,128)(2,1)S(1)}, u32[]{:S(2)}, u32[]{:S(2)}) collective-permute-start(bf16[6,64,256]{2,1,0:T(8,128)(2,1)S(1)} %get-tuple-element.28), channel_id=1, source_target_pairs={{0,16},{16,0},{1,17},{17,1},{2,18},{18,2},{3,19},{19,3},{4,20},{20... | collective-permute-start | bytes 589832 | tf_op jit(solution)/shard_map/ppermute | solution.py:404
  10.6 1.4 %collective-permute-start.2 = (bf16[2,96,256]{2,1,0:T(8,128)(2,1)S(1)}, bf16[2,96,256]{2,1,0:T(8,128)(2,1)S(1)}, u32[]{:S(2)}, u32[]{:S(2)}) collective-permute-start(bf16[2,96,256]{2,1,0:T(8,128)(2,1)S(1)} %pad_maximum_fusion), channel_id=1, source_target_pairs={{0,16},{16,0},{1,17},{17,1},{2,18},{18,2},{3,19},{19,3},{4,20},{20... | collective-permute-start | bytes 294920 | tf_op jit(solution)/shard_map/ppermute | solution.py:406
  17.5 5.4 %collective-permute-start.4 = (bf16[4,16,256]{2,1,0:T(8,128)(2,1)S(1)}, bf16[4,16,256]{2,1,0:T(8,128)(2,1)S(1)}, u32[]{:S(2)}, u32[]{:S(2)}) collective-permute-start(bf16[4,16,256]{2,1,0:T(8,128)(2,1)S(1)} %get-tuple-element.33), channel_id=1, source_target_pairs={{0,8},{1,9},{2,10},{3,11},{4,12},{5,13},{6,14},{7,15},{8,0},{9,1},... | collective-permute-start | bytes 98312 | tf_op jit(solution)/shard_map/ppermute | solution.py:465

commit v8 on v7

--- a/solution.py
+++ b/solution.py
@@ -13,7 +13,7 @@
 SIDE = 8
 LANES = 128
 STRIPS = ((0, STEPS - 1), (SIDE - STEPS, 0))
-PIECE_ROWS = 7
+PIECE_ROWS = 3
 
 lower_edge = 1.5
 upper_edge = 6.0

time: 37.3 us -> 37.2 us (level)
  no operation moved by 1% of the time
where the time goes in v8:
time: 37.2 us; the launch traced here: 37 us
  blocking collectives  13 us (35%)
  starting transfers between devices  10.1 us (27%)
  Pallas kernels  9.89 us (27%)
  waiting for transfers between devices  3.17 us (9%)
  between operations  0.71 us (2%)
    all_to_all x1, blocking collectives, body(): block = lax.all_to_all(spread, 'fcol', 0, 0, axis_index_groups=halves)  13 us
    ppermute x1, starting transfers between devices, body(): even_side = lax.ppermute(even, 'fcol', swaps[0])  5.74 us
    pallas_call x1, Pallas kernels, body(): pl.pallas_call(functools.partial(smooth_kernel, ends), out_shape=(jax.Sha...  5.42 us
    ppermute x1, starting transfers between devices, body(): pair = jnp.stack([coarse, lax.ppermute(coarse, 'fcol', across)])  3.53 us
    ppermute x1, waiting for transfers between devices, body(): pair = jnp.stack([coarse, lax.ppermute(coarse, 'fcol', across)])  1.89 us
    pallas_call x1, Pallas kernels, body(): pl.pallas_call(functools.partial(own_kernel, ends), out_shape=(pltpu.VMEM...  1.89 us
    pallas_call x1, Pallas kernels, body(): pl.pallas_call(edge_kernel, out_shape=(side, side, pltpu.VMEM((cols, LANE...  1.05 us
    pallas_call x1, Pallas kernels, body(): pl.pallas_call(widen_kernel, out_shape=jax.ShapeDtypeStruct(widened, F32)...  1.02 us
  transfers between devices with their start and end apart: 5, of which 4 were waited for; matrix products, arithmetic and copies ran while one was open for 0% of the time, Pallas kernels for 6%

profile of v8, /device:TPU:0, one launch (start us, length us, event | category | flops | bytes accessed | tf_op | source)
XLA Modules:
  0.0 37.0 jit_solution(1907531122009143442)
XLA Ops:
  0.6 1.1 %edges.1 = (bf16[96,256]{1,0:T(8,128)(2,1)S(1)}, bf16[96,256]{1,0:T(8,128)(2,1)S(1)}, f32[32,128]{1,0:T(8,128)S(1)}) custom-call(f32[8,32,256]{2,1,0:T(8,128)} %right_hbm.3, f32[8,32,256]{2,1,0:T(8,128)} %weight_hbm.3, s32[9,8,32]{2,1,0:T(8,128)} %bitcast.10), custom_call_target="tpu_custom_call" | custom-call | tf_op jit(solution)/shard_map/edges/pallas_call | solution.py:358
  1.7 0.7 %collective-permute-start = (bf16[96,256]{1,0:T(8,128)(2,1)S(1)}, bf16[96,256]{1,0:T(8,128)(2,1)S(1)}, u32[]{:S(2)}, u32[]{:S(2)}) collective-permute-start(bf16[96,256]{1,0:T(8,128)(2,1)S(1)} %get-tuple-element.20), channel_id=1, source_target_pairs={{1,2},{2,1},{3,4},{4,3},{5,6},{6,5},{7,8},{8,7},{9,10},{10,9},{11,... | collective-permute-start | bytes 147464 | tf_op jit(solution)/shard_map/ppermute | solution.py:373
  2.4 5.7 %collective-permute-start.1 = (bf16[96,256]{1,0:T(8,128)(2,1)S(1)}, bf16[96,256]{1,0:T(8,128)(2,1)S(1)}, u32[]{:S(2)}, u32[]{:S(2)}) collective-permute-start(bf16[96,256]{1,0:T(8,128)(2,1)S(1)} %get-tuple-element.21), channel_id=1, source_target_pairs={{0,1},{1,0},{2,3},{3,2},{4,5},{5,4},{6,7},{7,6},{8,9},{9,8},{10,11... | collective-permute-start | bytes 147464 | tf_op jit(solution)/shard_map/ppermute | solution.py:374
  8.1 1.9 %own.1 = (bf16[6,64,256]{2,1,0:T(8,128)(2,1)S(1)}, bf16[9,256,256]{2,1,0:T(8,128)(2,1)S(1)}, bf16[9,8,32,128]{3,2,1,0:T(8,128)(2,1)S(1)}, f32[8,32,256]{2,1,0:T(8,128)S(1)}, f32[8,32,256]{2,1,0:T(8,128)S(1)}) custom-call(bf16[9,256,256]{2,1,0:T(8,128)(2,1)} %stencil_hbm.1, f32[8,32,256]{2,1,0:T(8,128)} %right_hbm.3, f32[8,32,256]{2,1,0:T(8,128)} %weight_hbm.3, ...), custom_call_target="tpu_custom_call" | custom-call | bytes 6000000 | tf_op jit(solution)/shard_map/own/pallas_call | solution.py:391
  10.0 0.1 collective-permute-start.3
  10.1 0.0 collective-permute-done.odd_ref
  10.1 0.5 %collective-permute-done.1.even_ref = bf16[96,256]{1,0:T(8,128)(2,1)S(1)} collective-permute-done((bf16[96,256]{1,0:T(8,128)(2,1)S(1)}, bf16[96,256]{1,0:T(8,128)(2,1)S(1)}, u32[]{:S(2)}, u32[]{:S(2)}) %collective-permute-start.1) | collective-permute-done | bytes 49184 | tf_op jit(solution)/shard_map/ppermute | solution.py:374
  10.6 0.1 collective-permute-start.2
  10.7 0.2 sides.1
  10.9 0.6 %collective-permute-done.3.refs_0_ = bf16[6,64,256]{2,1,0:T(8,128)(2,1)S(1)} collective-permute-done((bf16[6,64,256]{2,1,0:T(8,128)(2,1)S(1)}, bf16[6,64,256]{2,1,0:T(8,128)(2,1)S(1)}, u32[]{:S(2)}, u32[]{:S(2)}) %collective-permute-start.3) | collective-permute-done | bytes 196640 | tf_op jit(solution)/shard_map/ppermute | solution.py:404
  11.5 0.3 rows.1
  11.8 0.2 collective-permute-done.2.refs_4_
  12.0 5.4 %smooth.1 = (f32[8,32,256]{2,1,0:T(8,128)}, bf16[4,16,256]{2,1,0:T(8,128)(2,1)S(1)}) custom-call(bf16[9,256,256]{2,1,0:T(8,128)(2,1)S(1)} %get-tuple-element.19.refs_0_, bf16[9,8,16,128]{3,2,1,0:T(8,128)(2,1)S(1)} %get-tuple-element.22.refs_1_, f32[8,16,256]{2,1,0:T(8,128)S(1)} %get-tuple-element.23.refs_2_, f32[8,16,256]{2,1,0:T(8,128)S(1)} %get-tuple-element.24.refs_3_, ...), custom_call_target="tpu_custom_call" | custom-call | tf_op jit(solution)/shard_map/smooth/pallas_call | solution.py:438
  17.4 3.5 %collective-permute-start.4 = (bf16[4,16,256]{2,1,0:T(8,128)(2,1)S(1)}, bf16[4,16,256]{2,1,0:T(8,128)(2,1)S(1)}, u32[]{:S(2)}, u32[]{:S(2)}) collective-permute-start(bf16[4,16,256]{2,1,0:T(8,128)(2,1)S(1)} %get-tuple-element.33), channel_id=1, source_target_pairs={{0,8},{1,9},{2,10},{3,11},{4,12},{5,13},{6,14},{7,15},{8,0},{9,1},... | collective-permute-start | bytes 98312 | tf_op jit(solution)/shard_map/ppermute | solution.py:465
  20.9 1.9 %collective-permute-done.4 = bf16[4,16,256]{2,1,0:T(8,128)(2,1)S(1)} collective-permute-done((bf16[4,16,256]{2,1,0:T(8,128)(2,1)S(1)}, bf16[4,16,256]{2,1,0:T(8,128)(2,1)S(1)}, u32[]{:S(2)}, u32[]{:S(2)}) %collective-permute-start.4) | collective-permute-done | bytes 32800 | tf_op jit(solution)/shard_map/ppermute | solution.py:465
  22.9 13.0 %all_to_all.5.block_ref = bf16[8,2,4,16,256]{4,3,2,1,0:T(8,128)(2,1)S(1)} all-to-all(bf16[8,2,4,16,256]{4,3,2,1,0:T(8,128)(2,1)S(1)} %broadcast_in_dim.2), channel_id=1, replica_groups={{0,1,2,3,4,5,6,7},{8,9,10,11,12,13,14,15},{16,17,18,19,20,21,22,23},{24..., dimensions={0} | all-to-all | bytes 1048576 | tf_op jit(solution)/shard_map/all_to_all | solution.py:468
  35.9 1.0 %widen.1 = f32[4,16,16,256]{3,2,1,0:T(8,128)} custom-call(bf16[8,2,4,16,256]{4,3,2,1,0:T(8,128)(2,1)S(1)} %all_to_all.5.block_ref), custom_call_target="tpu_custom_call" | custom-call | tf_op jit(solution)/shard_map/widen/pallas_call | solution.py:470
  (3 shorter events, 0.1 us)
Async XLA Ops:
  1.7 8.4 %collective-permute-start = (bf16[96,256]{1,0:T(8,128)(2,1)S(1)}, bf16[96,256]{1,0:T(8,128)(2,1)S(1)}, u32[]{:S(2)}, u32[]{:S(2)}) collective-permute-start(bf16[96,256]{1,0:T(8,128)(2,1)S(1)} %get-tuple-element.20), channel_id=1, source_target_pairs={{1,2},{2,1},{3,4},{4,3},{5,6},{6,5},{7,8},{8,7},{9,10},{10,9},{11,... | collective-permute-start | bytes 147464 | tf_op jit(solution)/shard_map/ppermute | solution.py:373
  2.4 8.2 %collective-permute-start.1 = (bf16[96,256]{1,0:T(8,128)(2,1)S(1)}, bf16[96,256]{1,0:T(8,128)(2,1)S(1)}, u32[]{:S(2)}, u32[]{:S(2)}) collective-permute-start(bf16[96,256]{1,0:T(8,128)(2,1)S(1)} %get-tuple-element.21), channel_id=1, source_target_pairs={{0,1},{1,0},{2,3},{3,2},{4,5},{5,4},{6,7},{7,6},{8,9},{9,8},{10,11... | collective-permute-start | bytes 147464 | tf_op jit(solution)/shard_map/ppermute | solution.py:374
  10.0 1.5 %collective-permute-start.3 = (bf16[6,64,256]{2,1,0:T(8,128)(2,1)S(1)}, bf16[6,64,256]{2,1,0:T(8,128)(2,1)S(1)}, u32[]{:S(2)}, u32[]{:S(2)}) collective-permute-start(bf16[6,64,256]{2,1,0:T(8,128)(2,1)S(1)} %get-tuple-element.28), channel_id=1, source_target_pairs={{0,16},{16,0},{1,17},{17,1},{2,18},{18,2},{3,19},{19,3},{4,20},{20... | collective-permute-start | bytes 589832 | tf_op jit(solution)/shard_map/ppermute | solution.py:404
  10.6 1.4 %collective-permute-start.2 = (bf16[2,96,256]{2,1,0:T(8,128)(2,1)S(1)}, bf16[2,96,256]{2,1,0:T(8,128)(2,1)S(1)}, u32[]{:S(2)}, u32[]{:S(2)}) collective-permute-start(bf16[2,96,256]{2,1,0:T(8,128)(2,1)S(1)} %pad_maximum_fusion), channel_id=1, source_target_pairs={{0,16},{16,0},{1,17},{17,1},{2,18},{18,2},{3,19},{19,3},{4,20},{20... | collective-permute-start | bytes 294920 | tf_op jit(solution)/shard_map/ppermute | solution.py:406
  17.4 5.4 %collective-permute-start.4 = (bf16[4,16,256]{2,1,0:T(8,128)(2,1)S(1)}, bf16[4,16,256]{2,1,0:T(8,128)(2,1)S(1)}, u32[]{:S(2)}, u32[]{:S(2)}) collective-permute-start(bf16[4,16,256]{2,1,0:T(8,128)(2,1)S(1)} %get-tuple-element.33), channel_id=1, source_target_pairs={{0,8},{1,9},{2,10},{3,11},{4,12},{5,13},{6,14},{7,15},{8,0},{9,1},... | collective-permute-start | bytes 98312 | tf_op jit(solution)/shard_map/ppermute | solution.py:465

commit v9 on v6

--- a/solution.py
+++ b/solution.py
@@ -202,7 +202,7 @@
     own_block = refs[4 + ends : 7 + ends]
     halo_blocks = [refs[7 + ends + 3 * i : 10 + ends + 3 * i] for i in range(ends)]
     solution_ref, coarse_ref, residual, weight, direction, shifted = refs[7 + 4 * ends :][:6]
-    far_masks, far_right, far_weight, strips, turned, smoothed, summed = refs[13 + 4 * ends :]
+    far_masks, far_right, far_weight, strips, turned, smoothed, summed, sent = refs[13 + 4 * ends :]
     own_rows, own_cols, pixels = solution_ref.shape
     slots = beside[0].shape[0]
     rows, cols, _ = residual.shape
@@ -260,12 +260,19 @@
     put_direction(0, 0, rows, value)
 
     own = slice(own_start, own_start + own_rows)
+    solution_copies = [
+        pltpu.make_async_copy(smoothed.at[at], solution_ref.at[row], sent.at[row])
+        for row, at in enumerate(place)
+    ]
     factors = step_factors()
     for step in range(STEPS):
         now, later = step % 2, 1 - step % 2
         last = step == STEPS - 1
         moved = direction[own, :own_cols, :]
         smoothed[...] = moved if step == 0 else smoothed[...] + moved
+        if last:
+            for copy in solution_copies:
+                copy.start()
         margin = STEPS - 1 - step
         count = own_rows + ends * margin
         start = own_start - (ends - 1) * margin
@@ -320,8 +327,8 @@
                 piece = summed[at, pl.ds(along, own_cols // 2, stride=2), :]
                 pieces.append(piece[:, :quarter])
         coarse_ref[row] = jnp.concatenate(pieces, 1).astype(BF16)
-    for row, at in enumerate(place):
-        solution_ref[row] = smoothed[at]
+    for copy in solution_copies:
+        copy.wait()
 
 
 def widen_kernel(block_ref, out_hbm, wide, sent):
@@ -442,7 +449,7 @@
             pltpu.VMEM((rows // 2, cols // 2, pixels), BF16),
         ),
         in_specs=[VMEM_SPEC] * (7 + 4 * ends),
-        out_specs=(VMEM_SPEC,) * 2,
+        out_specs=(HBM_SPEC, VMEM_SPEC),
         scratch_shapes=[
             pltpu.VMEM((rows_held, cols_held, pixels), F32),
             pltpu.VMEM((rows_held, cols_held, pixels), F32),
@@ -455,6 +462,7 @@
             pltpu.VMEM((2 * SIDE, LANES), F32),
             pltpu.VMEM((rows, cols, pixels), F32),
             pltpu.VMEM((rows, cols, LANES), F32),
+            pltpu.SemaphoreType.DMA((rows,)),
         ],
         compiler_params=pltpu.CompilerParams(vmem_limit_bytes=24 * 1024 * 1024),
         name="smooth",

time: 37 us -> 37.1 us (level)
  no operation moved by 1% of the time
where the time goes in v9:
time: 37.1 us; the launch traced here: 36.9 us
  blocking collectives  13 us (35%)
  starting transfers between devices  10.1 us (27%)
  Pallas kernels  9.72 us (26%)
  waiting for transfers between devices  3.18 us (9%)
  between operations  0.71 us (2%)
    all_to_all x1, blocking collectives, body(): block = lax.all_to_all(spread, 'fcol', 0, 0, axis_index_groups=halves)  13 us
    ppermute x1, starting transfers between devices, body(): even_side = lax.ppermute(even, 'fcol', swaps[0])  5.74 us
    pallas_call x1, Pallas kernels, body(): pl.pallas_call(functools.partial(smooth_kernel, ends), out_shape=(jax.Sha...  5.24 us
    ppermute x1, starting transfers between devices, body(): pair = jnp.stack([coarse, lax.ppermute(coarse, 'fcol', across)])  3.59 us
    ppermute x1, waiting for transfers between devices, body(): pair = jnp.stack([coarse, lax.ppermute(coarse, 'fcol', across)])  1.89 us
    pallas_call x1, Pallas kernels, body(): pl.pallas_call(functools.partial(own_kernel, ends), out_shape=(pltpu.VMEM...  1.89 us
    pallas_call x1, Pallas kernels, body(): pl.pallas_call(edge_kernel, out_shape=(side, side, pltpu.VMEM((cols, LANE...  1.05 us
    pallas_call x1, Pallas kernels, body(): pl.pallas_call(widen_kernel, out_shape=jax.ShapeDtypeStruct(widened, F32)...  1.02 us
  transfers between devices with their start and end apart: 5, of which 4 were waited for; matrix products, arithmetic and copies ran while one was open for 0% of the time, Pallas kernels for 7%

profile of v9, /device:TPU:0, one launch (start us, length us, event | category | flops | bytes accessed | tf_op | source)
XLA Modules:
  0.0 36.9 jit_solution(2588474941928510119)
XLA Ops:
  0.6 1.1 %edges.1 = (bf16[96,256]{1,0:T(8,128)(2,1)S(1)}, bf16[96,256]{1,0:T(8,128)(2,1)S(1)}, f32[32,128]{1,0:T(8,128)S(1)}) custom-call(f32[8,32,256]{2,1,0:T(8,128)} %right_hbm.3, f32[8,32,256]{2,1,0:T(8,128)} %weight_hbm.3, s32[9,8,32]{2,1,0:T(8,128)} %bitcast.10), custom_call_target="tpu_custom_call" | custom-call | tf_op jit(solution)/shard_map/edges/pallas_call | solution.py:365
  1.7 0.7 %collective-permute-start = (bf16[96,256]{1,0:T(8,128)(2,1)S(1)}, bf16[96,256]{1,0:T(8,128)(2,1)S(1)}, u32[]{:S(2)}, u32[]{:S(2)}) collective-permute-start(bf16[96,256]{1,0:T(8,128)(2,1)S(1)} %get-tuple-element.20), channel_id=1, source_target_pairs={{1,2},{2,1},{3,4},{4,3},{5,6},{6,5},{7,8},{8,7},{9,10},{10,9},{11,... | collective-permute-start | bytes 147464 | tf_op jit(solution)/shard_map/ppermute | solution.py:380
  2.4 5.7 %collective-permute-start.1 = (bf16[96,256]{1,0:T(8,128)(2,1)S(1)}, bf16[96,256]{1,0:T(8,128)(2,1)S(1)}, u32[]{:S(2)}, u32[]{:S(2)}) collective-permute-start(bf16[96,256]{1,0:T(8,128)(2,1)S(1)} %get-tuple-element.21), channel_id=1, source_target_pairs={{0,1},{1,0},{2,3},{3,2},{4,5},{5,4},{6,7},{7,6},{8,9},{9,8},{10,11... | collective-permute-start | bytes 147464 | tf_op jit(solution)/shard_map/ppermute | solution.py:381
  8.1 1.9 %own.1 = (bf16[6,64,256]{2,1,0:T(8,128)(2,1)S(1)}, bf16[9,256,256]{2,1,0:T(8,128)(2,1)S(1)}, bf16[9,8,32,128]{3,2,1,0:T(8,128)(2,1)S(1)}, f32[8,32,256]{2,1,0:T(8,128)S(1)}, f32[8,32,256]{2,1,0:T(8,128)S(1)}) custom-call(bf16[9,256,256]{2,1,0:T(8,128)(2,1)} %stencil_hbm.1, f32[8,32,256]{2,1,0:T(8,128)} %right_hbm.3, f32[8,32,256]{2,1,0:T(8,128)} %weight_hbm.3, ...), custom_call_target="tpu_custom_call" | custom-call | bytes 6000000 | tf_op jit(solution)/shard_map/own/pallas_call | solution.py:398
  10.0 0.1 collective-permute-start.3
  10.1 0.0 collective-permute-done.odd_ref
  10.1 0.5 %collective-permute-done.1.even_ref = bf16[96,256]{1,0:T(8,128)(2,1)S(1)} collective-permute-done((bf16[96,256]{1,0:T(8,128)(2,1)S(1)}, bf16[96,256]{1,0:T(8,128)(2,1)S(1)}, u32[]{:S(2)}, u32[]{:S(2)}) %collective-permute-start.1) | collective-permute-done | bytes 49184 | tf_op jit(solution)/shard_map/ppermute | solution.py:381
  10.6 0.1 collective-permute-start.2
  10.7 0.2 sides.1
  10.9 0.6 %collective-permute-done.3.refs_0_ = bf16[6,64,256]{2,1,0:T(8,128)(2,1)S(1)} collective-permute-done((bf16[6,64,256]{2,1,0:T(8,128)(2,1)S(1)}, bf16[6,64,256]{2,1,0:T(8,128)(2,1)S(1)}, u32[]{:S(2)}, u32[]{:S(2)}) %collective-permute-start.3) | collective-permute-done | bytes 196640 | tf_op jit(solution)/shard_map/ppermute | solution.py:411
  11.5 0.3 rows.1
  11.8 0.2 collective-permute-done.2.refs_4_
  12.0 5.2 %smooth.1 = (f32[8,32,256]{2,1,0:T(8,128)}, bf16[4,16,256]{2,1,0:T(8,128)(2,1)S(1)}) custom-call(bf16[9,256,256]{2,1,0:T(8,128)(2,1)S(1)} %get-tuple-element.19.refs_0_, bf16[9,8,16,128]{3,2,1,0:T(8,128)(2,1)S(1)} %get-tuple-element.22.refs_1_, f32[8,16,256]{2,1,0:T(8,128)S(1)} %get-tuple-element.23.refs_2_, f32[8,16,256]{2,1,0:T(8,128)S(1)} %get-tuple-element.24.refs_3_, ...), custom_call_target="tpu_custom_call" | custom-call | tf_op jit(solution)/shard_map/smooth/pallas_call | solution.py:445
  17.2 3.6 %collective-permute-start.4 = (bf16[4,16,256]{2,1,0:T(8,128)(2,1)S(1)}, bf16[4,16,256]{2,1,0:T(8,128)(2,1)S(1)}, u32[]{:S(2)}, u32[]{:S(2)}) collective-permute-start(bf16[4,16,256]{2,1,0:T(8,128)(2,1)S(1)} %get-tuple-element.33), channel_id=1, source_target_pairs={{0,8},{1,9},{2,10},{3,11},{4,12},{5,13},{6,14},{7,15},{8,0},{9,1},... | collective-permute-start | bytes 98312 | tf_op jit(solution)/shard_map/ppermute | solution.py:473
  20.8 1.9 %collective-permute-done.4 = bf16[4,16,256]{2,1,0:T(8,128)(2,1)S(1)} collective-permute-done((bf16[4,16,256]{2,1,0:T(8,128)(2,1)S(1)}, bf16[4,16,256]{2,1,0:T(8,128)(2,1)S(1)}, u32[]{:S(2)}, u32[]{:S(2)}) %collective-permute-start.4) | collective-permute-done | bytes 32800 | tf_op jit(solution)/shard_map/ppermute | solution.py:473
  22.8 13.0 %all_to_all.5.block_ref = bf16[8,2,4,16,256]{4,3,2,1,0:T(8,128)(2,1)S(1)} all-to-all(bf16[8,2,4,16,256]{4,3,2,1,0:T(8,128)(2,1)S(1)} %broadcast_in_dim.2), channel_id=1, replica_groups={{0,1,2,3,4,5,6,7},{8,9,10,11,12,13,14,15},{16,17,18,19,20,21,22,23},{24..., dimensions={0} | all-to-all | bytes 1048576 | tf_op jit(solution)/shard_map/all_to_all | solution.py:476
  35.8 1.0 %widen.1 = f32[4,16,16,256]{3,2,1,0:T(8,128)} custom-call(bf16[8,2,4,16,256]{4,3,2,1,0:T(8,128)(2,1)S(1)} %all_to_all.5.block_ref), custom_call_target="tpu_custom_call" | custom-call | tf_op jit(solution)/shard_map/widen/pallas_call | solution.py:478
  (3 shorter events, 0.1 us)
Async XLA Ops:
  1.7 8.4 %collective-permute-start = (bf16[96,256]{1,0:T(8,128)(2,1)S(1)}, bf16[96,256]{1,0:T(8,128)(2,1)S(1)}, u32[]{:S(2)}, u32[]{:S(2)}) collective-permute-start(bf16[96,256]{1,0:T(8,128)(2,1)S(1)} %get-tuple-element.20), channel_id=1, source_target_pairs={{1,2},{2,1},{3,4},{4,3},{5,6},{6,5},{7,8},{8,7},{9,10},{10,9},{11,... | collective-permute-start | bytes 147464 | tf_op jit(solution)/shard_map/ppermute | solution.py:380
  2.4 8.2 %collective-permute-start.1 = (bf16[96,256]{1,0:T(8,128)(2,1)S(1)}, bf16[96,256]{1,0:T(8,128)(2,1)S(1)}, u32[]{:S(2)}, u32[]{:S(2)}) collective-permute-start(bf16[96,256]{1,0:T(8,128)(2,1)S(1)} %get-tuple-element.21), channel_id=1, source_target_pairs={{0,1},{1,0},{2,3},{3,2},{4,5},{5,4},{6,7},{7,6},{8,9},{9,8},{10,11... | collective-permute-start | bytes 147464 | tf_op jit(solution)/shard_map/ppermute | solution.py:381
  10.0 1.5 %collective-permute-start.3 = (bf16[6,64,256]{2,1,0:T(8,128)(2,1)S(1)}, bf16[6,64,256]{2,1,0:T(8,128)(2,1)S(1)}, u32[]{:S(2)}, u32[]{:S(2)}) collective-permute-start(bf16[6,64,256]{2,1,0:T(8,128)(2,1)S(1)} %get-tuple-element.28), channel_id=1, source_target_pairs={{0,16},{16,0},{1,17},{17,1},{2,18},{18,2},{3,19},{19,3},{4,20},{20... | collective-permute-start | bytes 589832 | tf_op jit(solution)/shard_map/ppermute | solution.py:411
  10.6 1.4 %collective-permute-start.2 = (bf16[2,96,256]{2,1,0:T(8,128)(2,1)S(1)}, bf16[2,96,256]{2,1,0:T(8,128)(2,1)S(1)}, u32[]{:S(2)}, u32[]{:S(2)}) collective-permute-start(bf16[2,96,256]{2,1,0:T(8,128)(2,1)S(1)} %pad_maximum_fusion), channel_id=1, source_target_pairs={{0,16},{16,0},{1,17},{17,1},{2,18},{18,2},{3,19},{19,3},{4,20},{20... | collective-permute-start | bytes 294920 | tf_op jit(solution)/shard_map/ppermute | solution.py:413
  17.2 5.5 %collective-permute-start.4 = (bf16[4,16,256]{2,1,0:T(8,128)(2,1)S(1)}, bf16[4,16,256]{2,1,0:T(8,128)(2,1)S(1)}, u32[]{:S(2)}, u32[]{:S(2)}) collective-permute-start(bf16[4,16,256]{2,1,0:T(8,128)(2,1)S(1)} %get-tuple-element.33), channel_id=1, source_target_pairs={{0,8},{1,9},{2,10},{3,11},{4,12},{5,13},{6,14},{7,15},{8,0},{9,1},... | collective-permute-start | bytes 98312 | tf_op jit(solution)/shard_map/ppermute | solution.py:473

commit v10 on v6

--- a/solution.py
+++ b/solution.py
@@ -330,11 +330,16 @@
     own_half = lax.axis_index("fcol") // half
     copies = []
     for row in range(rows):
-        for i in range(half):
-            wide[row, own_half * half + i] = block_ref[i, 0, row].astype(F32)
-            wide[row, (1 - own_half) * half + i] = block_ref[i, 1, row].astype(F32)
-        copies.append(pltpu.make_async_copy(wide.at[row], out_hbm.at[row], sent.at[row]))
-        copies[-1].start()
+        for kept, part in enumerate((own_half, 1 - own_half)):
+            for i in range(half):
+                wide[row, part * half + i] = block_ref[i, kept, row].astype(F32)
+            here = pl.ds(part * half, half)
+            copies.append(
+                pltpu.make_async_copy(
+                    wide.at[row, here], out_hbm.at[row, here], sent.at[row, kept]
+                )
+            )
+            copies[-1].start()
     for copy in copies:
         copy.wait()
 
@@ -472,7 +477,7 @@
         out_shape=jax.ShapeDtypeStruct(widened, F32),
         in_specs=[VMEM_SPEC],
         out_specs=HBM_SPEC,
-        scratch_shapes=[pltpu.VMEM(widened, F32), pltpu.SemaphoreType.DMA((rows // 2,))],
+        scratch_shapes=[pltpu.VMEM(widened, F32), pltpu.SemaphoreType.DMA((rows // 2, 2))],
         compiler_params=small,
         name="widen",
     )(block)

time: 37 us -> 37.1 us (level)
  no operation moved by 1% of the time
where the time goes in v10:
time: 37.1 us; the launch traced here: 36.8 us
  blocking collectives  13.1 us (35%)
  starting transfers between devices  10.1 us (27%)
  Pallas kernels  9.74 us (26%)
  waiting for transfers between devices  3.17 us (9%)
  between operations  0.71 us (2%)
    all_to_all x1, blocking collectives, body(): block = lax.all_to_all(spread, 'fcol', 0, 0, axis_index_groups=halves)  13.1 us
    ppermute x1, starting transfers between devices, body(): even_side = lax.ppermute(even, 'fcol', swaps[0])  5.74 us
    pallas_call x1, Pallas kernels, body(): pl.pallas_call(functools.partial(smooth_kernel, ends), out_shape=(jax.Sha...  5.24 us
    ppermute x1, starting transfers between devices, body(): pair = jnp.stack([coarse, lax.ppermute(coarse, 'fcol', across)])  3.53 us
    ppermute x1, waiting for transfers between devices, body(): pair = jnp.stack([coarse, lax.ppermute(coarse, 'fcol', across)])  1.89 us
    pallas_call x1, Pallas kernels, body(): pl.pallas_call(functools.partial(own_kernel, ends), out_shape=(pltpu.VMEM...  1.89 us
    pallas_call x1, Pallas kernels, body(): pl.pallas_call(edge_kernel, out_shape=(side, side, pltpu.VMEM((cols, LANE...  1.05 us
    pallas_call x1, Pallas kernels, body(): pl.pallas_call(widen_kernel, out_shape=jax.ShapeDtypeStruct(widened, F32)...  1.04 us
  transfers between devices with their start and end apart: 5, of which 4 were waited for; matrix products, arithmetic and copies ran while one was open for 0% of the time, Pallas kernels for 7%

profile of v10, /device:TPU:0, one launch (start us, length us, event | category | flops | bytes accessed | tf_op | source)
XLA Modules:
  0.0 36.8 jit_solution(11330012754759540904)
XLA Ops:
  0.6 1.1 %edges.1 = (bf16[96,256]{1,0:T(8,128)(2,1)S(1)}, bf16[96,256]{1,0:T(8,128)(2,1)S(1)}, f32[32,128]{1,0:T(8,128)S(1)}) custom-call(f32[8,32,256]{2,1,0:T(8,128)} %right_hbm.3, f32[8,32,256]{2,1,0:T(8,128)} %weight_hbm.3, s32[9,8,32]{2,1,0:T(8,128)} %bitcast.10), custom_call_target="tpu_custom_call" | custom-call | tf_op jit(solution)/shard_map/edges/pallas_call | solution.py:363
  1.7 0.7 %collective-permute-start = (bf16[96,256]{1,0:T(8,128)(2,1)S(1)}, bf16[96,256]{1,0:T(8,128)(2,1)S(1)}, u32[]{:S(2)}, u32[]{:S(2)}) collective-permute-start(bf16[96,256]{1,0:T(8,128)(2,1)S(1)} %get-tuple-element.20), channel_id=1, source_target_pairs={{1,2},{2,1},{3,4},{4,3},{5,6},{6,5},{7,8},{8,7},{9,10},{10,9},{11,... | collective-permute-start | bytes 147464 | tf_op jit(solution)/shard_map/ppermute | solution.py:378
  2.4 5.7 %collective-permute-start.1 = (bf16[96,256]{1,0:T(8,128)(2,1)S(1)}, bf16[96,256]{1,0:T(8,128)(2,1)S(1)}, u32[]{:S(2)}, u32[]{:S(2)}) collective-permute-start(bf16[96,256]{1,0:T(8,128)(2,1)S(1)} %get-tuple-element.21), channel_id=1, source_target_pairs={{0,1},{1,0},{2,3},{3,2},{4,5},{5,4},{6,7},{7,6},{8,9},{9,8},{10,11... | collective-permute-start | bytes 147464 | tf_op jit(solution)/shard_map/ppermute | solution.py:379
  8.1 1.9 %own.1 = (bf16[6,64,256]{2,1,0:T(8,128)(2,1)S(1)}, bf16[9,256,256]{2,1,0:T(8,128)(2,1)S(1)}, bf16[9,8,32,128]{3,2,1,0:T(8,128)(2,1)S(1)}, f32[8,32,256]{2,1,0:T(8,128)S(1)}, f32[8,32,256]{2,1,0:T(8,128)S(1)}) custom-call(bf16[9,256,256]{2,1,0:T(8,128)(2,1)} %stencil_hbm.1, f32[8,32,256]{2,1,0:T(8,128)} %right_hbm.3, f32[8,32,256]{2,1,0:T(8,128)} %weight_hbm.3, ...), custom_call_target="tpu_custom_call" | custom-call | bytes 6000000 | tf_op jit(solution)/shard_map/own/pallas_call | solution.py:396
  10.0 0.1 collective-permute-start.3
  10.1 0.0 collective-permute-done.odd_ref
  10.1 0.5 %collective-permute-done.1.even_ref = bf16[96,256]{1,0:T(8,128)(2,1)S(1)} collective-permute-done((bf16[96,256]{1,0:T(8,128)(2,1)S(1)}, bf16[96,256]{1,0:T(8,128)(2,1)S(1)}, u32[]{:S(2)}, u32[]{:S(2)}) %collective-permute-start.1) | collective-permute-done | bytes 49184 | tf_op jit(solution)/shard_map/ppermute | solution.py:379
  10.6 0.1 collective-permute-start.2
  10.7 0.2 sides.1
  10.9 0.6 %collective-permute-done.3.refs_0_ = bf16[6,64,256]{2,1,0:T(8,128)(2,1)S(1)} collective-permute-done((bf16[6,64,256]{2,1,0:T(8,128)(2,1)S(1)}, bf16[6,64,256]{2,1,0:T(8,128)(2,1)S(1)}, u32[]{:S(2)}, u32[]{:S(2)}) %collective-permute-start.3) | collective-permute-done | bytes 196640 | tf_op jit(solution)/shard_map/ppermute | solution.py:409
  11.5 0.3 rows.1
  11.8 0.2 collective-permute-done.2.refs_4_
  12.0 5.2 %smooth.1 = (f32[8,32,256]{2,1,0:T(8,128)}, bf16[4,16,256]{2,1,0:T(8,128)(2,1)S(1)}) custom-call(bf16[9,256,256]{2,1,0:T(8,128)(2,1)S(1)} %get-tuple-element.19.refs_0_, bf16[9,8,16,128]{3,2,1,0:T(8,128)(2,1)S(1)} %get-tuple-element.22.refs_1_, f32[8,16,256]{2,1,0:T(8,128)S(1)} %get-tuple-element.23.refs_2_, f32[8,16,256]{2,1,0:T(8,128)S(1)} %get-tuple-element.24.refs_3_, ...), custom_call_target="tpu_custom_call" | custom-call | tf_op jit(solution)/shard_map/smooth/pallas_call | solution.py:443
  17.2 3.5 %collective-permute-start.4 = (bf16[4,16,256]{2,1,0:T(8,128)(2,1)S(1)}, bf16[4,16,256]{2,1,0:T(8,128)(2,1)S(1)}, u32[]{:S(2)}, u32[]{:S(2)}) collective-permute-start(bf16[4,16,256]{2,1,0:T(8,128)(2,1)S(1)} %get-tuple-element.33), channel_id=1, source_target_pairs={{0,8},{1,9},{2,10},{3,11},{4,12},{5,13},{6,14},{7,15},{8,0},{9,1},... | collective-permute-start | bytes 98312 | tf_op jit(solution)/shard_map/ppermute | solution.py:470
  20.8 1.9 %collective-permute-done.4 = bf16[4,16,256]{2,1,0:T(8,128)(2,1)S(1)} collective-permute-done((bf16[4,16,256]{2,1,0:T(8,128)(2,1)S(1)}, bf16[4,16,256]{2,1,0:T(8,128)(2,1)S(1)}, u32[]{:S(2)}, u32[]{:S(2)}) %collective-permute-start.4) | collective-permute-done | bytes 32800 | tf_op jit(solution)/shard_map/ppermute | solution.py:470
  22.7 13.1 %all_to_all.5.block_ref = bf16[8,2,4,16,256]{4,3,2,1,0:T(8,128)(2,1)S(1)} all-to-all(bf16[8,2,4,16,256]{4,3,2,1,0:T(8,128)(2,1)S(1)} %broadcast_in_dim.2), channel_id=1, replica_groups={{0,1,2,3,4,5,6,7},{8,9,10,11,12,13,14,15},{16,17,18,19,20,21,22,23},{24..., dimensions={0} | all-to-all | bytes 1048576 | tf_op jit(solution)/shard_map/all_to_all | solution.py:473
  35.8 1.0 %widen.1 = f32[4,16,16,256]{3,2,1,0:T(8,128)} custom-call(bf16[8,2,4,16,256]{4,3,2,1,0:T(8,128)(2,1)S(1)} %all_to_all.5.block_ref), custom_call_target="tpu_custom_call" | custom-call | tf_op jit(solution)/shard_map/widen/pallas_call | solution.py:475
  (3 shorter events, 0.1 us)
Async XLA Ops:
  1.7 8.4 %collective-permute-start = (bf16[96,256]{1,0:T(8,128)(2,1)S(1)}, bf16[96,256]{1,0:T(8,128)(2,1)S(1)}, u32[]{:S(2)}, u32[]{:S(2)}) collective-permute-start(bf16[96,256]{1,0:T(8,128)(2,1)S(1)} %get-tuple-element.20), channel_id=1, source_target_pairs={{1,2},{2,1},{3,4},{4,3},{5,6},{6,5},{7,8},{8,7},{9,10},{10,9},{11,... | collective-permute-start | bytes 147464 | tf_op jit(solution)/shard_map/ppermute | solution.py:378
  2.4 8.2 %collective-permute-start.1 = (bf16[96,256]{1,0:T(8,128)(2,1)S(1)}, bf16[96,256]{1,0:T(8,128)(2,1)S(1)}, u32[]{:S(2)}, u32[]{:S(2)}) collective-permute-start(bf16[96,256]{1,0:T(8,128)(2,1)S(1)} %get-tuple-element.21), channel_id=1, source_target_pairs={{0,1},{1,0},{2,3},{3,2},{4,5},{5,4},{6,7},{7,6},{8,9},{9,8},{10,11... | collective-permute-start | bytes 147464 | tf_op jit(solution)/shard_map/ppermute | solution.py:379
  10.0 1.5 %collective-permute-start.3 = (bf16[6,64,256]{2,1,0:T(8,128)(2,1)S(1)}, bf16[6,64,256]{2,1,0:T(8,128)(2,1)S(1)}, u32[]{:S(2)}, u32[]{:S(2)}) collective-permute-start(bf16[6,64,256]{2,1,0:T(8,128)(2,1)S(1)} %get-tuple-element.28), channel_id=1, source_target_pairs={{0,16},{16,0},{1,17},{17,1},{2,18},{18,2},{3,19},{19,3},{4,20},{20... | collective-permute-start | bytes 589832 | tf_op jit(solution)/shard_map/ppermute | solution.py:409
  10.6 1.4 %collective-permute-start.2 = (bf16[2,96,256]{2,1,0:T(8,128)(2,1)S(1)}, bf16[2,96,256]{2,1,0:T(8,128)(2,1)S(1)}, u32[]{:S(2)}, u32[]{:S(2)}) collective-permute-start(bf16[2,96,256]{2,1,0:T(8,128)(2,1)S(1)} %pad_maximum_fusion), channel_id=1, source_target_pairs={{0,16},{16,0},{1,17},{17,1},{2,18},{18,2},{3,19},{19,3},{4,20},{20... | collective-permute-start | bytes 294920 | tf_op jit(solution)/shard_map/ppermute | solution.py:411
  17.2 5.4 %collective-permute-start.4 = (bf16[4,16,256]{2,1,0:T(8,128)(2,1)S(1)}, bf16[4,16,256]{2,1,0:T(8,128)(2,1)S(1)}, u32[]{:S(2)}, u32[]{:S(2)}) collective-permute-start(bf16[4,16,256]{2,1,0:T(8,128)(2,1)S(1)} %get-tuple-element.33), channel_id=1, source_target_pairs={{0,8},{1,9},{2,10},{3,11},{4,12},{5,13},{6,14},{7,15},{8,0},{9,1},... | collective-permute-start | bytes 98312 | tf_op jit(solution)/shard_map/ppermute | solution.py:470

commit v11 on v8

--- a/solution.py
+++ b/solution.py
@@ -13,7 +13,7 @@
 SIDE = 8
 LANES = 128
 STRIPS = ((0, STEPS - 1), (SIDE - STEPS, 0))
-PIECE_ROWS = 3
+PIECE_ROWS = 5
 
 lower_edge = 1.5
 upper_edge = 6.0

time: 37.2 us -> 37.2 us (level)
  transfers between devices with their start and end apart: 5 -> 5, of which waited for: 4 -> 4; matrix products, arithmetic and copies ran while one was open for 0% -> 0% of each run, Pallas kernels for 6% -> 7%
where the time goes in v11:
time: 37.2 us; the launch traced here: 36.9 us
  blocking collectives  13 us (35%)
  starting transfers between devices  10.1 us (27%)
  Pallas kernels  9.88 us (27%)
  waiting for transfers between devices  3.17 us (9%)
  between operations  0.71 us (2%)
    all_to_all x1, blocking collectives, body(): block = lax.all_to_all(spread, 'fcol', 0, 0, axis_index_groups=halves)  13 us
    ppermute x1, starting transfers between devices, body(): even_side = lax.ppermute(even, 'fcol', swaps[0])  5.74 us
    pallas_call x1, Pallas kernels, body(): pl.pallas_call(functools.partial(smooth_kernel, ends), out_shape=(jax.Sha...  5.4 us
    ppermute x1, starting transfers between devices, body(): pair = jnp.stack([coarse, lax.ppermute(coarse, 'fcol', across)])  3.53 us
    ppermute x1, waiting for transfers between devices, body(): pair = jnp.stack([coarse, lax.ppermute(coarse, 'fcol', across)])  1.89 us
    pallas_call x1, Pallas kernels, body(): pl.pallas_call(functools.partial(own_kernel, ends), out_shape=(pltpu.VMEM...  1.89 us
    pallas_call x1, Pallas kernels, body(): pl.pallas_call(edge_kernel, out_shape=(side, side, pltpu.VMEM((cols, LANE...  1.05 us
    pallas_call x1, Pallas kernels, body(): pl.pallas_call(widen_kernel, out_shape=jax.ShapeDtypeStruct(widened, F32)...  1.02 us
  transfers between devices with their start and end apart: 5, of which 4 were waited for; matrix products, arithmetic and copies ran while one was open for 0% of the time, Pallas kernels for 7%

profile of v11, /device:TPU:0, one launch (start us, length us, event | category | flops | bytes accessed | tf_op | source)
XLA Modules:
  0.0 36.9 jit_solution(11300849895775019468)
XLA Ops:
  0.6 1.1 %edges.1 = (bf16[96,256]{1,0:T(8,128)(2,1)S(1)}, bf16[96,256]{1,0:T(8,128)(2,1)S(1)}, f32[32,128]{1,0:T(8,128)S(1)}) custom-call(f32[8,32,256]{2,1,0:T(8,128)} %right_hbm.3, f32[8,32,256]{2,1,0:T(8,128)} %weight_hbm.3, s32[9,8,32]{2,1,0:T(8,128)} %bitcast.10), custom_call_target="tpu_custom_call" | custom-call | tf_op jit(solution)/shard_map/edges/pallas_call | solution.py:358
  1.7 0.7 %collective-permute-start = (bf16[96,256]{1,0:T(8,128)(2,1)S(1)}, bf16[96,256]{1,0:T(8,128)(2,1)S(1)}, u32[]{:S(2)}, u32[]{:S(2)}) collective-permute-start(bf16[96,256]{1,0:T(8,128)(2,1)S(1)} %get-tuple-element.20), channel_id=1, source_target_pairs={{1,2},{2,1},{3,4},{4,3},{5,6},{6,5},{7,8},{8,7},{9,10},{10,9},{11,... | collective-permute-start | bytes 147464 | tf_op jit(solution)/shard_map/ppermute | solution.py:373
  2.4 5.7 %collective-permute-start.1 = (bf16[96,256]{1,0:T(8,128)(2,1)S(1)}, bf16[96,256]{1,0:T(8,128)(2,1)S(1)}, u32[]{:S(2)}, u32[]{:S(2)}) collective-permute-start(bf16[96,256]{1,0:T(8,128)(2,1)S(1)} %get-tuple-element.21), channel_id=1, source_target_pairs={{0,1},{1,0},{2,3},{3,2},{4,5},{5,4},{6,7},{7,6},{8,9},{9,8},{10,11... | collective-permute-start | bytes 147464 | tf_op jit(solution)/shard_map/ppermute | solution.py:374
  8.1 1.9 %own.1 = (bf16[6,64,256]{2,1,0:T(8,128)(2,1)S(1)}, bf16[9,256,256]{2,1,0:T(8,128)(2,1)S(1)}, bf16[9,8,32,128]{3,2,1,0:T(8,128)(2,1)S(1)}, f32[8,32,256]{2,1,0:T(8,128)S(1)}, f32[8,32,256]{2,1,0:T(8,128)S(1)}) custom-call(bf16[9,256,256]{2,1,0:T(8,128)(2,1)} %stencil_hbm.1, f32[8,32,256]{2,1,0:T(8,128)} %right_hbm.3, f32[8,32,256]{2,1,0:T(8,128)} %weight_hbm.3, ...), custom_call_target="tpu_custom_call" | custom-call | bytes 6000000 | tf_op jit(solution)/shard_map/own/pallas_call | solution.py:391
  10.0 0.1 collective-permute-start.3
  10.1 0.0 collective-permute-done.odd_ref
  10.1 0.5 %collective-permute-done.1.even_ref = bf16[96,256]{1,0:T(8,128)(2,1)S(1)} collective-permute-done((bf16[96,256]{1,0:T(8,128)(2,1)S(1)}, bf16[96,256]{1,0:T(8,128)(2,1)S(1)}, u32[]{:S(2)}, u32[]{:S(2)}) %collective-permute-start.1) | collective-permute-done | bytes 49184 | tf_op jit(solution)/shard_map/ppermute | solution.py:374
  10.6 0.1 collective-permute-start.2
  10.7 0.2 sides.1
  10.9 0.6 %collective-permute-done.3.refs_0_ = bf16[6,64,256]{2,1,0:T(8,128)(2,1)S(1)} collective-permute-done((bf16[6,64,256]{2,1,0:T(8,128)(2,1)S(1)}, bf16[6,64,256]{2,1,0:T(8,128)(2,1)S(1)}, u32[]{:S(2)}, u32[]{:S(2)}) %collective-permute-start.3) | collective-permute-done | bytes 196640 | tf_op jit(solution)/shard_map/ppermute | solution.py:404
  11.5 0.3 rows.1
  11.8 0.2 collective-permute-done.2.refs_4_
  12.0 5.4 %smooth.1 = (f32[8,32,256]{2,1,0:T(8,128)}, bf16[4,16,256]{2,1,0:T(8,128)(2,1)S(1)}) custom-call(bf16[9,256,256]{2,1,0:T(8,128)(2,1)S(1)} %get-tuple-element.19.refs_0_, bf16[9,8,16,128]{3,2,1,0:T(8,128)(2,1)S(1)} %get-tuple-element.22.refs_1_, f32[8,16,256]{2,1,0:T(8,128)S(1)} %get-tuple-element.23.refs_2_, f32[8,16,256]{2,1,0:T(8,128)S(1)} %get-tuple-element.24.refs_3_, ...), custom_call_target="tpu_custom_call" | custom-call | tf_op jit(solution)/shard_map/smooth/pallas_call | solution.py:438
  17.4 3.5 %collective-permute-start.4 = (bf16[4,16,256]{2,1,0:T(8,128)(2,1)S(1)}, bf16[4,16,256]{2,1,0:T(8,128)(2,1)S(1)}, u32[]{:S(2)}, u32[]{:S(2)}) collective-permute-start(bf16[4,16,256]{2,1,0:T(8,128)(2,1)S(1)} %get-tuple-element.33), channel_id=1, source_target_pairs={{0,8},{1,9},{2,10},{3,11},{4,12},{5,13},{6,14},{7,15},{8,0},{9,1},... | collective-permute-start | bytes 98312 | tf_op jit(solution)/shard_map/ppermute | solution.py:465
  20.9 1.9 %collective-permute-done.4 = bf16[4,16,256]{2,1,0:T(8,128)(2,1)S(1)} collective-permute-done((bf16[4,16,256]{2,1,0:T(8,128)(2,1)S(1)}, bf16[4,16,256]{2,1,0:T(8,128)(2,1)S(1)}, u32[]{:S(2)}, u32[]{:S(2)}) %collective-permute-start.4) | collective-permute-done | bytes 32800 | tf_op jit(solution)/shard_map/ppermute | solution.py:465
  22.9 13.0 %all_to_all.5.block_ref = bf16[8,2,4,16,256]{4,3,2,1,0:T(8,128)(2,1)S(1)} all-to-all(bf16[8,2,4,16,256]{4,3,2,1,0:T(8,128)(2,1)S(1)} %broadcast_in_dim.2), channel_id=1, replica_groups={{0,1,2,3,4,5,6,7},{8,9,10,11,12,13,14,15},{16,17,18,19,20,21,22,23},{24..., dimensions={0} | all-to-all | bytes 1048576 | tf_op jit(solution)/shard_map/all_to_all | solution.py:468
  35.9 1.0 %widen.1 = f32[4,16,16,256]{3,2,1,0:T(8,128)} custom-call(bf16[8,2,4,16,256]{4,3,2,1,0:T(8,128)(2,1)S(1)} %all_to_all.5.block_ref), custom_call_target="tpu_custom_call" | custom-call | tf_op jit(solution)/shard_map/widen/pallas_call | solution.py:470
  (3 shorter events, 0.1 us)
Async XLA Ops:
  1.7 8.4 %collective-permute-start = (bf16[96,256]{1,0:T(8,128)(2,1)S(1)}, bf16[96,256]{1,0:T(8,128)(2,1)S(1)}, u32[]{:S(2)}, u32[]{:S(2)}) collective-permute-start(bf16[96,256]{1,0:T(8,128)(2,1)S(1)} %get-tuple-element.20), channel_id=1, source_target_pairs={{1,2},{2,1},{3,4},{4,3},{5,6},{6,5},{7,8},{8,7},{9,10},{10,9},{11,... | collective-permute-start | bytes 147464 | tf_op jit(solution)/shard_map/ppermute | solution.py:373
  2.4 8.2 %collective-permute-start.1 = (bf16[96,256]{1,0:T(8,128)(2,1)S(1)}, bf16[96,256]{1,0:T(8,128)(2,1)S(1)}, u32[]{:S(2)}, u32[]{:S(2)}) collective-permute-start(bf16[96,256]{1,0:T(8,128)(2,1)S(1)} %get-tuple-element.21), channel_id=1, source_target_pairs={{0,1},{1,0},{2,3},{3,2},{4,5},{5,4},{6,7},{7,6},{8,9},{9,8},{10,11... | collective-permute-start | bytes 147464 | tf_op jit(solution)/shard_map/ppermute | solution.py:374
  10.0 1.5 %collective-permute-start.3 = (bf16[6,64,256]{2,1,0:T(8,128)(2,1)S(1)}, bf16[6,64,256]{2,1,0:T(8,128)(2,1)S(1)}, u32[]{:S(2)}, u32[]{:S(2)}) collective-permute-start(bf16[6,64,256]{2,1,0:T(8,128)(2,1)S(1)} %get-tuple-element.28), channel_id=1, source_target_pairs={{0,16},{16,0},{1,17},{17,1},{2,18},{18,2},{3,19},{19,3},{4,20},{20... | collective-permute-start | bytes 589832 | tf_op jit(solution)/shard_map/ppermute | solution.py:404
  10.6 1.4 %collective-permute-start.2 = (bf16[2,96,256]{2,1,0:T(8,128)(2,1)S(1)}, bf16[2,96,256]{2,1,0:T(8,128)(2,1)S(1)}, u32[]{:S(2)}, u32[]{:S(2)}) collective-permute-start(bf16[2,96,256]{2,1,0:T(8,128)(2,1)S(1)} %pad_maximum_fusion), channel_id=1, source_target_pairs={{0,16},{16,0},{1,17},{17,1},{2,18},{18,2},{3,19},{19,3},{4,20},{20... | collective-permute-start | bytes 294920 | tf_op jit(solution)/shard_map/ppermute | solution.py:406
  17.4 5.4 %collective-permute-start.4 = (bf16[4,16,256]{2,1,0:T(8,128)(2,1)S(1)}, bf16[4,16,256]{2,1,0:T(8,128)(2,1)S(1)}, u32[]{:S(2)}, u32[]{:S(2)}) collective-permute-start(bf16[4,16,256]{2,1,0:T(8,128)(2,1)S(1)} %get-tuple-element.33), channel_id=1, source_target_pairs={{0,8},{1,9},{2,10},{3,11},{4,12},{5,13},{6,14},{7,15},{8,0},{9,1},... | collective-permute-start | bytes 98312 | tf_op jit(solution)/shard_map/ppermute | solution.py:465
